TPU v7x, 256 devices: a whole 4x4x8 slice. The times are simulated.
256 devices in a mesh: tm: 32 (over y_lo, z, core), rows: 8 (over y_hi, x).
Axes of the slice: x: 4, y: 4 (y_hi: 2, y_lo: 2; y = y_hi * 2 + y_lo), z: 8, core: 2. Of those that a mesh axis runs over, the one named last changes fastest.
Arguments:
- video: bfloat16 [64, 16, 96, 256], P('tm', 'rows'), may hold values from -6 to 6
- kernel_a: bfloat16 [6912, 256], replicated, may hold values from -0.078125 to 0.078125
- project: bfloat16 [256, 128], replicated, may hold values from -0.375 to 0.375
- kernel_b: bfloat16 [3456, 128], replicated, may hold values from -0.109375 to 0.109375
- cotangent: bfloat16 [64, 16, 96, 128], P('tm', 'rows'), may hold values from -6 to 6
Outputs:
- output: float32 [64, 16, 96, 128], P('tm', 'rows')
- grad_video: float32 [64, 16, 96, 256], P('tm', 'rows')
- grad_kernel_a: float32 [6912, 256], P('tm', 'rows')
- grad_kernel_b: float32 [3456, 128], P('tm', 'rows')
- grad_project: float32 [256, 128], P('tm', 'rows')
All inputs are finite; a program needn't handle non-finite values.
Results may differ from a plain program's by a relative error of at most 0.0041.
Values may be sent and summed in bfloat16 or wider, within the bound.
A program may use at most 128 MiB of HBM per device.

v0:
```python
import jax
import jax.numpy as jnp
from jax import lax
from jax.sharding import PartitionSpec as P


def with_halo(x, sides, width):
    for axis, dim in sides:
        peers, length = (lax.axis_size(axis), x.shape[dim])
        up = [(i, (i + 1) % peers) for i in range(peers - 1)]
        down = [(j, i) for i, j in up]
        last = lax.slice_in_dim(x, length - width, length, axis=dim)
        leading = lax.slice_in_dim(x, 0, width, axis=dim)
        before = lax.ppermute(last, axis, up)
        after = lax.ppermute(leading, axis, down)
        x = jnp.concatenate([before, x, after], axis=dim)
    return x


def passed_along(block, axis, distance):
    devices = range(lax.axis_size(axis))
    route = [(i - distance, i) for i in devices if i - distance in devices]
    return lax.ppermute(block, axis, route)


def conv_taps(padded, weight, frames, rows, width, flip):
    cin = padded.shape[3]
    cout = weight.shape[1]
    total = jnp.zeros((frames * rows * width, weight.shape[0] // 27 if flip else cout), jnp.float32)
    for kt in range(3):
        for kr in range(3):
            for kc in range(3):
                tap = 9 * kt + 3 * kr + kc
                if flip:
                    piece = padded[
                        2 - kt : 2 - kt + frames, 2 - kr : 2 - kr + rows, 2 - kc : 2 - kc + width
                    ].reshape(-1, cin)
                    block = weight[
                        tap * (weight.shape[0] // 27) : (tap + 1) * (weight.shape[0] // 27)
                    ]
                    total = total + lax.dot_general(
                        piece, block, (((1,), (1,)), ((), ())), preferred_element_type=jnp.float32
                    )
                else:
                    piece = padded[kt : kt + frames, kr : kr + rows, kc : kc + width].reshape(
                        -1, cin
                    )
                    block = weight[tap * cin : (tap + 1) * cin]
                    total = total + jnp.dot(piece, block, preferred_element_type=jnp.float32)
    return total


def weight_grad(padded, grad, frames, rows, width):
    cin = padded.shape[3]
    flat = grad.reshape(-1, grad.shape[-1])
    blocks = []
    for kt in range(3):
        for kr in range(3):
            for kc in range(3):
                piece = padded[kt : kt + frames, kr : kr + rows, kc : kc + width].reshape(-1, cin)
                blocks.append(
                    lax.dot_general(
                        piece, flat, (((0,), (0,)), ((), ())), preferred_element_type=jnp.float32
                    )
                )
    return jnp.concatenate(blocks, 0)


def with_rims(block):
    return with_halo(block, (("rows", 1),), 1)


def pad_width(block):
    return jnp.pad(block, ((0, 0), (0, 0), (1, 1), (0, 0)))


def past_padded(block):
    banded = with_rims(block)
    earlier = passed_along(banded, "tm", 1)
    return pad_width(jnp.concatenate([earlier, banded], 0))


def future_padded(block):
    banded = with_rims(block)
    later = passed_along(banded, "tm", -1)
    return pad_width(jnp.concatenate([banded, later], 0))


def shards(video, kernel_a, project, kernel_b, cotangent):
    frames, rows, width, chan_a = video.shape
    chan_b = cotangent.shape[3]
    video_p = past_padded(video)
    pre = conv_taps(video_p, kernel_a, frames, rows, width, False)
    hidden = jax.nn.silu(pre).astype(jnp.bfloat16)
    mid = jnp.dot(hidden, project, preferred_element_type=jnp.float32)
    mid_b = mid.astype(jnp.bfloat16)
    mid_p = past_padded(mid_b.reshape(frames, rows, width, chan_b))
    result = conv_taps(mid_p, kernel_b, frames, rows, width, False) + mid
    cot_p = future_padded(cotangent)
    grad_mid = (
        cotangent.reshape(-1, chan_b).astype(jnp.float32)
        + conv_taps(cot_p, kernel_b, frames, rows, width, True)
    ).astype(jnp.bfloat16)
    total_cells = frames * lax.axis_size("tm") * rows * lax.axis_size("rows") * width
    scale = 1.0 / jnp.sqrt(jnp.float32(total_cells))
    grad_b = weight_grad(mid_p, cotangent, frames, rows, width) * scale
    grad_proj = (
        lax.dot_general(
            hidden, grad_mid, (((0,), (0,)), ((), ())), preferred_element_type=jnp.float32
        )
        * scale
    )
    grad_h = lax.dot_general(
        grad_mid, project, (((1,), (1,)), ((), ())), preferred_element_type=jnp.float32
    )
    sig = jax.nn.sigmoid(pre)
    grad_pre = (grad_h * sig * (1.0 + pre * (1.0 - sig))).astype(jnp.bfloat16)
    grad_pre_4 = grad_pre.reshape(frames, rows, width, chan_a)
    grad_pre_p = future_padded(grad_pre_4)
    grad_video = conv_taps(grad_pre_p, kernel_a, frames, rows, width, True)
    grad_a = weight_grad(video_p, grad_pre_4, frames, rows, width) * scale
    partial_value = (
        lax.psum_scatter(grad_a, "tm", scatter_dimension=0, tiled=True),
        lax.psum_scatter(grad_b, "tm", scatter_dimension=0, tiled=True),
        lax.psum_scatter(grad_proj, "tm", scatter_dimension=0, tiled=True),
    )
    summed = (
        lax.psum_scatter(partial_value[0], "rows", scatter_dimension=1, tiled=True),
        lax.psum_scatter(partial_value[1], "rows", scatter_dimension=1, tiled=True),
        lax.psum_scatter(partial_value[2], "rows", scatter_dimension=1, tiled=True),
    )
    return (
        result.reshape(frames, rows, width, chan_b),
        grad_video.reshape(frames, rows, width, chan_a),
        summed[0],
        summed[1],
        summed[2],
    )


def solution(mesh):
    in_specs = (P("tm", "rows", None, None), P(), P(), P(), P("tm", "rows", None, None))
    out_specs = (
        P("tm", "rows", None, None),
        P("tm", "rows", None, None),
        P("tm", "rows"),
        P("tm", "rows"),
        P("tm", "rows"),
    )
    return jax.shard_map(shards, mesh=mesh, in_specs=in_specs, out_specs=out_specs, check_vma=False)
```

profile of v0, /device:TPU:1, one launch (start us, length us, event | category | flops | bytes accessed | tf_op | source)
XLA Modules:
  0.0 626.3 jit_solution(45569789540430377)
XLA Ops:
  8.2 1.3 collective-permute-start.7
  9.4 4.6 collective-permute-start.6
  15.0 1.3 collective-permute-start.1
  16.3 4.0 collective-permute-start
  20.3 1.3 fusion.234
  23.0 1.0 pad_maximum_fusion.9
  24.0 5.7 collective-permute-start.8
  29.7 1.1 pad_maximum_fusion.6
  30.9 1.9 collective-permute-start.2
  39.0 1.3 copy-done.3
  46.2 1.0 multiply_convert_fusion
  49.0 1.2 fusion.10
  51.0 3.1 collective-permute-start.3
  54.1 1.3 collective-permute-start.4
  55.4 1.0 convolution_dynamic-update-slice_fusion.25
  57.1 6.5 %collective-permute-start.9 = (bf16[2,1,96,256]{3,2,1,0:T(8,128)(2,1)}, bf16[2,1,96,256]{3,2,1,0:T(8,128)(2,1)S(1)}, u32[]{:S(2)}, u32[]{:S(2)}) collective-permute-start(bf16[2,1,96,256]{3,2,1,0:T(8,128)(2,1)} %get-tuple-element.105), channel_id=1, source_target_pairs={{0,1},{1,2},{2,3},{3,4},{4,5},{5,6},{6,7},{8,9},{9,10},{10,11},{11... | collective-permute-start | bytes 294920 | tf_op jit(solution)/shard_map/ppermute | solution.py:14
  63.6 1.3 collective-permute-start.10
  64.9 1.9 convolution_dynamic-update-slice_fusion.24
  66.8 1.9 convolution_dynamic-update-slice_fusion.23
  68.7 1.9 convolution_dynamic-update-slice_fusion.22
  70.7 1.9 convolution_dynamic-update-slice_fusion.21
  73.5 1.9 convolution_dynamic-update-slice_fusion.19
  75.4 1.9 convolution_dynamic-update-slice_fusion.18
  78.3 1.9 convolution_dynamic-update-slice_fusion.16
  80.2 1.0 convolution_dynamic-update-slice_fusion.15
  81.2 1.0 convolution_dynamic-update-slice_fusion.14
  86.0 1.0 convolution_dynamic-update-slice_fusion.9
  89.0 1.0 convolution_dynamic-update-slice_fusion.6
  96.7 160.6 %all-reduce.9.cloned.1.call-done = f32[256,128]{1,0:T(8,128)} async-done(((f32[256,128]{1,0:T(8,128)}), f32[256,128]{1,0:T(8,128)}) %all-reduce.9.cloned.1.call-update) | async-done | bytes 131088
  258.9 6.4 %broadcast_multiply_fusion = f32[6912,256]{1,0:T(8,128)} fusion(f32[6912,256]{1,0:T(8,128)} %convolution_dynamic-update-slice_fusion), kind=kLoop, calls=%fused_computation | loop fusion | flops 1769472 | bytes 14155776 | tf_op jit(solution)/shard_map/mul | solution.py:121
  265.5 1.9 collective-permute-start.5
  268.2 1.7 pad_maximum_fusion.3
  269.8 2.4 collective-permute-start.11
  272.3 1.6 pad_maximum_fusion.4
  273.9 59.1 %reduce-scatter.19.cloned.1.call-done = f32[16,8]{1,0:T(8,128)} async-done(((f32[128,8]{1,0:T(8,128)}), f32[16,8]{1,0:T(8,128)}) %reduce-scatter.19.cloned.1.call-update) | async-done | bytes 528
  333.0 1.4 copy.46
  340.4 70.2 %fusion = f32[112,128]{1,0:T(8,128)S(1)} fusion(f32[3456,128]{1,0:T(8,128)S(1)} %broadcast_multiply_fusion.1), kind=kCustom, calls=%all-reduce-scatter | all-reduce-scatter fusion | flops 458753 | bytes 1827840
  410.7 2.1 collective-permute-start.12
  412.7 1.3 collective-permute-start.13
  421.2 1.1 concatenate.72
  423.1 1.0 pad_maximum_fusion.1
  424.9 1.3 copy-done.4
  432.4 30.6 %reduce-scatter.13.cloned.1.call-done = f32[216,256]{1,0:T(8,128)} async-done(((f32[6912,256]{1,0:T(8,128)}), f32[216,256]{1,0:T(8,128)}) %reduce-scatter.13.cloned.1.call-update) | async-done | bytes 221200 | tf_op jit(solution)/shard_map/reduce_scatter | solution.py:123
  463.0 1.8 copy.41
  464.8 1.1 fusion.59
  466.0 1.9 fusion.9
  467.9 72.7 %reduce-scatter.17.cloned.1.call-done = f32[16,108]{1,0:T(8,128)} async-done(((f32[128,108]{1,0:T(8,128)}), f32[16,108]{1,0:T(8,128)}) %reduce-scatter.17.cloned.1.call-update) | async-done | bytes 6928
  540.6 79.1 %reduce-scatter.15.cloned.1.call-done = f32[32,216]{1,0:T(8,128)} async-done(((f32[256,216]{1,0:T(8,128)}), f32[32,216]{1,0:T(8,128)}) %reduce-scatter.15.cloned.1.call-update) | async-done | bytes 27664
  (262 shorter events, 54.2 us)
Async XLA Ops:
  7.2 41.0 %copy-start = (bf16[256,128]{1,0:T(8,128)(2,1)S(1)}, bf16[256,128]{1,0:T(8,128)(2,1)}, u32[]{:S(2)}) copy-start(bf16[256,128]{1,0:T(8,128)(2,1)} %param.7) | copy-start | bytes 196612
  7.2 26.0 %copy-start.5 = (bf16[3456,128]{1,0:T(8,128)(2,1)S(1)}, bf16[3456,128]{1,0:T(8,128)(2,1)}, u32[]{:S(2)}) copy-start(bf16[3456,128]{1,0:T(8,128)(2,1)} %param.8) | copy-start | bytes 2654212
  7.2 250.1 %all-reduce.9.cloned.1.call-start = ((), (), s32[]{:S(2)}) async-start(), calls=%async_computation.8 | async-start | bytes 262144
  8.2 14.8 %collective-permute-start.7 = (bf16[2,1,96,128]{3,2,1,0:T(8,128)(2,1)S(1)}, bf16[2,1,96,128]{3,2,1,0:T(8,128)(2,1)S(1)}, u32[]{:S(2)}, u32[]{:S(2)}) collective-permute-start(bf16[2,1,96,128]{3,2,1,0:T(8,128)(2,1)S(1)} %get-tuple-element.121), channel_id=1, source_target_pairs={{1,0},{2,1},{3,2},{4,3},{5,4},{6,5},{7,6},{9,8},{10,9},{11,10},{12... | collective-permute-start | bytes 147464 | tf_op jit(solution)/shard_map/ppermute | solution.py:15
  9.4 13.5 %collective-permute-start.6 = (bf16[2,1,96,128]{3,2,1,0:T(8,128)(2,1)S(1)}, bf16[2,1,96,128]{3,2,1,0:T(8,128)(2,1)S(1)}, u32[]{:S(2)}, u32[]{:S(2)}) collective-permute-start(bf16[2,1,96,128]{3,2,1,0:T(8,128)(2,1)S(1)} %get-tuple-element.122), channel_id=1, source_target_pairs={{0,1},{1,2},{2,3},{3,4},{4,5},{5,6},{6,7},{8,9},{9,10},{10,11},{11... | collective-permute-start | bytes 147464 | tf_op jit(solution)/shard_map/ppermute | solution.py:14
  15.0 14.7 %collective-permute-start.1 = (bf16[2,1,96,256]{3,2,1,0:T(8,128)(2,1)S(1)}, bf16[2,1,96,256]{3,2,1,0:T(8,128)(2,1)S(1)}, u32[]{:S(2)}, u32[]{:S(2)}) collective-permute-start(bf16[2,1,96,256]{3,2,1,0:T(8,128)(2,1)S(1)} %get-tuple-element.116), channel_id=1, source_target_pairs={{1,0},{2,1},{3,2},{4,3},{5,4},{6,5},{7,6},{9,8},{10,9},{11,10},{12... | collective-permute-start | bytes 294920 | tf_op jit(solution)/shard_map/ppermute | solution.py:15
  16.3 13.4 %collective-permute-start = (bf16[2,1,96,256]{3,2,1,0:T(8,128)(2,1)S(1)}, bf16[2,1,96,256]{3,2,1,0:T(8,128)(2,1)S(1)}, u32[]{:S(2)}, u32[]{:S(2)}) collective-permute-start(bf16[2,1,96,256]{3,2,1,0:T(8,128)(2,1)S(1)} %get-tuple-element.117), channel_id=1, source_target_pairs={{0,1},{1,2},{2,3},{3,4},{4,5},{5,6},{6,7},{8,9},{9,10},{10,11},{11... | collective-permute-start | bytes 294920 | tf_op jit(solution)/shard_map/ppermute | solution.py:14
  24.0 8.8 %collective-permute-start.8 = (bf16[2,4,96,128]{3,2,1,0:T(8,128)(2,1)S(1)}, bf16[2,4,96,128]{3,2,1,0:T(8,128)(2,1)S(1)}, u32[]{:S(2)}, u32[]{:S(2)}) collective-permute-start(bf16[2,4,96,128]{3,2,1,0:T(8,128)(2,1)S(1)} %constant_dynamic-update-slice_fusion.3), channel_id=1, source_target_pairs={{8,0},{16,8},{24,16},{32,24},{40,32},{48,40},{56,48},{64,56},{72,6... | collective-permute-start | bytes 589832 | tf_op jit(solution)/shard_map/ppermute | solution.py:23
  30.8 14.3 %copy-start.21 = (bf16[2,2,96,256]{3,2,1,0:T(8,128)(2,1)}, bf16[2,2,96,256]{3,2,1,0:T(8,128)(2,1)S(1)}, u32[]{:S(2)}) copy-start(bf16[2,2,96,256]{3,2,1,0:T(8,128)(2,1)S(1)} %get-tuple-element.115) | copy-start | bytes 589828
  30.8 15.4 %copy-start.24 = (bf16[2,2,96,256]{3,2,1,0:T(8,128)(2,1)}, bf16[2,2,96,256]{3,2,1,0:T(8,128)(2,1)S(1)}, u32[]{:S(2)}) copy-start(bf16[2,2,96,256]{3,2,1,0:T(8,128)(2,1)S(1)} %get-tuple-element.113) | copy-start | bytes 589828
  30.9 7.4 %collective-permute-start.2 = (bf16[2,4,96,256]{3,2,1,0:T(8,128)(2,1)S(1)}, bf16[2,4,96,256]{3,2,1,0:T(8,128)(2,1)S(1)}, u32[]{:S(2)}, u32[]{:S(2)}) collective-permute-start(bf16[2,4,96,256]{3,2,1,0:T(8,128)(2,1)S(1)} %constant_dynamic-update-slice_fusion), channel_id=1, source_target_pairs={{0,8},{8,16},{16,24},{24,32},{32,40},{40,48},{48,56},{56,64},{64,7... | collective-permute-start | bytes 1179656 | tf_op jit(solution)/shard_map/ppermute | solution.py:23
  34.9 2.4 copy-start.2
  38.1 2.3 copy-start.3
  39.0 2.8 copy-start.17
  39.0 3.0 copy-start.16
  39.0 3.5 copy-start.13
  39.0 3.9 copy-start.10
  41.5 1.4 copy-start.18
  41.5 1.4 copy-start.19
  41.5 1.4 copy-start.20
  41.5 1.6 copy-start.14
  41.6 2.3 copy-start.11
  41.6 2.9 copy-start.8
  44.2 1.3 copy-start.7
  50.3 282.7 %reduce-scatter.19.cloned.1.call-start = ((), (), s32[]{:S(2)}) async-start(), calls=%async_computation.7 | async-start | bytes 73728
  50.3 29.9 %copy-start.15 = (bf16[2,2,96,256]{3,2,1,0:T(8,128)(2,1)S(1)}, bf16[2,2,96,256]{3,2,1,0:T(8,128)(2,1)}, u32[]{:S(2)}) copy-start(bf16[2,2,96,256]{3,2,1,0:T(8,128)(2,1)} %copy-done.14) | copy-start | bytes 589828
  51.0 214.5 %collective-permute-start.3 = (bf16[2,1,96,128]{3,2,1,0:T(8,128)(2,1)}, bf16[2,1,96,128]{3,2,1,0:T(8,128)(2,1)S(1)}, u32[]{:S(2)}, u32[]{:S(2)}) collective-permute-start(bf16[2,1,96,128]{3,2,1,0:T(8,128)(2,1)} %get-tuple-element.125), channel_id=1, source_target_pairs={{0,1},{1,2},{2,3},{3,4},{4,5},{5,6},{6,7},{8,9},{9,10},{10,11},{11... | collective-permute-start | bytes 147464 | tf_op jit(solution)/shard_map/ppermute | solution.py:14
  54.1 211.4 %collective-permute-start.4 = (bf16[2,1,96,128]{3,2,1,0:T(8,128)(2,1)}, bf16[2,1,96,128]{3,2,1,0:T(8,128)(2,1)S(1)}, u32[]{:S(2)}, u32[]{:S(2)}) collective-permute-start(bf16[2,1,96,128]{3,2,1,0:T(8,128)(2,1)} %get-tuple-element.126), channel_id=1, source_target_pairs={{1,0},{2,1},{3,2},{4,3},{5,4},{6,5},{7,6},{9,8},{10,9},{11,10},{12... | collective-permute-start | bytes 147464 | tf_op jit(solution)/shard_map/ppermute | solution.py:15
  57.1 211.1 %collective-permute-start.9 = (bf16[2,1,96,256]{3,2,1,0:T(8,128)(2,1)}, bf16[2,1,96,256]{3,2,1,0:T(8,128)(2,1)S(1)}, u32[]{:S(2)}, u32[]{:S(2)}) collective-permute-start(bf16[2,1,96,256]{3,2,1,0:T(8,128)(2,1)} %get-tuple-element.105), channel_id=1, source_target_pairs={{0,1},{1,2},{2,3},{3,4},{4,5},{5,6},{6,7},{8,9},{9,10},{10,11},{11... | collective-permute-start | bytes 294920 | tf_op jit(solution)/shard_map/ppermute | solution.py:14
  63.6 204.6 %collective-permute-start.10 = (bf16[2,1,96,256]{3,2,1,0:T(8,128)(2,1)}, bf16[2,1,96,256]{3,2,1,0:T(8,128)(2,1)}, u32[]{:S(2)}, u32[]{:S(2)}) collective-permute-start(bf16[2,1,96,256]{3,2,1,0:T(8,128)(2,1)} %get-tuple-element.106), channel_id=1, source_target_pairs={{1,0},{2,1},{3,2},{4,3},{5,4},{6,5},{7,6},{9,8},{10,9},{11,10},{12... | collective-permute-start | bytes 294920 | tf_op jit(solution)/shard_map/ppermute | solution.py:15
  66.8 16.4 %copy-start.12 = (bf16[2,2,96,256]{3,2,1,0:T(8,128)(2,1)S(1)}, bf16[2,2,96,256]{3,2,1,0:T(8,128)(2,1)}, u32[]{:S(2)}) copy-start(bf16[2,2,96,256]{3,2,1,0:T(8,128)(2,1)} %copy-done.11) | copy-start | bytes 589828
  72.6 13.5 %copy-start.9 = (bf16[2,2,96,256]{3,2,1,0:T(8,128)(2,1)S(1)}, bf16[2,2,96,256]{3,2,1,0:T(8,128)(2,1)}, u32[]{:S(2)}) copy-start(bf16[2,2,96,256]{3,2,1,0:T(8,128)(2,1)} %copy-done.8) | copy-start | bytes 589828
  77.4 11.6 %copy-start.22 = (bf16[2,2,96,256]{3,2,1,0:T(8,128)(2,1)S(1)}, bf16[2,2,96,256]{3,2,1,0:T(8,128)(2,1)}, u32[]{:S(2)}) copy-start(bf16[2,2,96,256]{3,2,1,0:T(8,128)(2,1)} %copy-done.21) | copy-start | bytes 589828
  84.1 10.7 %copy-start.25 = (bf16[2,2,96,256]{3,2,1,0:T(8,128)(2,1)S(1)}, bf16[2,2,96,256]{3,2,1,0:T(8,128)(2,1)}, u32[]{:S(2)}) copy-start(bf16[2,2,96,256]{3,2,1,0:T(8,128)(2,1)} %copy-done.24) | copy-start | bytes 589828
  258.7 204.3 %reduce-scatter.13.cloned.1.call-start = ((), (), s32[]{:S(2)}) async-start(), calls=%async_computation.4 | async-start | bytes 7299072 | tf_op jit(solution)/shard_map/reduce_scatter | solution.py:123
  265.4 275.2 %reduce-scatter.17.cloned.1.call-start = ((), (), s32[]{:S(2)}) async-start(), calls=%async_computation.6 | async-start | bytes 73728
  265.5 68.8 %collective-permute-start.5 = (bf16[2,4,96,128]{3,2,1,0:T(8,128)(2,1)S(1)}, bf16[2,4,96,128]{3,2,1,0:T(8,128)(2,1)S(1)}, u32[]{:S(2)}, u32[]{:S(2)}) collective-permute-start(bf16[2,4,96,128]{3,2,1,0:T(8,128)(2,1)S(1)} %pad_maximum_fusion.8), channel_id=1, source_target_pairs={{0,8},{8,16},{16,24},{24,32},{32,40},{40,48},{48,56},{56,64},{64,7... | collective-permute-start | bytes 589832 | tf_op jit(solution)/shard_map/ppermute | solution.py:23
  269.8 153.3 %collective-permute-start.11 = (bf16[2,4,96,256]{3,2,1,0:T(8,128)(2,1)}, bf16[2,4,96,256]{3,2,1,0:T(8,128)(2,1)S(1)}, u32[]{:S(2)}, u32[]{:S(2)}) collective-permute-start(bf16[2,4,96,256]{3,2,1,0:T(8,128)(2,1)} %pad_maximum_fusion.3), channel_id=1, source_target_pairs={{8,0},{16,8},{24,16},{32,24},{40,32},{48,40},{56,48},{64,56},{72,6... | collective-permute-start | bytes 1179656 | tf_op jit(solution)/shard_map/ppermute | solution.py:23
  410.6 5.7 copy-start.6
  410.7 10.6 %collective-permute-start.12 = (f32[112,128]{1,0:T(8,128)S(1)}, f32[112,128]{1,0:T(8,128)}, u32[]{:S(2)}, u32[]{:S(2)}) collective-permute-start(f32[112,128]{1,0:T(8,128)S(1)} %fusion), channel_id=1, source_target_pairs={{0,8},{8,16},{16,24},{24,32},{32,40},{40,48},{48,56},{56,64},{64,7... | collective-permute-start | bytes 172040
  412.7 8.5 %collective-permute-start.13 = (f32[12,128]{1,0:T(8,128)S(1)}, f32[12,128]{1,0:T(8,128)S(1)}, u32[]{:S(2)}, u32[]{:S(2)}) collective-permute-start(f32[12,128]{1,0:T(8,128)S(1)} %slice.878), channel_id=1, source_target_pairs={{0,16},{8,24},{16,32},{24,40},{32,48},{40,56},{48,64},{56,72},{64,... | collective-permute-start | bytes 18440
  417.3 2.2 copy-start.28
  418.2 2.2 copy-start.23
  418.2 2.2 copy-start.27
  423.1 196.7 %reduce-scatter.15.cloned.1.call-start = ((), (), s32[]{:S(2)}) async-start(), calls=%async_computation.5 | async-start | bytes 294912
  424.1 2.0 copy-start.4
  429.7 1.5 copy-start.26
  431.4 188.3 %copy-start.1 = (bf16[256,128]{1,0:T(8,128)(2,1)S(1)}, bf16[256,128]{1,0:T(8,128)(2,1)}, u32[]{:S(2)}) copy-start(bf16[256,128]{1,0:T(8,128)(2,1)} %param.7) | copy-start | bytes 196612
Sparse Core Ops, SparseCore 0:
  50.4 206.8 all-reduce.8
  261.6 71.3 reduce-scatter.18
  335.7 127.2 reduce-scatter.12
  467.8 72.7 reduce-scatter.16
  545.4 74.2 reduce-scatter.14
where the time goes:
time: 628 us; the launch traced here: 626 us
  waiting for transfers between devices  402 us (64%)
  blocking collectives  70.2 us (11%)
  matrix products  68.4 us (11%)
  starting transfers between devices  39 us (6%)
  between operations  16.5 us (3%)
  local copies, waits for them, and re-layouts  15.8 us (3%)
  other arithmetic  14 us (2%)
    unnamed x11, waiting for transfers between devices  372 us
    unnamed x1, blocking collectives  70.2 us
    dot_general x54, matrix products, weight_grad(): lax.dot_general(piece, flat, (((0,), (0,)), ((), ())), preferred_element_...  38.4 us
    reduce_scatter x1, waiting for transfers between devices, shards(): lax.psum_scatter(grad_a, 'tm', scatter_dimension=0, tiled=True)  30.6 us
    ppermute x4, starting transfers between devices, with_halo(): before = lax.ppermute(last, axis, up)  18.2 us
    dot_general x54, matrix products, conv_taps(): lax.dot_general(piece, block, (((1,), (1,)), ((), ())), preferred_element...  14 us
    dot_general x54, matrix products, conv_taps(): total = total + jnp.dot(piece, block, preferred_element_type=jnp.float32)  13 us
  transfers between devices with their start and end apart: 19, of which 5 were waited for; matrix products, arithmetic and copies ran while one was open for 25% of the time, Pallas kernels for 0%

commit v1 on v0

--- a/solution.py
+++ b/solution.py
@@ -1,6 +1,8 @@
 import jax
 import jax.numpy as jnp
 from jax import lax
+from jax.experimental import pallas as pl
+from jax.experimental.pallas import tpu as pltpu
 from jax.sharding import PartitionSpec as P
 
 
@@ -60,10 +62,195 @@
                 piece = padded[kt : kt + frames, kr : kr + rows, kc : kc + width].reshape(-1, cin)
                 blocks.append(
                     lax.dot_general(
-                        piece, flat, (((0,), (0,)), ((), ())), preferred_element_type=jnp.float32
+                        flat, piece, (((0,), (0,)), ((), ())), preferred_element_type=jnp.float32
                     )
                 )
-    return jnp.concatenate(blocks, 0)
+    return jnp.concatenate(blocks, 1)
+
+
+LANES = 4480
+LX = 2304
+LY = LANES - LX
+
+
+def arranged(grad_a, grad_b, grad_proj):
+    part_a = grad_a.reshape(8, 2, 16, 2, 3456)
+    halves = jnp.stack([grad_b[:, : 14 * 128], grad_b[:, 13 * 128 :]], 1)
+    part_b = halves.reshape(8, 2, 8, 2, 2, 896).transpose(0, 1, 4, 2, 3, 5)
+    part_b = part_b.reshape(8, 2, 16, 2, 896)
+    part_p = grad_proj.reshape(8, 2, 8, 2, 128)
+    part_p = jnp.pad(part_p, ((0, 0), (0, 0), (0, 8), (0, 0), (0, 0)))
+    whole = jnp.concatenate([part_a, part_b, part_p], 4).astype(jnp.bfloat16)
+    return whole.reshape(8, 2, 16, 2 * LANES)
+
+
+def rs_kernel(
+    p_ref, o_ref, recv0, s0x, s0y, r1x, r1y, s1x, s1y, r2y, r2x, t_ref, msg, r3,
+    sem0, sem1x, sem1y, sem2y, sem2x, sem3,
+):
+    f32, bf16 = jnp.float32, jnp.bfloat16
+    tm = lax.axis_index("tm")
+    rows = lax.axis_index("rows")
+    core = lax.rem(tm, 2)
+    b = lax.rem(tm, 16)
+    y_lo = tm // 16
+    y_hi = rows // 4
+    x = lax.rem(rows, 4)
+    y = y_hi * 2 + y_lo
+
+    def x_peer(d):
+        return (tm, y_hi * 4 + lax.rem(x + d, 4))
+
+    def y_peer(d):
+        to = lax.rem(y + d, 4)
+        return (lax.rem(to, 2) * 16 + b, (to // 2) * 4 + x)
+
+    def z_peer(d):
+        return (y_lo * 16 + lax.rem(b + d, 16), rows)
+
+    partner = (tm + 1 - 2 * core, rows)
+
+    def remote(src, dst, sem, slot, to):
+        return pltpu.make_async_remote_copy(
+            src_ref=src, dst_ref=dst, send_sem=sem.at[0, slot], recv_sem=sem.at[1, slot],
+            device_id=to, device_id_type=pl.DeviceIdType.MESH,
+        )
+
+    barrier = pltpu.get_barrier_semaphore()
+    for d in range(1, 4):
+        pl.semaphore_signal(barrier, inc=1, device_id=x_peer(d), device_id_type=pl.DeviceIdType.MESH)
+        pl.semaphore_signal(barrier, inc=1, device_id=y_peer(d), device_id_type=pl.DeviceIdType.MESH)
+    for d in range(1, 16):
+        pl.semaphore_signal(barrier, inc=1, device_id=z_peer(d), device_id_type=pl.DeviceIdType.MESH)
+    pl.semaphore_wait(barrier, 21)
+
+    order = [1, 2, 3, 0]
+    core_copies = []
+    for k, d in enumerate(order):
+        for yh in range(2):
+            j = yh * 4 + lax.rem(x + d, 4)
+            cp = remote(p_ref.at[j, 1 - core], recv0.at[j], sem0, 2 * k + yh, partner)
+            cp.start()
+            core_copies.append(cp)
+
+    x_copies, y_copies = [], []
+    for k, d in enumerate(order):
+        to = lax.rem(x + d, 4)
+        for yh in range(2):
+            j = yh * 4 + to
+            core_copies[2 * k + yh].wait()
+            for yl in range(2):
+                at = yl * LANES
+                s0x[to, yh * 2 + yl] = (
+                    p_ref[j, core, :, at : at + LX].astype(f32)
+                    + recv0[j, :, at : at + LX].astype(f32)
+                ).astype(bf16)
+                s0y[yh * 2 + yl, to] = (
+                    p_ref[j, core, :, at + LX : at + LANES].astype(f32)
+                    + recv0[j, :, at + LX : at + LANES].astype(f32)
+                ).astype(bf16)
+        if d:
+            cp = remote(s0x.at[to], r1x.at[d - 1], sem1x, d - 1, x_peer(d))
+            cp.start()
+            x_copies.append(cp)
+    for d in range(1, 4):
+        cp = remote(s0y.at[lax.rem(y + d, 4)], r1y.at[d - 1], sem1y, d - 1, y_peer(d))
+        cp.start()
+        y_copies.append(cp)
+
+    for cp in x_copies:
+        cp.wait()
+    second = []
+    for d in order:
+        to = lax.rem(y + d, 4)
+        acc = s0x[x, to].astype(f32)
+        for s in range(3):
+            acc = acc + r1x[s, to].astype(f32)
+        s1x[to] = acc.astype(bf16)
+        if d:
+            cp = remote(s1x.at[to], r2y.at[d - 1], sem2y, d - 1, y_peer(d))
+            cp.start()
+            second.append(cp)
+    for cp in y_copies:
+        cp.wait()
+    for d in order:
+        to = lax.rem(x + d, 4)
+        acc = s0y[y, to].astype(f32)
+        for s in range(3):
+            acc = acc + r1y[s, to].astype(f32)
+        s1y[to] = acc.astype(bf16)
+        if d:
+            cp = remote(s1y.at[to], r2x.at[d - 1], sem2x, d - 1, x_peer(d))
+            cp.start()
+            second.append(cp)
+    for cp in second:
+        cp.wait()
+    acc = s1x[y].astype(f32)
+    for s in range(3):
+        acc = acc + r2y[s].astype(f32)
+    t_ref[:, :LX] = acc
+    acc = s1y[x].astype(f32)
+    for s in range(3):
+        acc = acc + r2x[s].astype(f32)
+    t_ref[:, LX:] = acc
+
+    part_b = jnp.concatenate([t_ref[0:8, 3456:4352], t_ref[8:16, 3456:4352]], 1)
+    part_b = jnp.where(y_lo == 0, part_b[:, 0:1728], part_b[:, 64:1792])
+    part_p = t_ref[0:8, 4352:4480]
+    for k in range(16):
+        msg[k] = jnp.zeros((16, 384), bf16)
+        msg[k, :, 0:216] = t_ref[:, 216 * k : 216 * k + 216].astype(bf16)
+        low = jnp.concatenate(
+            [
+                part_b[:, 108 * k : 108 * k + 108], jnp.zeros((8, 4), f32),
+                part_p[:, 8 * k : 8 * k + 8], jnp.zeros((8, 8), f32),
+            ], 1,
+        )
+        msg[k, :, 256:384] = jnp.concatenate([low, jnp.zeros((8, 128), f32)], 0).astype(bf16)
+    last = []
+    for d in range(1, 16):
+        cp = remote(msg.at[lax.rem(b + d, 16)], r3.at[d - 1], sem3, d - 1, z_peer(d))
+        cp.start()
+        last.append(cp)
+    for cp in last:
+        cp.wait()
+    same = msg[b].astype(f32)
+    for d in range(2, 16, 2):
+        same = same + r3[d - 1].astype(f32)
+    other = r3[0].astype(f32)
+    for d in range(3, 16, 2):
+        other = other + r3[d - 1].astype(f32)
+    o_ref[core] = same
+    o_ref[1 - core] = other
+
+
+def reduce_scattered(partial):
+    bf16 = jnp.bfloat16
+    dma = pltpu.SemaphoreType.DMA
+    return pl.pallas_call(
+        rs_kernel,
+        out_shape=jax.ShapeDtypeStruct((2, 16, 384), jnp.float32),
+        in_specs=[pl.BlockSpec(memory_space=pltpu.VMEM)],
+        out_specs=pl.BlockSpec(memory_space=pltpu.VMEM),
+        scratch_shapes=[
+            pltpu.VMEM((8, 16, 2 * LANES), bf16),
+            pltpu.VMEM((4, 4, 16, LX), bf16),
+            pltpu.VMEM((4, 4, 16, LY), bf16),
+            pltpu.VMEM((3, 4, 16, LX), bf16),
+            pltpu.VMEM((3, 4, 16, LY), bf16),
+            pltpu.VMEM((4, 16, LX), bf16),
+            pltpu.VMEM((4, 16, LY), bf16),
+            pltpu.VMEM((3, 16, LX), bf16),
+            pltpu.VMEM((3, 16, LY), bf16),
+            pltpu.VMEM((16, LANES), jnp.float32),
+            pltpu.VMEM((16, 16, 384), bf16),
+            pltpu.VMEM((15, 16, 384), bf16),
+            dma((2, 8)), dma((2, 3)), dma((2, 3)), dma((2, 3)), dma((2, 3)), dma((2, 15)),
+        ],
+        compiler_params=pltpu.CompilerParams(
+            collective_id=0, has_side_effects=True, vmem_limit_bytes=40 * 1024 * 1024
+        ),
+    )(partial)
 
 
 def with_rims(block):
@@ -103,12 +290,9 @@
     ).astype(jnp.bfloat16)
     total_cells = frames * lax.axis_size("tm") * rows * lax.axis_size("rows") * width
     scale = 1.0 / jnp.sqrt(jnp.float32(total_cells))
-    grad_b = weight_grad(mid_p, cotangent, frames, rows, width) * scale
-    grad_proj = (
-        lax.dot_general(
-            hidden, grad_mid, (((0,), (0,)), ((), ())), preferred_element_type=jnp.float32
-        )
-        * scale
+    grad_b = weight_grad(mid_p, cotangent, frames, rows, width)
+    grad_proj = lax.dot_general(
+        grad_mid, hidden, (((0,), (0,)), ((), ())), preferred_element_type=jnp.float32
     )
     grad_h = lax.dot_general(
         grad_mid, project, (((1,), (1,)), ((), ())), preferred_element_type=jnp.float32
@@ -118,23 +302,15 @@
     grad_pre_4 = grad_pre.reshape(frames, rows, width, chan_a)
     grad_pre_p = future_padded(grad_pre_4)
     grad_video = conv_taps(grad_pre_p, kernel_a, frames, rows, width, True)
-    grad_a = weight_grad(video_p, grad_pre_4, frames, rows, width) * scale
-    partial_value = (
-        lax.psum_scatter(grad_a, "tm", scatter_dimension=0, tiled=True),
-        lax.psum_scatter(grad_b, "tm", scatter_dimension=0, tiled=True),
-        lax.psum_scatter(grad_proj, "tm", scatter_dimension=0, tiled=True),
-    )
-    summed = (
-        lax.psum_scatter(partial_value[0], "rows", scatter_dimension=1, tiled=True),
-        lax.psum_scatter(partial_value[1], "rows", scatter_dimension=1, tiled=True),
-        lax.psum_scatter(partial_value[2], "rows", scatter_dimension=1, tiled=True),
-    )
+    grad_a = weight_grad(video_p, grad_pre_4, frames, rows, width)
+    partial = arranged(grad_a, grad_b, grad_proj)
+    summed = reduce_scattered(partial) * scale
     return (
         result.reshape(frames, rows, width, chan_b),
         grad_video.reshape(frames, rows, width, chan_a),
-        summed[0],
-        summed[1],
-        summed[2],
+        summed[:, :, 0:216].reshape(32, 216).T,
+        summed[:, 0:8, 256:364].reshape(16, 108).T,
+        summed[:, 0:8, 368:376].reshape(16, 8).T,
     )
 
 

time: 628 us -> 214 us (0.34)
  waiting for transfers between devices: 402 us -> 0.03 us
  blocking collectives: 70.2 us -> 0 us
  Pallas kernels: 0 us -> 51.5 us
  local copies, waits for them, and re-layouts: 15.8 us -> 39 us
  between operations: 16.5 us -> 1.95 us
  matrix products: 68.4 us -> 60.3 us
  other arithmetic: 14 us -> 20.5 us
    unnamed x11 -> x0, waiting for transfers between devices: 372 us -> none
    unnamed x1 -> x0, blocking collectives: 70.2 us -> none
    pallas_call x0 -> x1, Pallas kernels: none -> 51.5 us  [reduce_scattered(): pl.pallas_call(rs_kernel, out_shape=jax.ShapeDtypeStruct((2, 16, 384), jn...]
    reduce_scatter x1 -> x0, waiting for transfers between devices: 30.6 us -> none  [shards(): lax.psum_scatter(grad_a, 'tm', scatter_dimension=0, tiled=True)]
    concatenate x0 -> x1, other arithmetic: none -> 14.4 us  [arranged(): whole = jnp.concatenate([part_a, part_b, part_p], 4).astype(jnp.bfloat16)]
    reshape x0 -> x4, local copies, waits for them, and re-layouts: none -> 8.73 us  [the longest x1 7.95 us: arranged(): part_a = grad_a.reshape(8, 2, 16, 2, 3456)]
    dot_general x55, matrix products: 39.3 us -> 31 us  [the longest x54 30.8 us: weight_grad(): lax.dot_general(flat, piece, (((0,), (0,)), ((), ())), preferred_element_...]
    concatenate x0 -> x3, local copies, waits for them, and re-layouts: none -> 8.16 us  [weight_grad(): return jnp.concatenate(blocks, 1)]
  transfers between devices with their start and end apart: 19 -> 12, of which waited for: 5 -> 0; matrix products, arithmetic and copies ran while one was open for 25% -> 34% of each run, Pallas kernels for 0% -> 24%
where the time goes in v1:
time: 214 us; the launch traced here: 213 us
  matrix products  60.3 us (28%)
  Pallas kernels  51.5 us (24%)
  starting transfers between devices  39.2 us (18%)
  local copies, waits for them, and re-layouts  39 us (18%)
  other arithmetic  20.5 us (10%)
    pallas_call x1, Pallas kernels, reduce_scattered(): pl.pallas_call(rs_kernel, out_shape=jax.ShapeDtypeStruct((2, 16, 384), jn...  51.5 us
    dot_general x54, matrix products, weight_grad(): lax.dot_general(flat, piece, (((0,), (0,)), ((), ())), preferred_element_...  30.8 us
    ppermute x4, starting transfers between devices, with_halo(): before = lax.ppermute(last, axis, up)  19.8 us
    dot_general x54, matrix products, conv_taps(): total = total + jnp.dot(piece, block, preferred_element_type=jnp.float32)  16.1 us
    concatenate x1, other arithmetic, arranged(): whole = jnp.concatenate([part_a, part_b, part_p], 4).astype(jnp.bfloat16)  14.4 us
    ppermute x4, starting transfers between devices, passed_along(): return lax.ppermute(block, axis, route)  14.1 us
    dot_general x54, matrix products, conv_taps(): lax.dot_general(piece, block, (((1,), (1,)), ((), ())), preferred_element...  12.1 us
    concatenate x3, local copies, waits for them, and re-layouts, weight_grad(): return jnp.concatenate(blocks, 1)  8.16 us
  transfers between devices with their start and end apart: 12, of which 0 were waited for; matrix products, arithmetic and copies ran while one was open for 34% of the time, Pallas kernels for 24%

profile of v1, /device:TPU:1, one launch (start us, length us, event | category | flops | bytes accessed | tf_op | source)
XLA Modules:
  0.0 212.5 jit_solution(7719164825428385927)
XLA Ops:
  1.6 3.9 %collective-permute-start.6 = (bf16[2,1,96,128]{3,2,1,0:T(8,128)(2,1)S(1)}, bf16[2,1,96,128]{3,2,1,0:T(8,128)(2,1)S(1)}, u32[]{:S(2)}, u32[]{:S(2)}) collective-permute-start(bf16[2,1,96,128]{3,2,1,0:T(8,128)(2,1)S(1)} %get-tuple-element.112), channel_id=1, source_target_pairs={{0,1},{1,2},{2,3},{3,4},{4,5},{5,6},{6,7},{8,9},{9,10},{10,11},{11... | collective-permute-start | bytes 147464 | tf_op jit(solution)/shard_map/ppermute | solution.py:16
  5.5 1.3 collective-permute-start.7
  6.8 1.0 fusion.310
  7.8 4.0 %collective-permute-start = (bf16[2,1,96,256]{3,2,1,0:T(8,128)(2,1)S(1)}, bf16[2,1,96,256]{3,2,1,0:T(8,128)(2,1)S(1)}, u32[]{:S(2)}, u32[]{:S(2)}) collective-permute-start(bf16[2,1,96,256]{3,2,1,0:T(8,128)(2,1)S(1)} %get-tuple-element.107), channel_id=1, source_target_pairs={{0,1},{1,2},{2,3},{3,4},{4,5},{5,6},{6,7},{8,9},{9,10},{10,11},{11... | collective-permute-start | bytes 294920 | tf_op jit(solution)/shard_map/ppermute | solution.py:16
  11.8 1.3 collective-permute-start.1
  13.1 1.0 pad_maximum_fusion.9
  14.2 3.4 %collective-permute-start.8 = (bf16[2,4,96,128]{3,2,1,0:T(8,128)(2,1)S(1)}, bf16[2,4,96,128]{3,2,1,0:T(8,128)(2,1)S(1)}, u32[]{:S(2)}, u32[]{:S(2)}) collective-permute-start(bf16[2,4,96,128]{3,2,1,0:T(8,128)(2,1)S(1)} %constant_dynamic-update-slice_fusion.3), channel_id=1, source_target_pairs={{8,0},{16,8},{24,16},{32,24},{40,32},{48,40},{56,48},{64,56},{72,6... | collective-permute-start | bytes 589832 | tf_op jit(solution)/shard_map/ppermute | solution.py:25
  17.6 1.1 pad_maximum_fusion.6
  18.7 5.6 %collective-permute-start.2 = (bf16[2,4,96,256]{3,2,1,0:T(8,128)(2,1)S(1)}, bf16[2,4,96,256]{3,2,1,0:T(8,128)(2,1)S(1)}, u32[]{:S(2)}, u32[]{:S(2)}) collective-permute-start(bf16[2,4,96,256]{3,2,1,0:T(8,128)(2,1)S(1)} %constant_dynamic-update-slice_fusion), channel_id=1, source_target_pairs={{0,8},{8,16},{16,24},{24,32},{32,40},{40,48},{48,56},{56,64},{64,7... | collective-permute-start | bytes 1179656 | tf_op jit(solution)/shard_map/ppermute | solution.py:25
  30.6 1.1 copy-done.5
  39.0 0.9 fusion.47
  39.9 0.9 fusion.46
  42.7 0.9 fusion.43
  44.5 0.9 fusion.41
  46.4 0.9 fusion.39
  47.3 0.9 fusion.38
  48.2 0.9 fusion.37
  49.1 0.9 fusion.36
  51.9 0.9 fusion.33
  53.7 0.9 fusion.31
  54.7 0.9 fusion.30
  55.6 0.9 fusion.29
  61.1 0.9 fusion.23
  62.1 0.9 fusion.22
  63.9 3.4 %collective-permute-start.3 = (bf16[2,1,96,128]{3,2,1,0:T(8,128)(2,1)S(1)}, bf16[2,1,96,128]{3,2,1,0:T(8,128)(2,1)S(1)}, u32[]{:S(2)}, u32[]{:S(2)}) collective-permute-start(bf16[2,1,96,128]{3,2,1,0:T(8,128)(2,1)S(1)} %get-tuple-element.115), channel_id=1, source_target_pairs={{0,1},{1,2},{2,3},{3,4},{4,5},{5,6},{6,7},{8,9},{9,10},{10,11},{11... | collective-permute-start | bytes 147464 | tf_op jit(solution)/shard_map/ppermute | solution.py:16
  67.3 1.5 collective-permute-start.4
  68.8 5.9 %copy.14 = bf16[256,6912]{1,0:T(8,128)(2,1)} copy(bf16[256,6912]{0,1:T(8,128)(2,1)} %fusion.21) | data formatting | bytes 7077888 | tf_op jit(solution)/shard_map/concatenate | solution.py:68
  74.8 7.9 %reshape.541 = bf16[8,2,16,2,3456]{4,3,2,1,0:T(2,128)(2,1)} reshape(bf16[256,6912]{1,0:T(8,128)(2,1)} %copy.14) | data formatting | bytes 7077888 | tf_op jit(solution)/shard_map/reshape | solution.py:77
  82.8 1.3 collective-permute-start.10
  84.1 8.5 %collective-permute-start.9 = (bf16[2,1,96,256]{3,2,1,0:T(8,128)(2,1)S(1)}, bf16[2,1,96,256]{3,2,1,0:T(8,128)(2,1)S(1)}, u32[]{:S(2)}, u32[]{:S(2)}) collective-permute-start(bf16[2,1,96,256]{3,2,1,0:T(8,128)(2,1)S(1)} %get-tuple-element.95), channel_id=1, source_target_pairs={{0,1},{1,2},{2,3},{3,4},{4,5},{5,6},{6,7},{8,9},{9,10},{10,11},{11... | collective-permute-start | bytes 294920 | tf_op jit(solution)/shard_map/ppermute | solution.py:16
  92.6 3.1 %collective-permute-start.5 = (bf16[2,4,96,128]{3,2,1,0:T(8,128)(2,1)S(1)}, bf16[2,4,96,128]{3,2,1,0:T(8,128)(2,1)S(1)}, u32[]{:S(2)}, u32[]{:S(2)}) collective-permute-start(bf16[2,4,96,128]{3,2,1,0:T(8,128)(2,1)S(1)} %pad_maximum_fusion.8), channel_id=1, source_target_pairs={{0,8},{8,16},{16,24},{24,32},{32,40},{40,48},{48,56},{56,64},{64,7... | collective-permute-start | bytes 589832 | tf_op jit(solution)/shard_map/ppermute | solution.py:25
  97.3 1.9 collective-permute-start.11
  106.4 2.0 copy.15
  108.4 1.1 stack.9
  109.5 1.3 maximum_bitcast_fusion
  110.8 0.9 copy.17
  111.8 14.4 %fusion = bf16[8,2,16,2,4480]{4,3,2,1,0:T(2,128)(2,1)} fusion(bf16[8,2,8,2,128]{4,3,2,1,0:T(2,128)(2,1)S(1)} %copy.18, bf16[8,2,16,2,896]{4,3,2,1,0:T(2,128)(2,1)S(1)} %bitcast.713, bf16[8,2,16,2,3456]{4,3,2,1,0:T(2,128)(2,1)S(1)} %copy-done.4), kind=kLoop, calls=%fused_computation.1 | loop fusion | flops 18350080 | bytes 9109504 | tf_op jit(solution)/shard_map/concatenate | solution.py:83
  126.2 7.9 %convert_element_type.33.p_ref = bf16[8,2,16,8960]{3,2,1,0:T(8,128)(2,1)} reshape(bf16[8,2,16,2,4480]{4,3,2,1,0:T(2,128)(2,1)} %fusion) | data formatting | bytes 9175040 | tf_op jit(solution)/shard_map/convert_element_type | solution.py:83
  134.1 2.3 %copy-done.2 = bf16[8,2,16,8960]{3,2,1,0:T(8,128)(2,1)S(1)} copy-done((bf16[8,2,16,8960]{3,2,1,0:T(8,128)(2,1)S(1)}, bf16[8,2,16,8960]{3,2,1,0:T(8,128)(2,1)}, u32[]{:S(2)}) %copy-start.2) | copy-done | bytes 4587544
  136.4 51.5 %shard_map.92 = f32[2,16,384]{2,1,0:T(8,128)S(1)} custom-call(bf16[8,2,16,8960]{3,2,1,0:T(8,128)(2,1)S(1)} %copy-done.2), custom_call_target="tpu_custom_call" | custom-call | tf_op jit(solution)/shard_map/pallas_call | solution.py:230
  191.7 1.0 fusion.267
  192.7 1.1 fusion.255
  193.8 1.0 fusion.247
  194.8 1.0 fusion.221
  196.1 1.1 convolution_add_fusion.86
  197.1 1.1 convolution_add_fusion.85
  203.7 1.3 copy-done.6
  211.6 1.0 fusion.9
  (228 shorter events, 50.3 us)
Async XLA Ops:
  0.6 37.0 %copy-start = (bf16[256,128]{1,0:T(8,128)(2,1)S(1)}, bf16[256,128]{1,0:T(8,128)(2,1)}, u32[]{:S(2)}) copy-start(bf16[256,128]{1,0:T(8,128)(2,1)} %param.7) | copy-start | bytes 196612
  0.6 24.1 %copy-start.7 = (bf16[3456,128]{1,0:T(8,128)(2,1)S(1)}, bf16[3456,128]{1,0:T(8,128)(2,1)}, u32[]{:S(2)}) copy-start(bf16[3456,128]{1,0:T(8,128)(2,1)} %param.8) | copy-start | bytes 2654212
  1.6 11.5 %collective-permute-start.6 = (bf16[2,1,96,128]{3,2,1,0:T(8,128)(2,1)S(1)}, bf16[2,1,96,128]{3,2,1,0:T(8,128)(2,1)S(1)}, u32[]{:S(2)}, u32[]{:S(2)}) collective-permute-start(bf16[2,1,96,128]{3,2,1,0:T(8,128)(2,1)S(1)} %get-tuple-element.112), channel_id=1, source_target_pairs={{0,1},{1,2},{2,3},{3,4},{4,5},{5,6},{6,7},{8,9},{9,10},{10,11},{11... | collective-permute-start | bytes 147464 | tf_op jit(solution)/shard_map/ppermute | solution.py:16
  5.5 7.6 %collective-permute-start.7 = (bf16[2,1,96,128]{3,2,1,0:T(8,128)(2,1)S(1)}, bf16[2,1,96,128]{3,2,1,0:T(8,128)(2,1)S(1)}, u32[]{:S(2)}, u32[]{:S(2)}) collective-permute-start(bf16[2,1,96,128]{3,2,1,0:T(8,128)(2,1)S(1)} %get-tuple-element.111), channel_id=1, source_target_pairs={{1,0},{2,1},{3,2},{4,3},{5,4},{6,5},{7,6},{9,8},{10,9},{11,10},{12... | collective-permute-start | bytes 147464 | tf_op jit(solution)/shard_map/ppermute | solution.py:17
  7.8 9.8 %collective-permute-start = (bf16[2,1,96,256]{3,2,1,0:T(8,128)(2,1)S(1)}, bf16[2,1,96,256]{3,2,1,0:T(8,128)(2,1)S(1)}, u32[]{:S(2)}, u32[]{:S(2)}) collective-permute-start(bf16[2,1,96,256]{3,2,1,0:T(8,128)(2,1)S(1)} %get-tuple-element.107), channel_id=1, source_target_pairs={{0,1},{1,2},{2,3},{3,4},{4,5},{5,6},{6,7},{8,9},{9,10},{10,11},{11... | collective-permute-start | bytes 294920 | tf_op jit(solution)/shard_map/ppermute | solution.py:16
  11.8 5.8 %collective-permute-start.1 = (bf16[2,1,96,256]{3,2,1,0:T(8,128)(2,1)S(1)}, bf16[2,1,96,256]{3,2,1,0:T(8,128)(2,1)S(1)}, u32[]{:S(2)}, u32[]{:S(2)}) collective-permute-start(bf16[2,1,96,256]{3,2,1,0:T(8,128)(2,1)S(1)} %get-tuple-element.106), channel_id=1, source_target_pairs={{1,0},{2,1},{3,2},{4,3},{5,4},{6,5},{7,6},{9,8},{10,9},{11,10},{12... | collective-permute-start | bytes 294920 | tf_op jit(solution)/shard_map/ppermute | solution.py:17
  14.2 10.2 %collective-permute-start.8 = (bf16[2,4,96,128]{3,2,1,0:T(8,128)(2,1)S(1)}, bf16[2,4,96,128]{3,2,1,0:T(8,128)(2,1)S(1)}, u32[]{:S(2)}, u32[]{:S(2)}) collective-permute-start(bf16[2,4,96,128]{3,2,1,0:T(8,128)(2,1)S(1)} %constant_dynamic-update-slice_fusion.3), channel_id=1, source_target_pairs={{8,0},{16,8},{24,16},{32,24},{40,32},{48,40},{56,48},{64,56},{72,6... | collective-permute-start | bytes 589832 | tf_op jit(solution)/shard_map/ppermute | solution.py:25
  18.7 11.1 %collective-permute-start.2 = (bf16[2,4,96,256]{3,2,1,0:T(8,128)(2,1)S(1)}, bf16[2,4,96,256]{3,2,1,0:T(8,128)(2,1)S(1)}, u32[]{:S(2)}, u32[]{:S(2)}) collective-permute-start(bf16[2,4,96,256]{3,2,1,0:T(8,128)(2,1)S(1)} %constant_dynamic-update-slice_fusion), channel_id=1, source_target_pairs={{0,8},{8,16},{16,24},{24,32},{32,40},{40,48},{48,56},{56,64},{64,7... | collective-permute-start | bytes 1179656 | tf_op jit(solution)/shard_map/ppermute | solution.py:25
  26.5 2.4 %copy-start.3 = (bf16[2,2,96,128]{3,2,1,0:T(8,128)(2,1)S(1)}, bf16[2,2,96,128]{3,2,1,0:T(8,128)(2,1)}, u32[]{:S(2)}) copy-start(bf16[2,2,96,128]{3,2,1,0:T(8,128)(2,1)} %param.9) | copy-start | bytes 294916
  29.6 2.0 copy-start.5
  35.3 1.3 copy-start.8
  63.9 28.7 %collective-permute-start.3 = (bf16[2,1,96,128]{3,2,1,0:T(8,128)(2,1)S(1)}, bf16[2,1,96,128]{3,2,1,0:T(8,128)(2,1)S(1)}, u32[]{:S(2)}, u32[]{:S(2)}) collective-permute-start(bf16[2,1,96,128]{3,2,1,0:T(8,128)(2,1)S(1)} %get-tuple-element.115), channel_id=1, source_target_pairs={{0,1},{1,2},{2,3},{3,4},{4,5},{5,6},{6,7},{8,9},{9,10},{10,11},{11... | collective-permute-start | bytes 147464 | tf_op jit(solution)/shard_map/ppermute | solution.py:16
  67.3 25.3 %collective-permute-start.4 = (bf16[2,1,96,128]{3,2,1,0:T(8,128)(2,1)S(1)}, bf16[2,1,96,128]{3,2,1,0:T(8,128)(2,1)S(1)}, u32[]{:S(2)}, u32[]{:S(2)}) collective-permute-start(bf16[2,1,96,128]{3,2,1,0:T(8,128)(2,1)S(1)} %get-tuple-element.116), channel_id=1, source_target_pairs={{1,0},{2,1},{3,2},{4,3},{5,4},{6,5},{7,6},{9,8},{10,9},{11,10},{12... | collective-permute-start | bytes 147464 | tf_op jit(solution)/shard_map/ppermute | solution.py:17
  82.8 13.7 %collective-permute-start.10 = (bf16[2,1,96,256]{3,2,1,0:T(8,128)(2,1)S(1)}, bf16[2,1,96,256]{3,2,1,0:T(8,128)(2,1)S(1)}, u32[]{:S(2)}, u32[]{:S(2)}) collective-permute-start(bf16[2,1,96,256]{3,2,1,0:T(8,128)(2,1)S(1)} %get-tuple-element.96), channel_id=1, source_target_pairs={{1,0},{2,1},{3,2},{4,3},{5,4},{6,5},{7,6},{9,8},{10,9},{11,10},{12... | collective-permute-start | bytes 294920 | tf_op jit(solution)/shard_map/ppermute | solution.py:17
  84.1 12.4 %collective-permute-start.9 = (bf16[2,1,96,256]{3,2,1,0:T(8,128)(2,1)S(1)}, bf16[2,1,96,256]{3,2,1,0:T(8,128)(2,1)S(1)}, u32[]{:S(2)}, u32[]{:S(2)}) collective-permute-start(bf16[2,1,96,256]{3,2,1,0:T(8,128)(2,1)S(1)} %get-tuple-element.95), channel_id=1, source_target_pairs={{0,1},{1,2},{2,3},{3,4},{4,5},{5,6},{6,7},{8,9},{9,10},{10,11},{11... | collective-permute-start | bytes 294920 | tf_op jit(solution)/shard_map/ppermute | solution.py:16
  92.6 7.3 %collective-permute-start.5 = (bf16[2,4,96,128]{3,2,1,0:T(8,128)(2,1)S(1)}, bf16[2,4,96,128]{3,2,1,0:T(8,128)(2,1)S(1)}, u32[]{:S(2)}, u32[]{:S(2)}) collective-permute-start(bf16[2,4,96,128]{3,2,1,0:T(8,128)(2,1)S(1)} %pad_maximum_fusion.8), channel_id=1, source_target_pairs={{0,8},{8,16},{16,24},{24,32},{32,40},{40,48},{48,56},{56,64},{64,7... | collective-permute-start | bytes 589832 | tf_op jit(solution)/shard_map/ppermute | solution.py:25
  97.3 105.6 %collective-permute-start.11 = (bf16[2,4,96,256]{3,2,1,0:T(8,128)(2,1)}, bf16[2,4,96,256]{3,2,1,0:T(8,128)(2,1)S(1)}, u32[]{:S(2)}, u32[]{:S(2)}) collective-permute-start(bf16[2,4,96,256]{3,2,1,0:T(8,128)(2,1)} %pad_maximum_fusion.3), channel_id=1, source_target_pairs={{8,0},{16,8},{24,16},{32,24},{40,32},{48,40},{56,48},{64,56},{72,6... | collective-permute-start | bytes 1179656 | tf_op jit(solution)/shard_map/ppermute | solution.py:25
  103.1 2.7 %copy-start.12 = (bf16[128,1792]{0,1:T(8,128)(2,1)}, bf16[128,1792]{0,1:T(8,128)(2,1)S(1)}, u32[]{:S(2)}) copy-start(bf16[128,1792]{0,1:T(8,128)(2,1)S(1)} %get-tuple-element.117) | copy-start | bytes 1376260
  109.5 2.3 %copy-start.4 = (bf16[8,2,16,2,3456]{4,3,2,1,0:T(2,128)(2,1)S(1)}, bf16[8,2,16,2,3456]{4,3,2,1,0:T(2,128)(2,1)}, u32[]{:S(2)}) copy-start(bf16[8,2,16,2,3456]{4,3,2,1,0:T(2,128)(2,1)} %reshape.541) | copy-start | bytes 10616836
  134.1 2.3 %copy-start.2 = (bf16[8,2,16,8960]{3,2,1,0:T(8,128)(2,1)S(1)}, bf16[8,2,16,8960]{3,2,1,0:T(8,128)(2,1)}, u32[]{:S(2)}) copy-start(bf16[8,2,16,8960]{3,2,1,0:T(8,128)(2,1)} %convert_element_type.33.p_ref) | copy-start | bytes 13762564
  191.0 7.4 %copy-start.15 = (bf16[2,2,96,128]{3,2,1,0:T(8,128)(2,1)S(1)}, bf16[2,2,96,128]{3,2,1,0:T(8,128)(2,1)}, u32[]{:S(2)}) copy-start(bf16[2,2,96,128]{3,2,1,0:T(8,128)(2,1)} %get-tuple-element.74) | copy-start | bytes 294916
  191.0 7.7 %copy-start.13 = (bf16[2,2,96,128]{3,2,1,0:T(8,128)(2,1)S(1)}, bf16[2,2,96,128]{3,2,1,0:T(8,128)(2,1)}, u32[]{:S(2)}) copy-start(bf16[2,2,96,128]{3,2,1,0:T(8,128)(2,1)} %get-tuple-element.76) | copy-start | bytes 294916
  191.0 7.9 %copy-start.14 = (bf16[2,2,96,128]{3,2,1,0:T(8,128)(2,1)S(1)}, bf16[2,2,96,128]{3,2,1,0:T(8,128)(2,1)}, u32[]{:S(2)}) copy-start(bf16[2,2,96,128]{3,2,1,0:T(8,128)(2,1)} %get-tuple-element.89) | copy-start | bytes 294916
  198.2 2.2 %copy-start.18 = (bf16[2,2,96,128]{3,2,1,0:T(8,128)(2,1)S(1)}, bf16[2,2,96,128]{3,2,1,0:T(8,128)(2,1)}, u32[]{:S(2)}) copy-start(bf16[2,2,96,128]{3,2,1,0:T(8,128)(2,1)} %get-tuple-element.114) | copy-start | bytes 294916
  198.7 2.2 %copy-start.17 = (bf16[2,2,96,128]{3,2,1,0:T(8,128)(2,1)S(1)}, bf16[2,2,96,128]{3,2,1,0:T(8,128)(2,1)}, u32[]{:S(2)}) copy-start(bf16[2,2,96,128]{3,2,1,0:T(8,128)(2,1)} %get-tuple-element.87) | copy-start | bytes 294916
  199.2 2.8 %copy-start.9 = (f32[384,128]{1,0:T(8,128)S(1)}, f32[384,128]{1,0:T(8,128)}, u32[]{:S(2)}) copy-start(f32[384,128]{1,0:T(8,128)} %get-tuple-element.122) | copy-start | bytes 589828
  199.2 2.8 %copy-start.16 = (bf16[2,2,96,128]{3,2,1,0:T(8,128)(2,1)S(1)}, bf16[2,2,96,128]{3,2,1,0:T(8,128)(2,1)}, u32[]{:S(2)}) copy-start(bf16[2,2,96,128]{3,2,1,0:T(8,128)(2,1)} %get-tuple-element.113) | copy-start | bytes 294916
  203.0 2.0 copy-start.6
  208.5 1.5 copy-start.11
  210.0 1.5 copy-start.10
  210.0 2.5 %copy-start.1 = (bf16[256,128]{1,0:T(8,128)(2,1)S(1)}, bf16[256,128]{1,0:T(8,128)(2,1)}, u32[]{:S(2)}) copy-start(bf16[256,128]{1,0:T(8,128)(2,1)} %param.7) | copy-start | bytes 196612

commit v2 on v0

v2 whole, which is shorter than its diff:
```python
import jax
import jax.numpy as jnp
from jax import lax
from jax.experimental import pallas as pl
from jax.experimental.pallas import tpu as pltpu
from jax.sharding import PartitionSpec as P

F32, BF16 = jnp.float32, jnp.bfloat16
MESH = pl.DeviceIdType.MESH
CA, CB, W = 256, 128, 96
CELLS = 4 * W
HALF_A = 27 * CA // 2
XA, YA = 1792, HALF_A - 1792
XB, YB = 512, 512
PB = 896
ORDER = (1, 2, 3, 0)


def dot(a, b, ca=1, cb=0):
    return lax.dot_general(a, b, (((ca,), (cb,)), ((), ())), preferred_element_type=F32)


def kernel(
    video, cot, ka_hbm, project, kb_hbm,
    out, grad_video, grad_a, grad_b, grad_p,
    ka, kb, vbuf, cbuf, mbuf, gbuf, mown, gown, xs, us, ms, gs,
    gt, ct, qt, send_a, recv_a, send_b, recv_b, part,
    s0xa, s0ya, r1xa, r1ya, s1xa, s1ya, r2ya, r2xa,
    s0xb, s0yb, r1xb, r1yb, s1xb, s1yb, r2yb, r2xb,
    t_a, t_b, msg, r3, total,
    sem_w, sem_v, sem_c, sem_m, sem_g, sem_a, sem_b,
    sem1xa, sem1ya, sem2ya, sem2xa, sem1xb, sem1yb, sem2yb, sem2xb, sem3,
):
    tm = lax.axis_index("tm")
    rows = lax.axis_index("rows")
    core = lax.rem(tm, 2)
    b = lax.rem(tm, 16)
    y_lo = tm // 16
    x = lax.rem(rows, 4)
    y = (rows // 4) * 2 + y_lo

    def x_peer(d):
        return (tm, (rows // 4) * 4 + lax.rem(x + d, 4))

    def y_peer(d):
        to = lax.rem(y + d, 4)
        return (lax.rem(to, 2) * 16 + b, (to // 2) * 4 + x)

    def z_peer(d):
        return (y_lo * 16 + lax.rem(b + d, 16), rows)

    def near(dt, dr):
        return (lax.rem(tm + 32 + dt, 32), lax.rem(rows + 8 + dr, 8))

    partner = (tm + 1 - 2 * core, rows)

    def remote(src, dst, sem, slot, to):
        return pltpu.make_async_remote_copy(
            src_ref=src, dst_ref=dst, send_sem=sem.at[0, slot], recv_sem=sem.at[1, slot],
            device_id=to, device_id_type=MESH,
        )

    load_b = pltpu.make_async_copy(kb_hbm, kb, sem_w.at[0])
    load_a = pltpu.make_async_copy(ka_hbm, ka, sem_w.at[1])
    load_b.start()
    load_a.start()

    barrier = pltpu.get_barrier_semaphore()
    peers = [near(dt, dr) for dt in (-1, 0, 1) for dr in (-1, 0, 1) if dt or dr]
    peers += [x_peer(d) for d in range(1, 4)] + [y_peer(d) for d in range(1, 4)]
    peers += [z_peer(d) for d in range(1, 16)]
    for to in peers:
        pl.semaphore_signal(barrier, inc=1, device_id=to, device_id_type=MESH)
    pl.semaphore_wait(barrier, len(peers))

    def halo(src, buf, way, sem):
        own = 2 if way > 0 else 0
        other = 2 - own
        copies = [
            remote(src, buf.at[pl.ds(other, 2), pl.ds(1, 2)], sem, 0, near(way, 0)),
            remote(src.at[:, 1], buf.at[pl.ds(own, 2), 0], sem, 1, near(0, 1)),
            remote(src.at[:, 0], buf.at[pl.ds(own, 2), 3], sem, 2, near(0, -1)),
            remote(src.at[:, 1], buf.at[pl.ds(other, 2), 0], sem, 3, near(way, 1)),
            remote(src.at[:, 0], buf.at[pl.ds(other, 2), 3], sem, 4, near(way, -1)),
        ]
        for cp in copies:
            cp.start()
        return copies

    def shifted(src, buf, dst, way, chan):
        own = 2 if way > 0 else 0
        inside = (tm > 0) if way > 0 else (tm < 31)
        cell = lax.broadcasted_iota(jnp.int32, (W, chan), 0)
        for f in range(4):
            mine = own <= f < own + 2
            for r in range(4):
                if mine and 1 <= r <= 2:
                    v = src[f - own, r - 1].astype(F32)
                else:
                    keep = None if mine else inside
                    if r == 0:
                        keep = (rows > 0) if keep is None else keep & (rows > 0)
                    if r == 3:
                        keep = (rows < 7) if keep is None else keep & (rows < 7)
                    v = jnp.where(keep, buf[f, r].astype(F32), 0.0)
                dst[f, r, :, chan : 2 * chan] = v.astype(BF16)
                left = jnp.where(cell == 0, 0.0, pltpu.roll(v, 1, 0))
                right = jnp.where(cell == W - 1, 0.0, pltpu.roll(v, W - 1, 0))
                dst[f, r, :, 0:chan] = left.astype(BF16)
                dst[f, r, :, 2 * chan : 3 * chan] = right.astype(BF16)

    def conv(src, weight, chan):
        acc = None
        for kt in range(3):
            for kr in range(3):
                at = (3 * kt + kr) * 3 * chan
                piece = src[kt : kt + 2, kr : kr + 2].reshape(CELLS, 3 * chan)
                term = dot(piece, weight[at : at + 3 * chan])
                acc = term if acc is None else acc + term
        return acc

    def back(src, weight, chan):
        acc = None
        for kt in range(3):
            for kr in range(3):
                for kc in range(3):
                    at = (9 * kt + 3 * kr + kc) * chan
                    piece = src[2 - kt : 4 - kt, 2 - kr : 4 - kr, :, (2 - kc) * chan : (3 - kc) * chan]
                    term = dot(piece.reshape(CELLS, chan), weight[at : at + chan], 1, 1)
                    acc = term if acc is None else acc + term
        return acc

    halo_c = halo(cot, cbuf, -1, sem_c)
    halo_v = halo(video, vbuf, 1, sem_v)

    load_b.wait()
    for cp in halo_c:
        cp.wait()
    shifted(cot, cbuf, us, -1, CB)
    grad_mid = cot[...].reshape(CELLS, CB).astype(F32) + back(us, kb, CB)
    cot_t = cot[...].reshape(CELLS, CB).astype(F32).T
    mid_t = grad_mid.T
    for c in range(2):
        pick = [slice(16 * j + 8 * c, 16 * j + 8 * c + 8) for j in range(8)]
        ct[c] = jnp.concatenate([cot_t[s] for s in pick], 0).astype(BF16)
        qt[c] = jnp.concatenate([mid_t[s] for s in pick], 0).astype(BF16)
    grad_h = dot(grad_mid.astype(BF16), project[...], 1, 1)

    load_a.wait()
    for cp in halo_v:
        cp.wait()
    shifted(video, vbuf, xs, 1, CA)
    pre = conv(xs, ka, CA)
    sig = jax.nn.sigmoid(pre)
    hidden = (pre * sig).astype(BF16)
    mid = dot(hidden, project[...])
    mown[...] = mid.astype(BF16).reshape(2, 2, W, CB)
    halo_m = halo(mown, mbuf, 1, sem_m)
    grad_pre = grad_h * sig * (1.0 + pre * (1.0 - sig))
    gown[...] = grad_pre.astype(BF16).reshape(2, 2, W, CA)
    halo_g = halo(gown, gbuf, -1, sem_g)
    out[...] = mid.reshape(2, 2, W, CB)
    grad_t = grad_pre.T
    for c in range(2):
        for j in range(8):
            gt[c, j] = grad_t[32 * j + 16 * c : 32 * j + 16 * c + 16].astype(BF16)

    def grad_chunk(src, left, k, chan):
        kt, kr = k // 3, k % 3
        piece = src[kt : kt + 2, kr : kr + 2].reshape(CELLS, 3 * chan)
        return dot(left, piece)

    copies_a = []
    theirs = gt[1 - core].reshape(128, CELLS)
    for k in range(9):
        send_a[k] = grad_chunk(xs, theirs, k, CA).astype(BF16).reshape(8, 16, 768)
        cp = remote(send_a.at[k], recv_a.at[k], sem_a, k, partner)
        cp.start()
        copies_a.append(cp)
    proj_theirs = dot(qt[1 - core], hidden)
    proj_mine = dot(qt[core], hidden)

    mine = gt[core].reshape(128, CELLS)
    cuts = sorted({768 * k for k in range(10)} | {0, XA, HALF_A, HALF_A + XA, 2 * HALF_A})
    for k in range(9):
        value = grad_chunk(xs, mine, k, CA)
        copies_a[k].wait()
        value = (value + recv_a[k].reshape(128, 768).astype(F32)).astype(BF16)
        inside = [c for c in cuts if 768 * k <= c <= 768 * k + 768]
        for lo, hi in zip(inside[:-1], inside[1:]):
            yl, at = lo // HALF_A, lo % HALF_A
            for j in range(8):
                cut = value[16 * j : 16 * j + 16, lo - 768 * k : hi - 768 * k]
                if at < XA:
                    s0xa[j % 4, (j // 4) * 2 + yl, :, at : at + hi - lo] = cut
                else:
                    s0ya[(j // 4) * 2 + yl, j % 4, :, at - XA : at - XA + hi - lo] = cut

    def first(s0x, r1x, sem1x, s0y, r1y, sem1y):
        in_x, in_y = [], []
        for d in (2, 1, 3):
            cp = remote(s0x.at[lax.rem(x + d, 4)], r1x.at[d - 1], sem1x, d - 1, x_peer(d))
            cp.start()
            in_x.append(cp)
            cp = remote(s0y.at[lax.rem(y + d, 4)], r1y.at[d - 1], sem1y, d - 1, y_peer(d))
            cp.start()
            in_y.append(cp)
        return in_x, in_y

    def second(copies, s0x, r1x, s1x, r2y, sem2y, s0y, r1y, s1y, r2x, sem2x):
        started = []
        for cp in copies[0]:
            cp.wait()
        for d in ORDER:
            to = lax.rem(y + d, 4)
            acc = s0x[x, to].astype(F32)
            for s in range(3):
                acc = acc + r1x[s, to].astype(F32)
            s1x[to] = acc.astype(BF16)
            if d:
                cp = remote(s1x.at[to], r2y.at[d - 1], sem2y, d - 1, y_peer(d))
                cp.start()
                started.append(cp)
        for cp in copies[1]:
            cp.wait()
        for d in ORDER:
            to = lax.rem(x + d, 4)
            acc = s0y[y, to].astype(F32)
            for s in range(3):
                acc = acc + r1y[s, to].astype(F32)
            s1y[to] = acc.astype(BF16)
            if d:
                cp = remote(s1y.at[to], r2x.at[d - 1], sem2x, d - 1, x_peer(d))
                cp.start()
                started.append(cp)
        return started

    def summed(copies, s1x, r2y, s1y, r2x, t_ref, lx):
        for cp in copies:
            cp.wait()
        acc = s1x[y].astype(F32)
        for s in range(3):
            acc = acc + r2y[s].astype(F32)
        t_ref[:, :lx] = acc
        acc = s1y[x].astype(F32)
        for s in range(3):
            acc = acc + r2x[s].astype(F32)
        t_ref[:, lx:] = acc

    first_a = first(s0xa, r1xa, sem1xa, s0ya, r1ya, sem1ya)

    for cp in halo_m:
        cp.wait()
    shifted(mown, mbuf, ms, 1, CB)

    def packed(half, proj):
        left = ct[half]
        for k in range(9):
            part[:, 384 * k : 384 * k + 384] = grad_chunk(ms, left, k, CB)
        blocks = []
        for j in range(8):
            row = slice(8 * j, 8 * j + 8)
            for yl in range(2):
                at = 13 * 128 * yl
                body = jnp.concatenate([part[row, at : at + PB], part[row, at + PB : at + 2 * PB]], 0)
                tail = jnp.concatenate([proj[row, 128 * yl : 128 * yl + 128], jnp.zeros((8, 128), F32)], 0)
                blocks.append((j, yl, jnp.concatenate([body, tail], 1)))
        return blocks

    for j, yl, value in packed(1 - core, proj_theirs):
        send_b[j, yl] = value.astype(BF16)
    copy_b = remote(send_b, recv_b, sem_b, 0, partner)
    copy_b.start()
    out[...] = out[...] + conv(ms, kb, CB).reshape(2, 2, W, CB)
    blocks = packed(core, proj_mine)
    copy_b.wait()
    for j, yl, value in blocks:
        value = (value + recv_b[j, yl].astype(F32)).astype(BF16)
        s0xb[j % 4, (j // 4) * 2 + yl] = value[:, :XB]
        s0yb[(j // 4) * 2 + yl, j % 4] = value[:, XB:]
    first_b = first(s0xb, r1xb, sem1xb, s0yb, r1yb, sem1yb)

    for cp in halo_g:
        cp.wait()
    shifted(gown, gbuf, gs, -1, CA)
    grad_video[...] = back(gs, ka, CA).reshape(2, 2, W, CA)

    second_a = second(first_a, s0xa, r1xa, s1xa, r2ya, sem2ya, s0ya, r1ya, s1ya, r2xa, sem2xa)
    second_b = second(first_b, s0xb, r1xb, s1xb, r2yb, sem2yb, s0yb, r1yb, s1yb, r2xb, sem2xb)
    summed(second_a, s1xa, r2ya, s1ya, r2xa, t_a, XA)
    summed(second_b, s1xb, r2yb, s1yb, r2xb, t_b, XB)

    part_b = jnp.concatenate([t_b[0:8, 0:PB], t_b[8:16, 0:PB]], 1)
    part_b = jnp.where(y_lo == 0, part_b[:, 0:1728], part_b[:, 64:1792])
    part_p = t_b[0:8, PB : PB + 128]
    for k in range(16):
        high = jnp.concatenate([t_a[:, 216 * k : 216 * k + 216], jnp.zeros((16, 40), F32)], 1)
        low = jnp.concatenate(
            [
                part_b[:, 108 * k : 108 * k + 108], jnp.zeros((8, 4), F32),
                part_p[:, 8 * k : 8 * k + 8], jnp.zeros((8, 8), F32),
            ], 1,
        )
        low = jnp.concatenate([low, jnp.zeros((8, 128), F32)], 0)
        msg[k] = jnp.concatenate([high, low], 1).astype(BF16)
    last = []
    for d in range(1, 16):
        cp = remote(msg.at[lax.rem(b + d, 16)], r3.at[d - 1], sem3, d - 1, z_peer(d))
        cp.start()
        last.append(cp)
    for cp in last:
        cp.wait()
    same = msg[b].astype(F32)
    for d in range(2, 16, 2):
        same = same + r3[d - 1].astype(F32)
    other = r3[0].astype(F32)
    for d in range(3, 16, 2):
        other = other + r3[d - 1].astype(F32)
    scale = 1.0 / (64 * 16 * W) ** 0.5
    total[core] = same * scale
    total[1 - core] = other * scale
    grad_a[...] = total[:, :, 0:256].reshape(32, 256).T[0:216]
    low = jnp.concatenate([total[0, 0:8, 256:384], total[1, 0:8, 256:384]], 0).T
    grad_b[...] = low[0:108]
    grad_p[...] = low[112:120]


def shards(video, kernel_a, project, kernel_b, cotangent):
    dma = pltpu.SemaphoreType.DMA
    vmem = pl.BlockSpec(memory_space=pltpu.VMEM)
    hbm = pl.BlockSpec(memory_space=pl.ANY)

    def group(lx, ly):
        return [
            pltpu.VMEM((4, 4, 16, lx), BF16), pltpu.VMEM((4, 4, 16, ly), BF16),
            pltpu.VMEM((3, 4, 16, lx), BF16), pltpu.VMEM((3, 4, 16, ly), BF16),
            pltpu.VMEM((4, 16, lx), BF16), pltpu.VMEM((4, 16, ly), BF16),
            pltpu.VMEM((3, 16, lx), BF16), pltpu.VMEM((3, 16, ly), BF16),
        ]

    return pl.pallas_call(
        kernel,
        out_shape=[
            jax.ShapeDtypeStruct((2, 2, W, CB), F32),
            jax.ShapeDtypeStruct((2, 2, W, CA), F32),
            jax.ShapeDtypeStruct((216, 32), F32),
            jax.ShapeDtypeStruct((108, 16), F32),
            jax.ShapeDtypeStruct((8, 16), F32),
        ],
        in_specs=[vmem, vmem, hbm, vmem, hbm],
        out_specs=[vmem] * 5,
        scratch_shapes=[
            pltpu.VMEM((27 * CA, CA), BF16), pltpu.VMEM((27 * CB, CB), BF16),
            pltpu.VMEM((4, 4, W, CA), BF16), pltpu.VMEM((4, 4, W, CB), BF16),
            pltpu.VMEM((4, 4, W, CB), BF16), pltpu.VMEM((4, 4, W, CA), BF16),
            pltpu.VMEM((2, 2, W, CB), BF16), pltpu.VMEM((2, 2, W, CA), BF16),
            pltpu.VMEM((4, 4, W, 3 * CA), BF16), pltpu.VMEM((4, 4, W, 3 * CB), BF16),
            pltpu.VMEM((4, 4, W, 3 * CB), BF16), pltpu.VMEM((4, 4, W, 3 * CA), BF16),
            pltpu.VMEM((2, 8, 16, CELLS), BF16), pltpu.VMEM((2, 64, CELLS), BF16),
            pltpu.VMEM((2, 64, CELLS), BF16),
            pltpu.VMEM((9, 8, 16, 768), BF16), pltpu.VMEM((9, 8, 16, 768), BF16),
            pltpu.VMEM((8, 2, 16, XB + YB), BF16), pltpu.VMEM((8, 2, 16, XB + YB), BF16),
            pltpu.VMEM((64, 27 * CB), F32),
            *group(XA, YA),
            *group(XB, YB),
            pltpu.VMEM((16, HALF_A), F32), pltpu.VMEM((16, XB + YB), F32),
            pltpu.VMEM((16, 16, 384), BF16), pltpu.VMEM((15, 16, 384), BF16),
            pltpu.VMEM((2, 16, 384), F32),
            dma((2,)), dma((2, 5)), dma((2, 5)), dma((2, 5)), dma((2, 5)), dma((2, 9)), dma((2, 1)),
            *[dma((2, 3)) for _ in range(8)],
            dma((2, 15)),
        ],
        compiler_params=pltpu.CompilerParams(
            collective_id=0, has_side_effects=True, vmem_limit_bytes=56 * 1024 * 1024
        ),
    )(video, cotangent, kernel_a, project, kernel_b)


def solution(mesh):
    cells = P("tm", "rows", None, None)
    return jax.shard_map(
        shards,
        mesh=mesh,
        in_specs=(cells, P(), P(), P(), cells),
        out_specs=(cells, cells, P("tm", "rows"), P("tm", "rows"), P("tm", "rows")),
        check_vma=False,
    )
```

time: 628 us -> 67.1 us (0.11)
  waiting for transfers between devices: 402 us -> 0 us
  blocking collectives: 70.2 us -> 0 us
  matrix products: 68.4 us -> 0 us
  Pallas kernels: 0 us -> 58.5 us
  starting transfers between devices: 39 us -> 0 us
  between operations: 16.5 us -> 0.64 us
  other arithmetic: 14 us -> 0 us
  local copies, waits for them, and re-layouts: 15.8 us -> 7.72 us
    unnamed x11 -> x0, waiting for transfers between devices: 372 us -> none
    unnamed x1 -> x0, blocking collectives: 70.2 us -> none
    dot_general x165 -> x0, matrix products: 68.4 us -> none  [the longest x54 38.4 us: weight_grad(): lax.dot_general(piece, flat, (((0,), (0,)), ((), ())), preferred_element_...]
    pallas_call x0 -> x1, Pallas kernels: none -> 58.5 us  [shards(): pl.pallas_call(kernel, out_shape=[jax.ShapeDtypeStruct((2, 2, W, CB), F32...]
    ppermute x12 -> x0, starting transfers between devices: 35.3 us -> none  [the longest x4 18.2 us: with_halo(): before = lax.ppermute(last, axis, up)]
    reduce_scatter x1 -> x0, waiting for transfers between devices: 30.6 us -> none  [shards(): lax.psum_scatter(grad_a, 'tm', scatter_dimension=0, tiled=True)]
    concatenate x11 -> x0, other arithmetic: 6.72 us -> none  [the longest x5 5.44 us: with_halo(): x = jnp.concatenate([before, x, after], axis=dim)]
    mul x2 -> x0, other arithmetic: 6.59 us -> none  [the longest x1 6.44 us: shards(): grad_a = weight_grad(video_p, grad_pre_4, frames, rows, width) * scale]
  transfers between devices with their start and end apart: 19 -> 0, of which waited for: 5 -> 0; matrix products, arithmetic and copies ran while one was open for 25% -> 0% of each run, Pallas kernels for 0% -> 0%
where the time goes in v2:
time: 67.1 us; the launch traced here: 66.9 us
  Pallas kernels  58.5 us (87%)
  local copies, waits for them, and re-layouts  7.72 us (12%)
    pallas_call x1, Pallas kernels, shards(): pl.pallas_call(kernel, out_shape=[jax.ShapeDtypeStruct((2, 2, W, CB), F32...  58.5 us
    unnamed x3, local copies, waits for them, and re-layouts  4.65 us
    pallas_call x2, local copies, waits for them, and re-layouts, shards(): pl.pallas_call(kernel, out_shape=[jax.ShapeDtypeStruct((2, 2, W, CB), F32...  3.07 us

profile of v2, /device:TPU:1, one launch (start us, length us, event | category | flops | bytes accessed | tf_op | source)
XLA Modules:
  0.0 66.9 jit_solution(6335294760856462615)
XLA Ops:
  0.6 58.5 %shard_map.92 = (f32[2,2,96,128]{3,2,1,0:T(8,128)}, f32[2,2,96,256]{3,2,1,0:T(8,128)}, f32[216,32]{1,0:T(8,128)}, f32[108,16]{1,0:T(8,128)}, f32[8,16]{1,0:T(8,128)}) custom-call(bf16[2,2,96,256]{3,2,1,0:T(8,128)(2,1)} %video.1, bf16[2,2,96,128]{3,2,1,0:T(8,128)(2,1)} %cot.1, bf16[6912,256]{1,0:T(8,128)(2,1)} %ka_hbm.1, bf16[256,128]{1,0:T(8,128)(2,1)} %project.1, ...), custom_call_target="tpu_custom_call" | custom-call | tf_op jit(solution)/shard_map/pallas_call | solution.py:341
  59.1 1.5 %copy.11 = f32[108,16]{0,1:T(8,128)} copy(f32[108,16]{1,0:T(8,128)} %get-tuple-element.8) | data formatting | bytes 13824 | tf_op jit(solution)/shard_map/pallas_call | solution.py:341
  60.6 1.6 %copy.10 = f32[216,32]{0,1:T(8,128)} copy(f32[216,32]{1,0:T(8,128)} %get-tuple-element.7) | data formatting | bytes 55296 | tf_op jit(solution)/shard_map/pallas_call | solution.py:341
  62.2 1.6 %copy.15 = f32[2,2,96,128]{3,2,1,0:T(8,128)} copy(f32[2,2,96,128]{3,2,1,0:T(8,128)} %get-tuple-element.15) | data formatting | bytes 393216
  63.8 1.8 %copy.16 = f32[2,2,96,256]{3,2,1,0:T(8,128)} copy(f32[2,2,96,256]{3,2,1,0:T(8,128)} %get-tuple-element.16) | data formatting | bytes 786432
  65.6 1.3 %copy.17 = f32[8,16]{1,0:T(8,128)} copy(f32[8,16]{1,0:T(8,128)} %get-tuple-element.19) | data formatting | bytes 1024

commit v3 on v2

v3 whole, which is shorter than its diff:
```python
import jax
import jax.numpy as jnp
from jax import lax
from jax.experimental import pallas as pl
from jax.experimental.pallas import tpu as pltpu
from jax.sharding import PartitionSpec as P

F32, BF16 = jnp.float32, jnp.bfloat16
MESH = pl.DeviceIdType.MESH
CA, CB, W = 256, 128, 96
CELLS = 4 * W
HALF_A = 27 * CA // 2
XA, YA = 1792, HALF_A - 1792
XB, YB = 512, 512
PB = 896
ORDER = (1, 2, 3, 0)


def dot(a, b, ca=1, cb=0):
    return lax.dot_general(a, b, (((ca,), (cb,)), ((), ())), preferred_element_type=F32)


def kernel(
    video_hbm, cot_hbm, ka_hbm, project_hbm, kb_hbm,
    out, grad_video, grad_a, grad_b, grad_p,
    video, cot, project, ka, kb, vbuf, cbuf, mbuf, gbuf, mown, gown, xs, us, ms, gs,
    gt, qt, send_a, recv_a, send_b, recv_b, part,
    s0xa, s0ya, r1xa, r1ya, s1xa, s1ya, r2ya, r2xa,
    s0xb, s0yb, r1xb, r1yb, s1xb, s1yb, r2yb, r2xb,
    t_a, t_b, msg, r3, total,
    sem_w, sem_v, sem_c, sem_m, sem_g, sem_a, sem_b,
    sem1xa, sem1ya, sem2ya, sem2xa, sem1xb, sem1yb, sem2yb, sem2xb, sem3,
):
    tm = lax.axis_index("tm")
    rows = lax.axis_index("rows")
    core = lax.rem(tm, 2)
    b = lax.rem(tm, 16)
    y_lo = tm // 16
    x = lax.rem(rows, 4)
    y = (rows // 4) * 2 + y_lo
    upper, lower = rows > 0, rows < 7

    def x_peer(d):
        return (tm, (rows // 4) * 4 + lax.rem(x + d, 4))

    def y_peer(d):
        to = lax.rem(y + d, 4)
        return (lax.rem(to, 2) * 16 + b, (to // 2) * 4 + x)

    def z_peer(d):
        return (y_lo * 16 + lax.rem(b + d, 16), rows)

    def near(dt, dr):
        return (lax.rem(tm + 32 + dt, 32), lax.rem(rows + 8 + dr, 8))

    partner = (tm + 1 - 2 * core, rows)

    def remote(src, dst, sem, slot, to):
        return pltpu.make_async_remote_copy(
            src_ref=src, dst_ref=dst, send_sem=sem.at[0, slot], recv_sem=sem.at[1, slot],
            device_id=to, device_id_type=MESH,
        )

    barrier = pltpu.get_barrier_semaphore()
    peers = [near(dt, dr) for dt, dr in ((0, 1), (0, -1), (1, 0), (-1, 0))]
    peers += [x_peer(d) for d in range(1, 4)] + [y_peer(d) for d in range(1, 4)]
    peers += [z_peer(d) for d in range(1, 16)]
    for to in peers:
        pl.semaphore_signal(barrier, inc=1, device_id=to, device_id_type=MESH)

    loads = [
        pltpu.make_async_copy(src, dst, sem_w.at[i])
        for i, (src, dst) in enumerate(
            ((cot_hbm, cot), (video_hbm, video), (kb_hbm, kb), (project_hbm, project), (ka_hbm, ka))
        )
    ]
    for cp in loads:
        cp.start()

    for buf, chan in ((vbuf, CA), (cbuf, CB), (mbuf, CB), (gbuf, CA)):

        @pl.when(rows == 0)
        def _():
            buf[:, 0] = jnp.zeros((4, W, chan), BF16)

        @pl.when(rows == 7)
        def _():
            buf[:, 3] = jnp.zeros((4, W, chan), BF16)

    class Halo:
        def __init__(self, src, buf, way, sem):
            own = 2 if way > 0 else 0
            mine, theirs = pl.ds(own, 2), pl.ds(2 - own, 2)
            beside = near(way, 0)
            self.full = remote(src, buf.at[theirs, pl.ds(1, 2)], sem, 0, beside)
            self.down = remote(src.at[:, 1], buf.at[mine, 0], sem, 1, near(0, 1))
            self.up = remote(src.at[:, 0], buf.at[mine, 3], sem, 2, near(0, -1))
            self.on_top = remote(buf.at[mine, 0], buf.at[theirs, 0], sem, 3, beside)
            self.on_low = remote(buf.at[mine, 3], buf.at[theirs, 3], sem, 4, beside)

        def rims(self):
            pl.when(lower)(self.down.start)
            pl.when(upper)(self.up.start)

        def forward(self):
            @pl.when(upper)
            def _():
                self.down.wait_recv()
                self.on_top.start()

            @pl.when(lower)
            def _():
                self.up.wait_recv()
                self.on_low.start()

        def corners(self):
            @pl.when(upper)
            def _():
                self.on_top.wait()
                self.up.wait_send()

            @pl.when(lower)
            def _():
                self.on_low.wait()
                self.down.wait_send()

    class Shifts:
        def __init__(self, src, buf, dst, way, chan):
            self.own = 2 if way > 0 else 0
            self.inside = (tm > 0) if way > 0 else (tm < 31)
            self.src, self.buf, self.dst, self.chan = src, buf, dst, chan

        def make(self, frames, rows_of):
            chan, dst = self.chan, self.dst
            cell = lax.broadcasted_iota(jnp.int32, (W, chan), 0)
            first = self.own if frames == "own" else 2 - self.own
            for f in (first, first + 1):
                for r in rows_of:
                    if frames == "own" and 1 <= r <= 2:
                        v = self.src[f - self.own, r - 1]
                    else:
                        v = self.buf[f, r]
                    v = v.astype(F32)
                    if frames != "own":
                        v = jnp.where(self.inside, v, 0.0)
                    dst[f, r, :, chan : 2 * chan] = v.astype(BF16)
                    left = jnp.where(cell == 0, 0.0, pltpu.roll(v, 1, 0))
                    right = jnp.where(cell == W - 1, 0.0, pltpu.roll(v, W - 1, 0))
                    dst[f, r, :, 0:chan] = left.astype(BF16)
                    dst[f, r, :, 2 * chan : 3 * chan] = right.astype(BF16)

    CENTRE, EDGE, PAST, CORNERS = (
        [(2, 1)], [(2, 0), (2, 2)], [(0, 1), (1, 1)], [(0, 0), (0, 2), (1, 0), (1, 2)],
    )

    def conv(acc, src, weight, chan, taps):
        for kt, kr in taps:
            at = (3 * kt + kr) * 3 * chan
            piece = src[kt : kt + 2, kr : kr + 2].reshape(CELLS, 3 * chan)
            term = dot(piece, weight[at : at + 3 * chan])
            acc = term if acc is None else acc + term
        return acc

    def back(acc, src, weight, chan, taps):
        for kt, kr in taps:
            for kc in range(3):
                at = (9 * kt + 3 * kr + kc) * chan
                piece = src[2 - kt : 4 - kt, 2 - kr : 4 - kr, :, (2 - kc) * chan : (3 - kc) * chan]
                term = dot(piece.reshape(CELLS, chan), weight[at : at + chan], 1, 1)
                acc = term if acc is None else acc + term
        return acc

    halo_c = Halo(cot, cbuf, -1, sem_c)
    halo_v = Halo(video, vbuf, 1, sem_v)
    shift_c = Shifts(cot, cbuf, us, -1, CB)
    shift_v = Shifts(video, vbuf, xs, 1, CA)

    loads[0].wait()
    loads[1].wait()
    shift_c.make("own", (1, 2))
    shift_v.make("own", (1, 2))
    loads[2].wait()
    loads[3].wait()
    back_b = back(None, us, kb, CB, CENTRE)
    loads[4].wait()
    pre = conv(None, xs, ka, CA, CENTRE)

    pl.semaphore_wait(barrier, len(peers))
    halo_c.rims()
    halo_v.rims()
    halo_c.full.start()
    halo_v.full.start()
    halo_c.forward()
    halo_v.forward()
    shift_c.make("own", (0, 3))
    shift_v.make("own", (0, 3))
    back_b = back(back_b, us, kb, CB, EDGE)
    pre = conv(pre, xs, ka, CA, EDGE)
    halo_c.full.wait()
    shift_c.make("other", (1, 2))
    back_b = back(back_b, us, kb, CB, PAST)
    halo_v.full.wait()
    shift_v.make("other", (1, 2))
    pre = conv(pre, xs, ka, CA, PAST)
    halo_c.corners()
    shift_c.make("other", (0, 3))
    back_b = back(back_b, us, kb, CB, CORNERS)
    grad_mid = cot[...].reshape(CELLS, CB).astype(F32) + back_b
    mid_t = grad_mid.T
    for c in range(2):
        pick = [mid_t[16 * j + 8 * c : 16 * j + 8 * c + 8] for j in range(8)]
        qt[c] = jnp.concatenate(pick, 0).astype(BF16)
    grad_h = dot(grad_mid.astype(BF16), project[...], 1, 1)

    halo_v.corners()
    shift_v.make("other", (0, 3))
    pre = conv(pre, xs, ka, CA, CORNERS)
    sig = jax.nn.sigmoid(pre)
    hidden = (pre * sig).astype(BF16)
    mid = dot(hidden, project[...])
    mown[...] = mid.astype(BF16).reshape(2, 2, W, CB)
    halo_m = Halo(mown, mbuf, 1, sem_m)
    halo_m.rims()
    halo_m.full.start()
    grad_pre = grad_h * sig * (1.0 + pre * (1.0 - sig))
    gown[...] = grad_pre.astype(BF16).reshape(2, 2, W, CA)
    halo_g = Halo(gown, gbuf, -1, sem_g)
    halo_g.rims()
    halo_g.full.start()
    out[...] = mid.reshape(2, 2, W, CB)
    grad_t = grad_pre.T
    for c in range(2):
        for j in range(8):
            gt[c, j] = grad_t[32 * j + 16 * c : 32 * j + 16 * c + 16].astype(BF16)

    def chunk_a(left, k):
        kt, kr = k // 3, k % 3
        return dot(left, xs[kt : kt + 2, kr : kr + 2].reshape(CELLS, 3 * CA))

    copies_a = []
    theirs = gt[1 - core].reshape(128, CELLS)
    for k in range(9):
        send_a[k] = chunk_a(theirs, k).astype(BF16).reshape(8, 16, 768)
        cp = remote(send_a.at[k], recv_a.at[k], sem_a, k, partner)
        cp.start()
        copies_a.append(cp)

    class Group:
        def __init__(self, s0x, r1x, s1x, r2y, sem1x, sem2y, s0y, r1y, s1y, r2x, sem1y, sem2x):
            self.s0x, self.r1x, self.s1x, self.r2y, self.sem1x, self.sem2y = s0x, r1x, s1x, r2y, sem1x, sem2y
            self.s0y, self.r1y, self.s1y, self.r2x, self.sem1y, self.sem2x = s0y, r1y, s1y, r2x, sem1y, sem2x

        def x1(self, d, yl):
            src = self.s0x.at[lax.rem(x + d, 4), yl]
            return remote(src, self.r1x.at[d - 1, yl], self.sem1x, 2 * (d - 1) + yl, x_peer(d))

        def y1(self, d):
            return remote(self.s0y.at[lax.rem(y + d, 4)], self.r1y.at[d - 1], self.sem1y, d - 1, y_peer(d))

        def y2(self, d):
            return remote(self.s1x.at[lax.rem(y + d, 4)], self.r2y.at[d - 1], self.sem2y, d - 1, y_peer(d))

        def x2(self, d):
            return remote(self.s1y.at[lax.rem(x + d, 4)], self.r2x.at[d - 1], self.sem2x, d - 1, x_peer(d))

        def send_x(self, yl):
            for d in (2, 1, 3):
                self.x1(d, yl).start()

        def send_y(self, yl):
            for yh in range(2):
                d = lax.rem(2 * yh + yl - y + 4, 4)

                @pl.when(d > 0)
                def _():
                    self.y1(d).start()

        def add_x(self, yl):
            for d in (1, 2, 3):
                self.x1(d, yl).wait()
            for yh in range(2):
                to = 2 * yh + yl
                acc = self.s0x[x, yl, yh].astype(F32)
                for s in range(3):
                    acc = acc + self.r1x[s, yl, yh].astype(F32)
                self.s1x[to] = acc.astype(BF16)
                d = lax.rem(to - y + 4, 4)

                @pl.when(d > 0)
                def _():
                    self.y2(d).start()

        def add_y(self):
            for d in (1, 2, 3):
                self.y1(d).wait()
            for d in ORDER:
                to = lax.rem(x + d, 4)
                acc = self.s0y[y, to].astype(F32)
                for s in range(3):
                    acc = acc + self.r1y[s, to].astype(F32)
                self.s1y[to] = acc.astype(BF16)
                if d:
                    self.x2(d).start()

        def finish(self, t_ref, lx):
            for d in (1, 2, 3):
                self.y2(d).wait()
            acc = self.s1x[y].astype(F32)
            for s in range(3):
                acc = acc + self.r2y[s].astype(F32)
            t_ref[:, :lx] = acc
            for d in (1, 2, 3):
                self.x2(d).wait()
            acc = self.s1y[x].astype(F32)
            for s in range(3):
                acc = acc + self.r2x[s].astype(F32)
            t_ref[:, lx:] = acc

    group_a = Group(s0xa, r1xa, s1xa, r2ya, sem1xa, sem2ya, s0ya, r1ya, s1ya, r2xa, sem1ya, sem2xa)
    group_b = Group(s0xb, r1xb, s1xb, r2yb, sem1xb, sem2yb, s0yb, r1yb, s1yb, r2xb, sem1yb, sem2xb)

    mine = gt[core].reshape(128, CELLS)
    cuts = sorted({768 * k for k in range(10)} | {0, XA, HALF_A, HALF_A + XA, 2 * HALF_A})
    for k in range(9):
        value = chunk_a(mine, k)
        copies_a[k].wait()
        value = (value + recv_a[k].reshape(128, 768).astype(F32)).astype(BF16)
        inside = [c for c in cuts if 768 * k <= c <= 768 * k + 768]
        for lo, hi in zip(inside[:-1], inside[1:]):
            yl, at = lo // HALF_A, lo % HALF_A
            for j in range(8):
                cut = value[16 * j : 16 * j + 16, lo - 768 * k : hi - 768 * k]
                if at < XA:
                    s0xa[j % 4, yl, j // 4, :, at : at + hi - lo] = cut
                else:
                    s0ya[(j // 4) * 2 + yl, j % 4, :, at - XA : at - XA + hi - lo] = cut
            if hi % HALF_A == XA:
                group_a.send_x(yl)
            if hi % HALF_A == 0:
                group_a.send_y(yl)

    mid_own = mid.T.astype(BF16)
    for k in range(9):
        kt, kr = k // 3, k % 3
        value = dot(mid_own, us[2 - kt : 4 - kt, 2 - kr : 4 - kr].reshape(CELLS, 3 * CB))
        for kc in range(3):
            tap = value[:, (2 - kc) * CB : (3 - kc) * CB].T
            at = (3 * k + kc) * CB
            for c in range(2):
                for j in range(8):
                    part[c, j, :, at : at + CB] = tap[16 * j + 8 * c : 16 * j + 8 * c + 8]

    def packed(half):
        proj = dot(qt[half], hidden)
        for j in range(8):
            for yl in range(2):
                at = 13 * CB * yl
                upper_half = part[half, j, :, at : at + PB]
                lower_half = part[half, j, :, at + PB : at + 2 * PB]
                body = jnp.concatenate([upper_half, lower_half], 0)
                tail = proj[8 * j : 8 * j + 8, 128 * yl : 128 * yl + 128]
                tail = jnp.concatenate([tail, jnp.zeros((8, 128), F32)], 0)
                yield j, yl, jnp.concatenate([body, tail], 1)

    for j, yl, value in packed(1 - core):
        send_b[j, yl] = value.astype(BF16)
    copy_b = remote(send_b, recv_b, sem_b, 0, partner)
    copy_b.start()
    halo_m.forward()
    halo_g.forward()
    copy_b.wait()
    for j, yl, value in packed(core):
        value = (value + recv_b[j, yl].astype(F32)).astype(BF16)
        s0xb[j % 4, yl, j // 4] = value[:, :XB]
        s0yb[(j // 4) * 2 + yl, j % 4] = value[:, XB:]
    for yl in range(2):
        group_b.send_x(yl)
        group_b.send_y(yl)

    every = CENTRE + EDGE + PAST + CORNERS
    shift_m = Shifts(mown, mbuf, ms, 1, CB)
    shift_m.make("own", (0, 1, 2, 3))
    halo_m.full.wait()
    halo_m.corners()
    shift_m.make("other", (0, 1, 2, 3))
    out[...] = out[...] + conv(None, ms, kb, CB, every).reshape(2, 2, W, CB)
    shift_g = Shifts(gown, gbuf, gs, -1, CA)
    shift_g.make("own", (0, 1, 2, 3))
    halo_g.full.wait()
    halo_g.corners()
    shift_g.make("other", (0, 1, 2, 3))
    grad_video[...] = back(None, gs, ka, CA, every).reshape(2, 2, W, CA)

    group_a.add_x(0)
    group_a.add_x(1)
    group_a.add_y()
    group_b.add_x(0)
    group_b.add_x(1)
    group_b.add_y()
    group_a.finish(t_a, XA)
    group_b.finish(t_b, XB)

    part_b = jnp.concatenate([t_b[0:8, 0:PB], t_b[8:16, 0:PB]], 1)
    part_b = jnp.where(y_lo == 0, part_b[:, 0:1728], part_b[:, 64:1792])
    part_p = t_b[0:8, PB : PB + 128]
    for k in range(16):
        high = jnp.concatenate([t_a[:, 216 * k : 216 * k + 216], jnp.zeros((16, 40), F32)], 1)
        low = jnp.concatenate(
            [
                part_b[:, 108 * k : 108 * k + 108], jnp.zeros((8, 4), F32),
                part_p[:, 8 * k : 8 * k + 8], jnp.zeros((8, 8), F32),
            ], 1,
        )
        low = jnp.concatenate([low, jnp.zeros((8, 128), F32)], 0)
        msg[k] = jnp.concatenate([high, low], 1).astype(BF16)
    last = []
    for d in range(1, 16):
        cp = remote(msg.at[lax.rem(b + d, 16)], r3.at[d - 1], sem3, d - 1, z_peer(d))
        cp.start()
        last.append(cp)
    for cp in last:
        cp.wait()
    same = msg[b].astype(F32)
    for d in range(2, 16, 2):
        same = same + r3[d - 1].astype(F32)
    other = r3[0].astype(F32)
    for d in range(3, 16, 2):
        other = other + r3[d - 1].astype(F32)
    scale = 1.0 / (64 * 16 * W) ** 0.5
    total[core] = same * scale
    total[1 - core] = other * scale
    grad_a[...] = total[:, :, 0:216].reshape(32, 216)
    low = jnp.concatenate([total[0, 0:8, 256:384], total[1, 0:8, 256:384]], 0)
    grad_b[...] = low[:, 0:108]
    grad_p[...] = low.T[112:120]


def written(*refs):
    for i in range(5):
        refs[5 + i][...] = refs[i][...]


def shards(video, kernel_a, project, kernel_b, cotangent):
    dma = pltpu.SemaphoreType.DMA
    vmem = pl.BlockSpec(memory_space=pltpu.VMEM)
    hbm = pl.BlockSpec(memory_space=pl.ANY)

    def group(lx, ly):
        return [
            pltpu.VMEM((4, 2, 2, 16, lx), BF16), pltpu.VMEM((4, 4, 16, ly), BF16),
            pltpu.VMEM((3, 2, 2, 16, lx), BF16), pltpu.VMEM((3, 4, 16, ly), BF16),
            pltpu.VMEM((4, 16, lx), BF16), pltpu.VMEM((4, 16, ly), BF16),
            pltpu.VMEM((3, 16, lx), BF16), pltpu.VMEM((3, 16, ly), BF16),
        ]

    results = pl.pallas_call(
        kernel,
        out_shape=[
            jax.ShapeDtypeStruct((2, 2, W, CB), F32),
            jax.ShapeDtypeStruct((2, 2, W, CA), F32),
            jax.ShapeDtypeStruct((32, 216), F32),
            jax.ShapeDtypeStruct((16, 108), F32),
            jax.ShapeDtypeStruct((8, 16), F32),
        ],
        in_specs=[hbm] * 5,
        out_specs=[vmem] * 5,
        scratch_shapes=[
            pltpu.VMEM((2, 2, W, CA), BF16), pltpu.VMEM((2, 2, W, CB), BF16), pltpu.VMEM((CA, CB), BF16),
            pltpu.VMEM((27 * CA, CA), BF16), pltpu.VMEM((27 * CB, CB), BF16),
            pltpu.VMEM((4, 4, W, CA), BF16), pltpu.VMEM((4, 4, W, CB), BF16),
            pltpu.VMEM((4, 4, W, CB), BF16), pltpu.VMEM((4, 4, W, CA), BF16),
            pltpu.VMEM((2, 2, W, CB), BF16), pltpu.VMEM((2, 2, W, CA), BF16),
            pltpu.VMEM((4, 4, W, 3 * CA), BF16), pltpu.VMEM((4, 4, W, 3 * CB), BF16),
            pltpu.VMEM((4, 4, W, 3 * CB), BF16), pltpu.VMEM((4, 4, W, 3 * CA), BF16),
            pltpu.VMEM((2, 8, 16, CELLS), BF16), pltpu.VMEM((2, 64, CELLS), BF16),
            pltpu.VMEM((9, 8, 16, 768), BF16), pltpu.VMEM((9, 8, 16, 768), BF16),
            pltpu.VMEM((8, 2, 16, XB + YB), BF16), pltpu.VMEM((8, 2, 16, XB + YB), BF16),
            pltpu.VMEM((2, 8, 8, 27 * CB), F32),
            *group(XA, YA),
            *group(XB, YB),
            pltpu.VMEM((16, HALF_A), F32), pltpu.VMEM((16, XB + YB), F32),
            pltpu.VMEM((16, 16, 384), BF16), pltpu.VMEM((15, 16, 384), BF16),
            pltpu.VMEM((2, 16, 384), F32),
            dma((5,)), dma((2, 5)), dma((2, 5)), dma((2, 5)), dma((2, 5)), dma((2, 9)), dma((2, 1)),
            *[dma((2, n)) for n in (6, 3, 3, 3) * 2],
            dma((2, 15)),
        ],
        compiler_params=pltpu.CompilerParams(
            collective_id=0, has_side_effects=True, vmem_limit_bytes=56 * 1024 * 1024
        ),
    )(video, cotangent, kernel_a, project, kernel_b)
    results = pl.pallas_call(
        written,
        out_shape=[jax.ShapeDtypeStruct(r.shape, F32) for r in results],
        in_specs=[vmem] * 5,
        out_specs=[vmem] * 5,
    )(*results)
    return results[0], results[1], results[2].T, results[3].T, results[4]


def solution(mesh):
    cells = P("tm", "rows", None, None)
    return jax.shard_map(
        shards,
        mesh=mesh,
        in_specs=(cells, P(), P(), P(), cells),
        out_specs=(cells, cells, P("tm", "rows"), P("tm", "rows"), P("tm", "rows")),
        check_vma=False,
    )
```

time: 67.1 us -> 56.7 us (0.85)
  local copies, waits for them, and re-layouts: 7.72 us -> 0 us
  Pallas kernels: 58.5 us -> 55.9 us
    unnamed x3 -> x0, local copies, waits for them, and re-layouts: 4.65 us -> none
    pallas_call x1, Pallas kernels: 58.5 us -> 54 us  [shards(): pl.pallas_call(kernel, out_shape=[jax.ShapeDtypeStruct((2, 2, W, CB), F32...]
    pallas_call x2 -> x0, local copies, waits for them, and re-layouts: 3.07 us -> none  [shards(): pl.pallas_call(kernel, out_shape=[jax.ShapeDtypeStruct((2, 2, W, CB), F32...]
    pallas_call x0 -> x1, Pallas kernels: none -> 1.91 us  [shards(): pl.pallas_call(written, out_shape=[jax.ShapeDtypeStruct(r.shape, F32) for...]
where the time goes in v3:
time: 56.7 us; the launch traced here: 56.5 us
  Pallas kernels  55.9 us (99%)
  between operations  0.64 us (1%)
    pallas_call x1, Pallas kernels, shards(): pl.pallas_call(kernel, out_shape=[jax.ShapeDtypeStruct((2, 2, W, CB), F32...  54 us
    pallas_call x1, Pallas kernels, shards(): pl.pallas_call(written, out_shape=[jax.ShapeDtypeStruct(r.shape, F32) for...  1.91 us

profile of v3, /device:TPU:1, one launch (start us, length us, event | category | flops | bytes accessed | tf_op | source)
XLA Modules:
  0.0 56.5 jit_solution(11738453899087800616)
XLA Ops:
  0.6 54.0 %shard_map.92 = (f32[2,2,96,128]{3,2,1,0:T(8,128)}, f32[2,2,96,256]{3,2,1,0:T(8,128)}, f32[32,216]{1,0:T(8,128)}, f32[16,108]{1,0:T(8,128)}, f32[8,16]{1,0:T(8,128)}) custom-call(bf16[2,2,96,256]{3,2,1,0:T(8,128)(2,1)} %video_hbm.1, bf16[2,2,96,128]{3,2,1,0:T(8,128)(2,1)} %cot_hbm.1, bf16[6912,256]{1,0:T(8,128)(2,1)} %ka_hbm.1, ...), custom_call_target="tpu_custom_call" | custom-call | tf_op jit(solution)/shard_map/pallas_call | solution.py:456
  54.6 1.9 %shard_map.93 = (f32[2,2,96,128]{3,2,1,0:T(8,128)}, f32[2,2,96,256]{3,2,1,0:T(8,128)}, f32[32,216]{1,0:T(8,128)}, f32[16,108]{1,0:T(8,128)}, f32[8,16]{1,0:T(8,128)}) custom-call(f32[2,2,96,128]{3,2,1,0:T(8,128)} %get-tuple-element.15.refs_0_, f32[2,2,96,256]{3,2,1,0:T(8,128)} %get-tuple-element.16.refs_1_, f32[32,216]{1,0:T(8,128)} %get-tuple-element.17.refs_2_, ...), custom_call_target="tpu_custom_call" | custom-call | tf_op jit(solution)/shard_map/pallas_call | solution.py:492

commit v4 on v3

--- a/solution.py
+++ b/solution.py
@@ -11,8 +11,6 @@
 CELLS = 4 * W
 HALF_A = 27 * CA // 2
 XA, YA = 1792, HALF_A - 1792
-XB, YB = 512, 512
-PB = 896
 ORDER = (1, 2, 3, 0)
 
 
@@ -22,14 +20,14 @@
 
 def kernel(
     video_hbm, cot_hbm, ka_hbm, project_hbm, kb_hbm,
-    out, grad_video, grad_a, grad_b, grad_p,
-    video, cot, project, ka, kb, vbuf, cbuf, mbuf, gbuf, mown, gown, xs, us, ms, gs,
+    out_hbm, grad_video_hbm, grad_a, grad_b, grad_p,
+    out, grad_video, video, cot, project, ka, kb, vbuf, cbuf, mbuf, gbuf, mown, gown, xs, us, ms, gs,
     gt, qt, send_a, recv_a, send_b, recv_b, part,
     s0xa, s0ya, r1xa, r1ya, s1xa, s1ya, r2ya, r2xa,
-    s0xb, s0yb, r1xb, r1yb, s1xb, s1yb, r2yb, r2xb,
-    t_a, t_b, msg, r3, total,
+    s0b, r1b, s1b, r2b, tb, gb,
+    t_a, msg, r3, total,
     sem_w, sem_v, sem_c, sem_m, sem_g, sem_a, sem_b,
-    sem1xa, sem1ya, sem2ya, sem2xa, sem1xb, sem1yb, sem2yb, sem2xb, sem3,
+    sem1xa, sem1ya, sem2ya, sem2xa, sem3, sem1b, sem2b, sem3b, sem_o,
 ):
     tm = lax.axis_index("tm")
     rows = lax.axis_index("rows")
@@ -39,6 +37,7 @@
     x = lax.rem(rows, 4)
     y = (rows // 4) * 2 + y_lo
     upper, lower = rows > 0, rows < 7
+    since, until = tm > 0, tm < 31
 
     def x_peer(d):
         return (tm, (rows // 4) * 4 + lax.rem(x + d, 4))
@@ -49,6 +48,13 @@
 
     def z_peer(d):
         return (y_lo * 16 + lax.rem(b + d, 16), rows)
+
+    def same_core(d):
+        return (y_lo * 16 + lax.rem(b + 2 * d, 16), rows)
+
+    def plane(dx, dy):
+        to = lax.rem(y + dy, 4)
+        return (lax.rem(to, 2) * 16 + b, (to // 2) * 4 + lax.rem(x + dx, 4))
 
     def near(dt, dr):
         return (lax.rem(tm + 32 + dt, 32), lax.rem(rows + 8 + dr, 8))
@@ -62,8 +68,8 @@
         )
 
     barrier = pltpu.get_barrier_semaphore()
-    peers = [near(dt, dr) for dt, dr in ((0, 1), (0, -1), (1, 0), (-1, 0))]
-    peers += [x_peer(d) for d in range(1, 4)] + [y_peer(d) for d in range(1, 4)]
+    peers = [near(dt, dr) for dt in (-1, 0, 1) for dr in (-1, 0, 1) if dt or dr]
+    peers += [plane(dx, dy) for dx in range(4) for dy in range(4) if dx or dy]
     peers += [z_peer(d) for d in range(1, 16)]
     for to in peers:
         pl.semaphore_signal(barrier, inc=1, device_id=to, device_id_type=MESH)
@@ -87,47 +93,65 @@
         def _():
             buf[:, 3] = jnp.zeros((4, W, chan), BF16)
 
+    @pl.when(tm == 0)
+    def _():
+        vbuf[0:2] = jnp.zeros((2, 4, W, CA), BF16)
+        mbuf[0:2] = jnp.zeros((2, 4, W, CB), BF16)
+
+    @pl.when(tm == 31)
+    def _():
+        cbuf[2:4] = jnp.zeros((2, 4, W, CB), BF16)
+        gbuf[2:4] = jnp.zeros((2, 4, W, CA), BF16)
+
     class Halo:
-        def __init__(self, src, buf, way, sem):
+        def __init__(self, src, buf, way, sem, direct):
             own = 2 if way > 0 else 0
             mine, theirs = pl.ds(own, 2), pl.ds(2 - own, 2)
-            beside = near(way, 0)
-            self.full = remote(src, buf.at[theirs, pl.ds(1, 2)], sem, 0, beside)
+            self.gives, self.takes = (until, since) if way > 0 else (since, until)
+            self.full = remote(src, buf.at[theirs, pl.ds(1, 2)], sem, 0, near(way, 0))
             self.down = remote(src.at[:, 1], buf.at[mine, 0], sem, 1, near(0, 1))
             self.up = remote(src.at[:, 0], buf.at[mine, 3], sem, 2, near(0, -1))
-            self.on_top = remote(buf.at[mine, 0], buf.at[theirs, 0], sem, 3, beside)
-            self.on_low = remote(buf.at[mine, 3], buf.at[theirs, 3], sem, 4, beside)
+            if direct:
+                self.top = remote(src.at[:, 1], buf.at[theirs, 0], sem, 3, near(way, 1))
+                self.low = remote(src.at[:, 0], buf.at[theirs, 3], sem, 4, near(way, -1))
+                self.gives_top, self.gives_low = self.gives & lower, self.gives & upper
+            else:
+                self.top = remote(buf.at[mine, 0], buf.at[theirs, 0], sem, 3, near(way, 0))
+                self.low = remote(buf.at[mine, 3], buf.at[theirs, 3], sem, 4, near(way, 0))
+                self.gives_top, self.gives_low = self.gives & upper, self.gives & lower
 
         def rims(self):
             pl.when(lower)(self.down.start)
             pl.when(upper)(self.up.start)
 
-        def forward(self):
-            @pl.when(upper)
-            def _():
-                self.down.wait_recv()
-                self.on_top.start()
-
-            @pl.when(lower)
-            def _():
-                self.up.wait_recv()
-                self.on_low.start()
+        def ahead(self):
+            pl.when(self.gives)(self.full.start)
 
         def corners(self):
-            @pl.when(upper)
-            def _():
-                self.on_top.wait()
-                self.up.wait_send()
-
-            @pl.when(lower)
-            def _():
-                self.on_low.wait()
-                self.down.wait_send()
+            pl.when(self.gives_top)(self.top.start)
+            pl.when(self.gives_low)(self.low.start)
+
+        def wait_rims(self):
+            pl.when(upper)(self.down.wait_recv)
+            pl.when(lower)(self.up.wait_recv)
+
+        def wait_ahead(self):
+            pl.when(self.takes)(self.full.wait_recv)
+
+        def wait_corners(self):
+            pl.when(self.takes & upper)(self.top.wait_recv)
+            pl.when(self.takes & lower)(self.low.wait_recv)
+
+        def sent(self):
+            pl.when(lower)(self.down.wait_send)
+            pl.when(upper)(self.up.wait_send)
+            pl.when(self.gives)(self.full.wait_send)
+            pl.when(self.gives_top)(self.top.wait_send)
+            pl.when(self.gives_low)(self.low.wait_send)
 
     class Shifts:
         def __init__(self, src, buf, dst, way, chan):
             self.own = 2 if way > 0 else 0
-            self.inside = (tm > 0) if way > 0 else (tm < 31)
             self.src, self.buf, self.dst, self.chan = src, buf, dst, chan
 
         def make(self, frames, rows_of):
@@ -141,8 +165,6 @@
                     else:
                         v = self.buf[f, r]
                     v = v.astype(F32)
-                    if frames != "own":
-                        v = jnp.where(self.inside, v, 0.0)
                     dst[f, r, :, chan : 2 * chan] = v.astype(BF16)
                     left = jnp.where(cell == 0, 0.0, pltpu.roll(v, 1, 0))
                     right = jnp.where(cell == W - 1, 0.0, pltpu.roll(v, W - 1, 0))
@@ -170,8 +192,8 @@
                 acc = term if acc is None else acc + term
         return acc
 
-    halo_c = Halo(cot, cbuf, -1, sem_c)
-    halo_v = Halo(video, vbuf, 1, sem_v)
+    halo_c = Halo(cot, cbuf, -1, sem_c, True)
+    halo_v = Halo(video, vbuf, 1, sem_v, True)
     shift_c = Shifts(cot, cbuf, us, -1, CB)
     shift_v = Shifts(video, vbuf, xs, 1, CA)
 
@@ -188,21 +210,23 @@
     pl.semaphore_wait(barrier, len(peers))
     halo_c.rims()
     halo_v.rims()
-    halo_c.full.start()
-    halo_v.full.start()
-    halo_c.forward()
-    halo_v.forward()
+    halo_c.corners()
+    halo_v.corners()
+    halo_c.ahead()
+    halo_v.ahead()
+    halo_c.wait_rims()
     shift_c.make("own", (0, 3))
+    back_b = back(back_b, us, kb, CB, EDGE)
+    halo_v.wait_rims()
     shift_v.make("own", (0, 3))
-    back_b = back(back_b, us, kb, CB, EDGE)
     pre = conv(pre, xs, ka, CA, EDGE)
-    halo_c.full.wait()
+    halo_c.wait_ahead()
     shift_c.make("other", (1, 2))
     back_b = back(back_b, us, kb, CB, PAST)
-    halo_v.full.wait()
+    halo_v.wait_ahead()
     shift_v.make("other", (1, 2))
     pre = conv(pre, xs, ka, CA, PAST)
-    halo_c.corners()
+    halo_c.wait_corners()
     shift_c.make("other", (0, 3))
     back_b = back(back_b, us, kb, CB, CORNERS)
     grad_mid = cot[...].reshape(CELLS, CB).astype(F32) + back_b
@@ -212,21 +236,21 @@
         qt[c] = jnp.concatenate(pick, 0).astype(BF16)
     grad_h = dot(grad_mid.astype(BF16), project[...], 1, 1)
 
-    halo_v.corners()
+    halo_v.wait_corners()
     shift_v.make("other", (0, 3))
     pre = conv(pre, xs, ka, CA, CORNERS)
     sig = jax.nn.sigmoid(pre)
     hidden = (pre * sig).astype(BF16)
     mid = dot(hidden, project[...])
     mown[...] = mid.astype(BF16).reshape(2, 2, W, CB)
-    halo_m = Halo(mown, mbuf, 1, sem_m)
+    halo_m = Halo(mown, mbuf, 1, sem_m, False)
     halo_m.rims()
-    halo_m.full.start()
+    halo_m.ahead()
     grad_pre = grad_h * sig * (1.0 + pre * (1.0 - sig))
     gown[...] = grad_pre.astype(BF16).reshape(2, 2, W, CA)
-    halo_g = Halo(gown, gbuf, -1, sem_g)
+    halo_g = Halo(gown, gbuf, -1, sem_g, False)
     halo_g.rims()
-    halo_g.full.start()
+    halo_g.ahead()
     out[...] = mid.reshape(2, 2, W, CB)
     grad_t = grad_pre.T
     for c in range(2):
@@ -317,7 +341,6 @@
             t_ref[:, lx:] = acc
 
     group_a = Group(s0xa, r1xa, s1xa, r2ya, sem1xa, sem2ya, s0ya, r1ya, s1ya, r2xa, sem1ya, sem2xa)
-    group_b = Group(s0xb, r1xb, s1xb, r2yb, sem1xb, sem2yb, s0yb, r1yb, s1yb, r2xb, sem1yb, sem2xb)
 
     mine = gt[core].reshape(128, CELLS)
     cuts = sorted({768 * k for k in range(10)} | {0, XA, HALF_A, HALF_A + XA, 2 * HALF_A})
@@ -354,70 +377,88 @@
         proj = dot(qt[half], hidden)
         for j in range(8):
             for yl in range(2):
-                at = 13 * CB * yl
-                upper_half = part[half, j, :, at : at + PB]
-                lower_half = part[half, j, :, at + PB : at + 2 * PB]
-                body = jnp.concatenate([upper_half, lower_half], 0)
-                tail = proj[8 * j : 8 * j + 8, 128 * yl : 128 * yl + 128]
-                tail = jnp.concatenate([tail, jnp.zeros((8, 128), F32)], 0)
-                yield j, yl, jnp.concatenate([body, tail], 1)
-
-    for j, yl, value in packed(1 - core):
-        send_b[j, yl] = value.astype(BF16)
+                for z in range(8):
+                    both = []
+                    for c in range(2):
+                        at, to = 1728 * yl + 216 * z + 108 * c, 128 * yl + 16 * z + 8 * c
+                        tail = proj[8 * j : 8 * j + 8, to : to + 8]
+                        both.append(jnp.concatenate([part[half, j, :, at : at + 108], tail, jnp.zeros((8, 12), F32)], 1))
+                    yield z, j, yl, jnp.concatenate(both, 0)
+
+    for z, j, yl, value in packed(1 - core):
+        send_b[z, j, yl] = value.astype(BF16)
     copy_b = remote(send_b, recv_b, sem_b, 0, partner)
     copy_b.start()
-    halo_m.forward()
-    halo_g.forward()
+    halo_m.wait_rims()
+    halo_m.corners()
+    halo_g.wait_rims()
+    halo_g.corners()
     copy_b.wait()
-    for j, yl, value in packed(core):
-        value = (value + recv_b[j, yl].astype(F32)).astype(BF16)
-        s0xb[j % 4, yl, j // 4] = value[:, :XB]
-        s0yb[(j // 4) * 2 + yl, j % 4] = value[:, XB:]
-    for yl in range(2):
-        group_b.send_x(yl)
-        group_b.send_y(yl)
+    for z, j, yl, value in packed(core):
+        s0b[z, j, yl] = (value + recv_b[z, j, yl].astype(F32)).astype(BF16)
+    me_z = b // 2
+    first_b = [
+        remote(s0b.at[lax.rem(me_z + d, 8)], r1b.at[d - 1], sem1b, d - 1, same_core(d)) for d in range(1, 8)
+    ]
+    for d in (4, 3, 5, 2, 6, 1, 7):
+        first_b[d - 1].start()
 
     every = CENTRE + EDGE + PAST + CORNERS
     shift_m = Shifts(mown, mbuf, ms, 1, CB)
     shift_m.make("own", (0, 1, 2, 3))
-    halo_m.full.wait()
-    halo_m.corners()
+    halo_m.wait_ahead()
+    halo_m.wait_corners()
     shift_m.make("other", (0, 1, 2, 3))
     out[...] = out[...] + conv(None, ms, kb, CB, every).reshape(2, 2, W, CB)
+    done = [pltpu.make_async_copy(out, out_hbm, sem_o.at[0]), pltpu.make_async_copy(grad_video, grad_video_hbm, sem_o.at[1])]
+    done[0].start()
     shift_g = Shifts(gown, gbuf, gs, -1, CA)
     shift_g.make("own", (0, 1, 2, 3))
-    halo_g.full.wait()
-    halo_g.corners()
+    halo_g.wait_ahead()
+    halo_g.wait_corners()
     shift_g.make("other", (0, 1, 2, 3))
     grad_video[...] = back(None, gs, ka, CA, every).reshape(2, 2, W, CA)
+
+    done[1].start()
 
     group_a.add_x(0)
     group_a.add_x(1)
     group_a.add_y()
-    group_b.add_x(0)
-    group_b.add_x(1)
-    group_b.add_y()
+    for cp in first_b:
+        cp.wait()
+    for j in range(8):
+        acc = s0b[me_z, j].astype(F32)
+        for s in range(7):
+            acc = acc + r1b[s, j].astype(F32)
+        s1b[j // 4, j % 4] = acc.astype(BF16)
+    second_b = []
+    for dx in range(4):
+        for dy in range(4):
+            if dx or dy:
+                to = lax.rem(y + dy, 4)
+                src = s1b.at[to // 2, lax.rem(x + dx, 4), lax.rem(to, 2)]
+                slot = 4 * dx + dy - 1
+                cp = remote(src, r2b.at[slot], sem2b, slot, plane(dx, dy))
+                cp.start()
+                second_b.append(cp)
     group_a.finish(t_a, XA)
-    group_b.finish(t_b, XB)
-
-    part_b = jnp.concatenate([t_b[0:8, 0:PB], t_b[8:16, 0:PB]], 1)
-    part_b = jnp.where(y_lo == 0, part_b[:, 0:1728], part_b[:, 64:1792])
-    part_p = t_b[0:8, PB : PB + 128]
     for k in range(16):
         high = jnp.concatenate([t_a[:, 216 * k : 216 * k + 216], jnp.zeros((16, 40), F32)], 1)
-        low = jnp.concatenate(
-            [
-                part_b[:, 108 * k : 108 * k + 108], jnp.zeros((8, 4), F32),
-                part_p[:, 8 * k : 8 * k + 8], jnp.zeros((8, 8), F32),
-            ], 1,
-        )
-        low = jnp.concatenate([low, jnp.zeros((8, 128), F32)], 0)
-        msg[k] = jnp.concatenate([high, low], 1).astype(BF16)
+        msg[k] = high.astype(BF16)
     last = []
     for d in range(1, 16):
         cp = remote(msg.at[lax.rem(b + d, 16)], r3.at[d - 1], sem3, d - 1, z_peer(d))
         cp.start()
         last.append(cp)
+    for cp in second_b:
+        cp.wait()
+    acc = s1b[y // 2, x, lax.rem(y, 2)].astype(F32)
+    for s in range(15):
+        acc = acc + r2b[s].astype(F32)
+    scale = 1.0 / (64 * 16 * W) ** 0.5
+    tb[...] = (acc * scale).reshape(2, 8, 128)
+    swap = remote(tb.at[1 - core], gb.at[core], sem3b, 0, partner)
+    swap.start()
     for cp in last:
         cp.wait()
     same = msg[b].astype(F32)
@@ -426,18 +467,31 @@
     other = r3[0].astype(F32)
     for d in range(3, 16, 2):
         other = other + r3[d - 1].astype(F32)
-    scale = 1.0 / (64 * 16 * W) ** 0.5
     total[core] = same * scale
     total[1 - core] = other * scale
     grad_a[...] = total[:, :, 0:216].reshape(32, 216)
-    low = jnp.concatenate([total[0, 0:8, 256:384], total[1, 0:8, 256:384]], 0)
+    swap.wait()
+    gb[core] = tb[core]
+    low = gb[...].reshape(16, 128)
     grad_b[...] = low[:, 0:108]
-    grad_p[...] = low.T[112:120]
+    grad_p[...] = low.T[108:116]
+    for halo in (halo_c, halo_v, halo_m, halo_g):
+        halo.sent()
+    for cp in done:
+        cp.wait()
 
 
 def written(*refs):
+    took, gives, held, sem = refs[:5], refs[5:10], refs[10:15], refs[15]
+    reads = [pltpu.make_async_copy(took[i], held[i], sem.at[0, i]) for i in range(5)]
+    writes = [pltpu.make_async_copy(held[i], gives[i], sem.at[1, i]) for i in range(5)]
+    for cp in reads:
+        cp.start()
     for i in range(5):
-        refs[5 + i][...] = refs[i][...]
+        reads[i].wait()
+        writes[i].start()
+    for cp in writes:
+        cp.wait()
 
 
 def shards(video, kernel_a, project, kernel_b, cotangent):
@@ -463,8 +517,9 @@
             jax.ShapeDtypeStruct((8, 16), F32),
         ],
         in_specs=[hbm] * 5,
-        out_specs=[vmem] * 5,
+        out_specs=[hbm, hbm, vmem, vmem, vmem],
         scratch_shapes=[
+            pltpu.VMEM((2, 2, W, CB), F32), pltpu.VMEM((2, 2, W, CA), F32),
             pltpu.VMEM((2, 2, W, CA), BF16), pltpu.VMEM((2, 2, W, CB), BF16), pltpu.VMEM((CA, CB), BF16),
             pltpu.VMEM((27 * CA, CA), BF16), pltpu.VMEM((27 * CB, CB), BF16),
             pltpu.VMEM((4, 4, W, CA), BF16), pltpu.VMEM((4, 4, W, CB), BF16),
@@ -474,16 +529,18 @@
             pltpu.VMEM((4, 4, W, 3 * CB), BF16), pltpu.VMEM((4, 4, W, 3 * CA), BF16),
             pltpu.VMEM((2, 8, 16, CELLS), BF16), pltpu.VMEM((2, 64, CELLS), BF16),
             pltpu.VMEM((9, 8, 16, 768), BF16), pltpu.VMEM((9, 8, 16, 768), BF16),
-            pltpu.VMEM((8, 2, 16, XB + YB), BF16), pltpu.VMEM((8, 2, 16, XB + YB), BF16),
+            pltpu.VMEM((8, 8, 2, 16, 128), BF16), pltpu.VMEM((8, 8, 2, 16, 128), BF16),
             pltpu.VMEM((2, 8, 8, 27 * CB), F32),
             *group(XA, YA),
-            *group(XB, YB),
-            pltpu.VMEM((16, HALF_A), F32), pltpu.VMEM((16, XB + YB), F32),
-            pltpu.VMEM((16, 16, 384), BF16), pltpu.VMEM((15, 16, 384), BF16),
-            pltpu.VMEM((2, 16, 384), F32),
+            pltpu.VMEM((8, 8, 2, 16, 128), BF16), pltpu.VMEM((7, 8, 2, 16, 128), BF16),
+            pltpu.VMEM((2, 4, 2, 16, 128), BF16), pltpu.VMEM((15, 16, 128), BF16),
+            pltpu.VMEM((2, 8, 128), F32), pltpu.VMEM((2, 8, 128), F32),
+            pltpu.VMEM((16, HALF_A), F32),
+            pltpu.VMEM((16, 16, 256), BF16), pltpu.VMEM((15, 16, 256), BF16),
+            pltpu.VMEM((2, 16, 256), F32),
             dma((5,)), dma((2, 5)), dma((2, 5)), dma((2, 5)), dma((2, 5)), dma((2, 9)), dma((2, 1)),
-            *[dma((2, n)) for n in (6, 3, 3, 3) * 2],
-            dma((2, 15)),
+            *[dma((2, n)) for n in (6, 3, 3, 3, 15, 7, 15, 1)],
+            dma((2,)),
         ],
         compiler_params=pltpu.CompilerParams(
             collective_id=0, has_side_effects=True, vmem_limit_bytes=56 * 1024 * 1024
@@ -492,8 +549,9 @@
     results = pl.pallas_call(
         written,
         out_shape=[jax.ShapeDtypeStruct(r.shape, F32) for r in results],
-        in_specs=[vmem] * 5,
-        out_specs=[vmem] * 5,
+        in_specs=[hbm] * 5,
+        out_specs=[hbm] * 5,
+        scratch_shapes=[*[pltpu.VMEM(r.shape, F32) for r in results], dma((2, 5))],
     )(*results)
     return results[0], results[1], results[2].T, results[3].T, results[4]
 

time: 56.7 us -> 61.8 us (1.090)
  Pallas kernels: 55.9 us -> 61 us
    pallas_call x1, Pallas kernels: 54 us -> 59.1 us  [shards(): pl.pallas_call(kernel, out_shape=[jax.ShapeDtypeStruct((2, 2, W, CB), F32...]
where the time goes in v4:
time: 61.8 us; the launch traced here: 61.7 us
  Pallas kernels  61 us (99%)
  between operations  0.64 us (1%)
    pallas_call x1, Pallas kernels, shards(): pl.pallas_call(kernel, out_shape=[jax.ShapeDtypeStruct((2, 2, W, CB), F32...  59.1 us
    pallas_call x1, Pallas kernels, shards(): pl.pallas_call(written, out_shape=[jax.ShapeDtypeStruct(r.shape, F32) for...  1.94 us

profile of v4, /device:TPU:1, one launch (start us, length us, event | category | flops | bytes accessed | tf_op | source)
XLA Modules:
  0.0 61.7 jit_solution(11656003511557494750)
XLA Ops:
  0.6 59.1 %shard_map.92 = (f32[2,2,96,128]{3,2,1,0:T(8,128)}, f32[2,2,96,256]{3,2,1,0:T(8,128)}, f32[32,216]{1,0:T(8,128)}, f32[16,108]{1,0:T(8,128)}, f32[8,16]{1,0:T(8,128)}) custom-call(bf16[2,2,96,256]{3,2,1,0:T(8,128)(2,1)} %video_hbm.1, bf16[2,2,96,128]{3,2,1,0:T(8,128)(2,1)} %cot_hbm.1, bf16[6912,256]{1,0:T(8,128)(2,1)} %ka_hbm.1, ...), custom_call_target="tpu_custom_call" | custom-call | tf_op jit(solution)/shard_map/pallas_call | solution.py:510
  59.7 1.9 %shard_map.93 = (f32[2,2,96,128]{3,2,1,0:T(8,128)}, f32[2,2,96,256]{3,2,1,0:T(8,128)}, f32[32,216]{1,0:T(8,128)}, f32[16,108]{1,0:T(8,128)}, f32[8,16]{1,0:T(8,128)}) custom-call(f32[2,2,96,128]{3,2,1,0:T(8,128)} %get-tuple-element.15.refs_0_, f32[2,2,96,256]{3,2,1,0:T(8,128)} %get-tuple-element.16.refs_1_, f32[32,216]{1,0:T(8,128)} %get-tuple-element.17.refs_2_, ...), custom_call_target="tpu_custom_call" | custom-call | tf_op jit(solution)/shard_map/pallas_call | solution.py:549

commit v5 on v3

--- a/solution.py
+++ b/solution.py
@@ -10,9 +10,10 @@
 CA, CB, W = 256, 128, 96
 CELLS = 4 * W
 HALF_A = 27 * CA // 2
-XA, YA = 1792, HALF_A - 1792
+XA, YA = 1664, HALF_A - 1664
 XB, YB = 512, 512
 PB = 896
+LAG = 3
 ORDER = (1, 2, 3, 0)
 
 
@@ -22,14 +23,14 @@
 
 def kernel(
     video_hbm, cot_hbm, ka_hbm, project_hbm, kb_hbm,
-    out, grad_video, grad_a, grad_b, grad_p,
-    video, cot, project, ka, kb, vbuf, cbuf, mbuf, gbuf, mown, gown, xs, us, ms, gs,
-    gt, qt, send_a, recv_a, send_b, recv_b, part,
-    s0xa, s0ya, r1xa, r1ya, s1xa, s1ya, r2ya, r2xa,
-    s0xb, s0yb, r1xb, r1yb, s1xb, s1yb, r2yb, r2xb,
+    out_hbm, grad_video_hbm, grad_a, grad_b, grad_p,
+    out, grad_video, video, cot, project, ka, kb, vbuf, cbuf, mbuf, gbuf, mown, gown, xs, us, ms, gs,
+    gt, qt, send_a, recv_a, own_a, send_b, recv_b, part,
+    s0xa, s0ya, q1xa, q1ya, r1xa, r1ya, s1xa, s1ya, r2ya, r2xa,
+    s0xb, s0yb, q1xb, q1yb, r1xb, r1yb, s1xb, s1yb, r2yb, r2xb,
     t_a, t_b, msg, r3, total,
     sem_w, sem_v, sem_c, sem_m, sem_g, sem_a, sem_b,
-    sem1xa, sem1ya, sem2ya, sem2xa, sem1xb, sem1yb, sem2yb, sem2xb, sem3,
+    sem1xa, sem1ya, sem2ya, sem2xa, sem1xb, sem1yb, sem2yb, sem2xb, sem3, sem_o,
 ):
     tm = lax.axis_index("tm")
     rows = lax.axis_index("rows")
@@ -39,6 +40,7 @@
     x = lax.rem(rows, 4)
     y = (rows // 4) * 2 + y_lo
     upper, lower = rows > 0, rows < 7
+    since, until = tm > 0, tm < 31
 
     def x_peer(d):
         return (tm, (rows // 4) * 4 + lax.rem(x + d, 4))
@@ -87,47 +89,60 @@
         def _():
             buf[:, 3] = jnp.zeros((4, W, chan), BF16)
 
+    @pl.when(tm == 0)
+    def _():
+        vbuf[0:2] = jnp.zeros((2, 4, W, CA), BF16)
+        mbuf[0:2] = jnp.zeros((2, 4, W, CB), BF16)
+
+    @pl.when(tm == 31)
+    def _():
+        cbuf[2:4] = jnp.zeros((2, 4, W, CB), BF16)
+        gbuf[2:4] = jnp.zeros((2, 4, W, CA), BF16)
+
     class Halo:
         def __init__(self, src, buf, way, sem):
             own = 2 if way > 0 else 0
             mine, theirs = pl.ds(own, 2), pl.ds(2 - own, 2)
-            beside = near(way, 0)
-            self.full = remote(src, buf.at[theirs, pl.ds(1, 2)], sem, 0, beside)
+            self.gives, self.takes = (until, since) if way > 0 else (since, until)
+            self.full = remote(src, buf.at[theirs, pl.ds(1, 2)], sem, 0, near(way, 0))
             self.down = remote(src.at[:, 1], buf.at[mine, 0], sem, 1, near(0, 1))
             self.up = remote(src.at[:, 0], buf.at[mine, 3], sem, 2, near(0, -1))
-            self.on_top = remote(buf.at[mine, 0], buf.at[theirs, 0], sem, 3, beside)
-            self.on_low = remote(buf.at[mine, 3], buf.at[theirs, 3], sem, 4, beside)
+            self.top = remote(buf.at[mine, 0], buf.at[theirs, 0], sem, 3, near(way, 0))
+            self.low = remote(buf.at[mine, 3], buf.at[theirs, 3], sem, 4, near(way, 0))
+            self.gives_top, self.gives_low = self.gives & upper, self.gives & lower
 
         def rims(self):
             pl.when(lower)(self.down.start)
             pl.when(upper)(self.up.start)
 
-        def forward(self):
-            @pl.when(upper)
-            def _():
-                self.down.wait_recv()
-                self.on_top.start()
-
-            @pl.when(lower)
-            def _():
-                self.up.wait_recv()
-                self.on_low.start()
+        def ahead(self):
+            pl.when(self.gives)(self.full.start)
 
         def corners(self):
-            @pl.when(upper)
-            def _():
-                self.on_top.wait()
-                self.up.wait_send()
-
-            @pl.when(lower)
-            def _():
-                self.on_low.wait()
-                self.down.wait_send()
+            pl.when(self.gives_top)(self.top.start)
+            pl.when(self.gives_low)(self.low.start)
+
+        def wait_rims(self):
+            pl.when(upper)(self.down.wait_recv)
+            pl.when(lower)(self.up.wait_recv)
+
+        def wait_ahead(self):
+            pl.when(self.takes)(self.full.wait_recv)
+
+        def wait_corners(self):
+            pl.when(self.takes & upper)(self.top.wait_recv)
+            pl.when(self.takes & lower)(self.low.wait_recv)
+
+        def sent(self):
+            pl.when(lower)(self.down.wait_send)
+            pl.when(upper)(self.up.wait_send)
+            pl.when(self.gives)(self.full.wait_send)
+            pl.when(self.gives_top)(self.top.wait_send)
+            pl.when(self.gives_low)(self.low.wait_send)
 
     class Shifts:
         def __init__(self, src, buf, dst, way, chan):
             self.own = 2 if way > 0 else 0
-            self.inside = (tm > 0) if way > 0 else (tm < 31)
             self.src, self.buf, self.dst, self.chan = src, buf, dst, chan
 
         def make(self, frames, rows_of):
@@ -141,8 +156,6 @@
                     else:
                         v = self.buf[f, r]
                     v = v.astype(F32)
-                    if frames != "own":
-                        v = jnp.where(self.inside, v, 0.0)
                     dst[f, r, :, chan : 2 * chan] = v.astype(BF16)
                     left = jnp.where(cell == 0, 0.0, pltpu.roll(v, 1, 0))
                     right = jnp.where(cell == W - 1, 0.0, pltpu.roll(v, W - 1, 0))
@@ -188,21 +201,23 @@
     pl.semaphore_wait(barrier, len(peers))
     halo_c.rims()
     halo_v.rims()
-    halo_c.full.start()
-    halo_v.full.start()
-    halo_c.forward()
-    halo_v.forward()
+    halo_c.ahead()
+    halo_v.ahead()
+    halo_c.wait_rims()
+    halo_c.corners()
+    halo_v.wait_rims()
+    halo_v.corners()
     shift_c.make("own", (0, 3))
+    back_b = back(back_b, us, kb, CB, EDGE)
     shift_v.make("own", (0, 3))
-    back_b = back(back_b, us, kb, CB, EDGE)
     pre = conv(pre, xs, ka, CA, EDGE)
-    halo_c.full.wait()
+    halo_c.wait_ahead()
     shift_c.make("other", (1, 2))
     back_b = back(back_b, us, kb, CB, PAST)
-    halo_v.full.wait()
+    halo_v.wait_ahead()
     shift_v.make("other", (1, 2))
     pre = conv(pre, xs, ka, CA, PAST)
-    halo_c.corners()
+    halo_c.wait_corners()
     shift_c.make("other", (0, 3))
     back_b = back(back_b, us, kb, CB, CORNERS)
     grad_mid = cot[...].reshape(CELLS, CB).astype(F32) + back_b
@@ -212,7 +227,7 @@
         qt[c] = jnp.concatenate(pick, 0).astype(BF16)
     grad_h = dot(grad_mid.astype(BF16), project[...], 1, 1)
 
-    halo_v.corners()
+    halo_v.wait_corners()
     shift_v.make("other", (0, 3))
     pre = conv(pre, xs, ka, CA, CORNERS)
     sig = jax.nn.sigmoid(pre)
@@ -221,12 +236,12 @@
     mown[...] = mid.astype(BF16).reshape(2, 2, W, CB)
     halo_m = Halo(mown, mbuf, 1, sem_m)
     halo_m.rims()
-    halo_m.full.start()
+    halo_m.ahead()
     grad_pre = grad_h * sig * (1.0 + pre * (1.0 - sig))
     gown[...] = grad_pre.astype(BF16).reshape(2, 2, W, CA)
     halo_g = Halo(gown, gbuf, -1, sem_g)
     halo_g.rims()
-    halo_g.full.start()
+    halo_g.ahead()
     out[...] = mid.reshape(2, 2, W, CB)
     grad_t = grad_pre.T
     for c in range(2):
@@ -237,25 +252,29 @@
         kt, kr = k // 3, k % 3
         return dot(left, xs[kt : kt + 2, kr : kr + 2].reshape(CELLS, 3 * CA))
 
-    copies_a = []
-    theirs = gt[1 - core].reshape(128, CELLS)
-    for k in range(9):
-        send_a[k] = chunk_a(theirs, k).astype(BF16).reshape(8, 16, 768)
-        cp = remote(send_a.at[k], recv_a.at[k], sem_a, k, partner)
-        cp.start()
-        copies_a.append(cp)
-
     class Group:
-        def __init__(self, s0x, r1x, s1x, r2y, sem1x, sem2y, s0y, r1y, s1y, r2x, sem1y, sem2x):
-            self.s0x, self.r1x, self.s1x, self.r2y, self.sem1x, self.sem2y = s0x, r1x, s1x, r2y, sem1x, sem2y
-            self.s0y, self.r1y, self.s1y, self.r2x, self.sem1y, self.sem2x = s0y, r1y, s1y, r2x, sem1y, sem2x
-
-        def x1(self, d, yl):
-            src = self.s0x.at[lax.rem(x + d, 4), yl]
-            return remote(src, self.r1x.at[d - 1, yl], self.sem1x, 2 * (d - 1) + yl, x_peer(d))
-
-        def y1(self, d):
-            return remote(self.s0y.at[lax.rem(y + d, 4)], self.r1y.at[d - 1], self.sem1y, d - 1, y_peer(d))
+        def __init__(self, s0x, q1x, r1x, s1x, r2y, s0y, q1y, r1y, s1y, r2x, sem1x, sem1y, sem2y, sem2x):
+            self.s0x, self.q1x, self.r1x, self.s1x, self.r2y = s0x, q1x, r1x, s1x, r2y
+            self.s0y, self.q1y, self.r1y, self.s1y, self.r2x = s0y, q1y, r1y, s1y, r2x
+            self.sem1x, self.sem1y, self.sem2y, self.sem2x = sem1x, sem1y, sem2y, sem2x
+
+        def x_far(self, yl, h):
+            src = self.s0x.at[lax.rem(x + 2, 4), yl, h]
+            return remote(src, self.q1x.at[yl, h], self.sem1x, 6 * yl + h, x_peer((1, 3)[h]))
+
+        def x_near(self, yl, side, h):
+            d = (1, 3)[side]
+            src = self.s0x.at[lax.rem(x + d, 4), yl, h]
+            return remote(src, self.r1x.at[side, yl, h], self.sem1x, 6 * yl + 2 + 2 * side + h, x_peer(d))
+
+        def y_far(self, h):
+            src = self.s0y.at[lax.rem(y + 2, 4), pl.ds(2 * h, 2)]
+            return remote(src, self.q1y.at[h], self.sem1y, h, y_peer((1, 3)[h]))
+
+        def y_near(self, side, h):
+            d = (1, 3)[side]
+            src = self.s0y.at[lax.rem(y + d, 4), pl.ds(2 * h, 2)]
+            return remote(src, self.r1y.at[side, pl.ds(2 * h, 2)], self.sem1y, 2 + 2 * side + h, y_peer(d))
 
         def y2(self, d):
             return remote(self.s1x.at[lax.rem(y + d, 4)], self.r2y.at[d - 1], self.sem2y, d - 1, y_peer(d))
@@ -264,25 +283,43 @@
             return remote(self.s1y.at[lax.rem(x + d, 4)], self.r2x.at[d - 1], self.sem2x, d - 1, x_peer(d))
 
         def send_x(self, yl):
-            for d in (2, 1, 3):
-                self.x1(d, yl).start()
-
-        def send_y(self, yl):
-            for yh in range(2):
-                d = lax.rem(2 * yh + yl - y + 4, 4)
-
-                @pl.when(d > 0)
-                def _():
-                    self.y1(d).start()
+            self.x_far(yl, 0).start()
+            self.x_far(yl, 1).start()
+            self.x_near(yl, 0, 1).start()
+            self.x_near(yl, 1, 0).start()
+
+        def send_y(self):
+            self.y_far(0).start()
+            self.y_far(1).start()
+            self.y_near(0, 1).start()
+            self.y_near(1, 0).start()
+
+        def relay_x(self, yl):
+            for h in range(2):
+                to = lax.rem(x + (1, 3)[h], 4)
+                self.x_far(yl, h).wait_recv()
+                both = self.s0x[to, yl, h].astype(F32) + self.q1x[yl, h].astype(F32)
+                self.s0x[to, yl, h] = both.astype(BF16)
+                self.x_near(yl, h, h).start()
+
+        def relay_y(self):
+            for h in range(2):
+                to, part = lax.rem(y + (1, 3)[h], 4), slice(2 * h, 2 * h + 2)
+                self.y_far(h).wait_recv()
+                both = self.s0y[to, part].astype(F32) + self.q1y[h].astype(F32)
+                self.s0y[to, part] = both.astype(BF16)
+                self.y_near(h, h).start()
 
         def add_x(self, yl):
-            for d in (1, 2, 3):
-                self.x1(d, yl).wait()
+            for h in range(2):
+                self.x_far(yl, h).wait_send()
+                for side in range(2):
+                    self.x_near(yl, side, h).wait()
             for yh in range(2):
                 to = 2 * yh + yl
                 acc = self.s0x[x, yl, yh].astype(F32)
-                for s in range(3):
-                    acc = acc + self.r1x[s, yl, yh].astype(F32)
+                for side in range(2):
+                    acc = acc + self.r1x[side, yl, yh].astype(F32)
                 self.s1x[to] = acc.astype(BF16)
                 d = lax.rem(to - y + 4, 4)
 
@@ -291,13 +328,15 @@
                     self.y2(d).start()
 
         def add_y(self):
-            for d in (1, 2, 3):
-                self.y1(d).wait()
+            for h in range(2):
+                self.y_far(h).wait_send()
+                for side in range(2):
+                    self.y_near(side, h).wait()
             for d in ORDER:
                 to = lax.rem(x + d, 4)
                 acc = self.s0y[y, to].astype(F32)
-                for s in range(3):
-                    acc = acc + self.r1y[s, to].astype(F32)
+                for side in range(2):
+                    acc = acc + self.r1y[side, to].astype(F32)
                 self.s1y[to] = acc.astype(BF16)
                 if d:
                     self.x2(d).start()
@@ -316,15 +355,25 @@
                 acc = acc + self.r2x[s].astype(F32)
             t_ref[:, lx:] = acc
 
-    group_a = Group(s0xa, r1xa, s1xa, r2ya, sem1xa, sem2ya, s0ya, r1ya, s1ya, r2xa, sem1ya, sem2xa)
-    group_b = Group(s0xb, r1xb, s1xb, r2yb, sem1xb, sem2yb, s0yb, r1yb, s1yb, r2xb, sem1yb, sem2xb)
-
-    mine = gt[core].reshape(128, CELLS)
+    group_a = Group(s0xa, q1xa, r1xa, s1xa, r2ya, s0ya, q1ya, r1ya, s1ya, r2xa, sem1xa, sem1ya, sem2ya, sem2xa)
+    group_b = Group(s0xb, q1xb, r1xb, s1xb, r2yb, s0yb, q1yb, r1yb, s1yb, r2xb, sem1xb, sem1yb, sem2yb, sem2xb)
+
+    left = jnp.concatenate([gt[1 - core].reshape(128, CELLS), gt[core].reshape(128, CELLS)], 0)
     cuts = sorted({768 * k for k in range(10)} | {0, XA, HALF_A, HALF_A + XA, 2 * HALF_A})
-    for k in range(9):
-        value = chunk_a(mine, k)
+    copies_a = []
+    for step in range(9 + LAG):
+        if step < 9:
+            value = chunk_a(left, step)
+            send_a[step] = value[0:128].astype(BF16).reshape(8, 16, 768)
+            cp = remote(send_a.at[step], recv_a.at[step], sem_a, step, partner)
+            cp.start()
+            copies_a.append(cp)
+            own_a[step] = value[128:256]
+        k = step - LAG
+        if k < 0:
+            continue
         copies_a[k].wait()
-        value = (value + recv_a[k].reshape(128, 768).astype(F32)).astype(BF16)
+        value = (own_a[k] + recv_a[k].reshape(128, 768).astype(F32)).astype(BF16)
         inside = [c for c in cuts if 768 * k <= c <= 768 * k + 768]
         for lo, hi in zip(inside[:-1], inside[1:]):
             yl, at = lo // HALF_A, lo % HALF_A
@@ -336,8 +385,7 @@
                     s0ya[(j // 4) * 2 + yl, j % 4, :, at - XA : at - XA + hi - lo] = cut
             if hi % HALF_A == XA:
                 group_a.send_x(yl)
-            if hi % HALF_A == 0:
-                group_a.send_y(yl)
+    group_a.send_y()
 
     mid_own = mid.T.astype(BF16)
     for k in range(9):
@@ -366,8 +414,10 @@
         send_b[j, yl] = value.astype(BF16)
     copy_b = remote(send_b, recv_b, sem_b, 0, partner)
     copy_b.start()
-    halo_m.forward()
-    halo_g.forward()
+    halo_m.wait_rims()
+    halo_m.corners()
+    halo_g.wait_rims()
+    halo_g.corners()
     copy_b.wait()
     for j, yl, value in packed(core):
         value = (value + recv_b[j, yl].astype(F32)).astype(BF16)
@@ -375,28 +425,38 @@
         s0yb[(j // 4) * 2 + yl, j % 4] = value[:, XB:]
     for yl in range(2):
         group_b.send_x(yl)
-        group_b.send_y(yl)
-
+    group_b.send_y()
+    for yl in range(2):
+        group_a.relay_x(yl)
+    group_a.relay_y()
+    for yl in range(2):
+        group_b.relay_x(yl)
+    group_b.relay_y()
+    group_a.add_x(0)
     every = CENTRE + EDGE + PAST + CORNERS
     shift_m = Shifts(mown, mbuf, ms, 1, CB)
     shift_m.make("own", (0, 1, 2, 3))
-    halo_m.full.wait()
-    halo_m.corners()
+    halo_m.wait_ahead()
+    halo_m.wait_corners()
     shift_m.make("other", (0, 1, 2, 3))
     out[...] = out[...] + conv(None, ms, kb, CB, every).reshape(2, 2, W, CB)
-    shift_g = Shifts(gown, gbuf, gs, -1, CA)
-    shift_g.make("own", (0, 1, 2, 3))
-    halo_g.full.wait()
-    halo_g.corners()
-    shift_g.make("other", (0, 1, 2, 3))
-    grad_video[...] = back(None, gs, ka, CA, every).reshape(2, 2, W, CA)
-
-    group_a.add_x(0)
+    done = [
+        pltpu.make_async_copy(out, out_hbm, sem_o.at[0]),
+        pltpu.make_async_copy(grad_video, grad_video_hbm, sem_o.at[1]),
+    ]
+    done[0].start()
     group_a.add_x(1)
     group_a.add_y()
     group_b.add_x(0)
     group_b.add_x(1)
     group_b.add_y()
+    shift_g = Shifts(gown, gbuf, gs, -1, CA)
+    shift_g.make("own", (0, 1, 2, 3))
+    halo_g.wait_ahead()
+    halo_g.wait_corners()
+    shift_g.make("other", (0, 1, 2, 3))
+    grad_video[...] = back(None, gs, ka, CA, every).reshape(2, 2, W, CA)
+    done[1].start()
     group_a.finish(t_a, XA)
     group_b.finish(t_b, XB)
 
@@ -433,11 +493,23 @@
     low = jnp.concatenate([total[0, 0:8, 256:384], total[1, 0:8, 256:384]], 0)
     grad_b[...] = low[:, 0:108]
     grad_p[...] = low.T[112:120]
+    for halo in (halo_c, halo_v, halo_m, halo_g):
+        halo.sent()
+    for cp in done:
+        cp.wait()
 
 
 def written(*refs):
+    took, gives, held, sem = refs[:5], refs[5:10], refs[10:15], refs[15]
+    reads = [pltpu.make_async_copy(took[i], held[i], sem.at[0, i]) for i in range(5)]
+    writes = [pltpu.make_async_copy(held[i], gives[i], sem.at[1, i]) for i in range(5)]
+    for cp in reads:
+        cp.start()
     for i in range(5):
-        refs[5 + i][...] = refs[i][...]
+        reads[i].wait()
+        writes[i].start()
+    for cp in writes:
+        cp.wait()
 
 
 def shards(video, kernel_a, project, kernel_b, cotangent):
@@ -448,7 +520,8 @@
     def group(lx, ly):
         return [
             pltpu.VMEM((4, 2, 2, 16, lx), BF16), pltpu.VMEM((4, 4, 16, ly), BF16),
-            pltpu.VMEM((3, 2, 2, 16, lx), BF16), pltpu.VMEM((3, 4, 16, ly), BF16),
+            pltpu.VMEM((2, 2, 16, lx), BF16), pltpu.VMEM((2, 2, 16, ly), BF16),
+            pltpu.VMEM((2, 2, 2, 16, lx), BF16), pltpu.VMEM((2, 4, 16, ly), BF16),
             pltpu.VMEM((4, 16, lx), BF16), pltpu.VMEM((4, 16, ly), BF16),
             pltpu.VMEM((3, 16, lx), BF16), pltpu.VMEM((3, 16, ly), BF16),
         ]
@@ -463,8 +536,9 @@
             jax.ShapeDtypeStruct((8, 16), F32),
         ],
         in_specs=[hbm] * 5,
-        out_specs=[vmem] * 5,
+        out_specs=[hbm, hbm, vmem, vmem, vmem],
         scratch_shapes=[
+            pltpu.VMEM((2, 2, W, CB), F32), pltpu.VMEM((2, 2, W, CA), F32),
             pltpu.VMEM((2, 2, W, CA), BF16), pltpu.VMEM((2, 2, W, CB), BF16), pltpu.VMEM((CA, CB), BF16),
             pltpu.VMEM((27 * CA, CA), BF16), pltpu.VMEM((27 * CB, CB), BF16),
             pltpu.VMEM((4, 4, W, CA), BF16), pltpu.VMEM((4, 4, W, CB), BF16),
@@ -474,6 +548,7 @@
             pltpu.VMEM((4, 4, W, 3 * CB), BF16), pltpu.VMEM((4, 4, W, 3 * CA), BF16),
             pltpu.VMEM((2, 8, 16, CELLS), BF16), pltpu.VMEM((2, 64, CELLS), BF16),
             pltpu.VMEM((9, 8, 16, 768), BF16), pltpu.VMEM((9, 8, 16, 768), BF16),
+            pltpu.VMEM((9, 128, 768), F32),
             pltpu.VMEM((8, 2, 16, XB + YB), BF16), pltpu.VMEM((8, 2, 16, XB + YB), BF16),
             pltpu.VMEM((2, 8, 8, 27 * CB), F32),
             *group(XA, YA),
@@ -482,8 +557,8 @@
             pltpu.VMEM((16, 16, 384), BF16), pltpu.VMEM((15, 16, 384), BF16),
             pltpu.VMEM((2, 16, 384), F32),
             dma((5,)), dma((2, 5)), dma((2, 5)), dma((2, 5)), dma((2, 5)), dma((2, 9)), dma((2, 1)),
-            *[dma((2, n)) for n in (6, 3, 3, 3) * 2],
-            dma((2, 15)),
+            *[dma((2, n)) for n in (12, 6, 3, 3, 12, 6, 3, 3, 15)],
+            dma((2,)),
         ],
         compiler_params=pltpu.CompilerParams(
             collective_id=0, has_side_effects=True, vmem_limit_bytes=56 * 1024 * 1024
@@ -492,8 +567,9 @@
     results = pl.pallas_call(
         written,
         out_shape=[jax.ShapeDtypeStruct(r.shape, F32) for r in results],
-        in_specs=[vmem] * 5,
-        out_specs=[vmem] * 5,
+        in_specs=[hbm] * 5,
+        out_specs=[hbm] * 5,
+        scratch_shapes=[*[pltpu.VMEM(r.shape, F32) for r in results], dma((2, 5))],
     )(*results)
     return results[0], results[1], results[2].T, results[3].T, results[4]
 

time: 56.7 us -> 57.7 us (1.018)
  Pallas kernels: 55.9 us -> 56.9 us
    pallas_call x1, Pallas kernels: 54 us -> 55 us  [shards(): pl.pallas_call(kernel, out_shape=[jax.ShapeDtypeStruct((2, 2, W, CB), F32...]
where the time goes in v5:
time: 57.7 us; the launch traced here: 57.6 us
  Pallas kernels  56.9 us (99%)
  between operations  0.64 us (1%)
    pallas_call x1, Pallas kernels, shards(): pl.pallas_call(kernel, out_shape=[jax.ShapeDtypeStruct((2, 2, W, CB), F32...  55 us
    pallas_call x1, Pallas kernels, shards(): pl.pallas_call(written, out_shape=[jax.ShapeDtypeStruct(r.shape, F32) for...  1.94 us

profile of v5, /device:TPU:1, one launch (start us, length us, event | category | flops | bytes accessed | tf_op | source)
XLA Modules:
  0.0 57.6 jit_solution(4541577695239193961)
XLA Ops:
  0.6 55.0 %shard_map.92 = (f32[2,2,96,128]{3,2,1,0:T(8,128)}, f32[2,2,96,256]{3,2,1,0:T(8,128)}, f32[32,216]{1,0:T(8,128)}, f32[16,108]{1,0:T(8,128)}, f32[8,16]{1,0:T(8,128)}) custom-call(bf16[2,2,96,256]{3,2,1,0:T(8,128)(2,1)} %video_hbm.1, bf16[2,2,96,128]{3,2,1,0:T(8,128)(2,1)} %cot_hbm.1, bf16[6912,256]{1,0:T(8,128)(2,1)} %ka_hbm.1, ...), custom_call_target="tpu_custom_call" | custom-call | tf_op jit(solution)/shard_map/pallas_call | solution.py:529
  55.6 1.9 %shard_map.93 = (f32[2,2,96,128]{3,2,1,0:T(8,128)}, f32[2,2,96,256]{3,2,1,0:T(8,128)}, f32[32,216]{1,0:T(8,128)}, f32[16,108]{1,0:T(8,128)}, f32[8,16]{1,0:T(8,128)}) custom-call(f32[2,2,96,128]{3,2,1,0:T(8,128)} %get-tuple-element.15.refs_0_, f32[2,2,96,256]{3,2,1,0:T(8,128)} %get-tuple-element.16.refs_1_, f32[32,216]{1,0:T(8,128)} %get-tuple-element.17.refs_2_, ...), custom_call_target="tpu_custom_call" | custom-call | tf_op jit(solution)/shard_map/pallas_call | solution.py:567

commit v6 on v4

--- a/solution.py
+++ b/solution.py
@@ -10,7 +10,8 @@
 CA, CB, W = 256, 128, 96
 CELLS = 4 * W
 HALF_A = 27 * CA // 2
-XA, YA = 1792, HALF_A - 1792
+XA, YA = 1664, HALF_A - 1664
+LAG = 3
 ORDER = (1, 2, 3, 0)
 
 
@@ -22,7 +23,7 @@
     video_hbm, cot_hbm, ka_hbm, project_hbm, kb_hbm,
     out_hbm, grad_video_hbm, grad_a, grad_b, grad_p,
     out, grad_video, video, cot, project, ka, kb, vbuf, cbuf, mbuf, gbuf, mown, gown, xs, us, ms, gs,
-    gt, qt, send_a, recv_a, send_b, recv_b, part,
+    gt, qt, send_a, recv_a, own_a, send_b, recv_b, part,
     s0xa, s0ya, r1xa, r1ya, s1xa, s1ya, r2ya, r2xa,
     s0b, r1b, s1b, r2b, tb, gb,
     t_a, msg, r3, total,
@@ -192,8 +193,8 @@
                 acc = term if acc is None else acc + term
         return acc
 
-    halo_c = Halo(cot, cbuf, -1, sem_c, True)
-    halo_v = Halo(video, vbuf, 1, sem_v, True)
+    halo_c = Halo(cot, cbuf, -1, sem_c, False)
+    halo_v = Halo(video, vbuf, 1, sem_v, False)
     shift_c = Shifts(cot, cbuf, us, -1, CB)
     shift_v = Shifts(video, vbuf, xs, 1, CA)
 
@@ -210,14 +211,14 @@
     pl.semaphore_wait(barrier, len(peers))
     halo_c.rims()
     halo_v.rims()
-    halo_c.corners()
-    halo_v.corners()
     halo_c.ahead()
     halo_v.ahead()
     halo_c.wait_rims()
+    halo_c.corners()
+    halo_v.wait_rims()
+    halo_v.corners()
     shift_c.make("own", (0, 3))
     back_b = back(back_b, us, kb, CB, EDGE)
-    halo_v.wait_rims()
     shift_v.make("own", (0, 3))
     pre = conv(pre, xs, ka, CA, EDGE)
     halo_c.wait_ahead()
@@ -248,7 +249,7 @@
     halo_m.ahead()
     grad_pre = grad_h * sig * (1.0 + pre * (1.0 - sig))
     gown[...] = grad_pre.astype(BF16).reshape(2, 2, W, CA)
-    halo_g = Halo(gown, gbuf, -1, sem_g, False)
+    halo_g = Halo(gown, gbuf, -1, sem_g, True)
     halo_g.rims()
     halo_g.ahead()
     out[...] = mid.reshape(2, 2, W, CB)
@@ -260,14 +261,6 @@
     def chunk_a(left, k):
         kt, kr = k // 3, k % 3
         return dot(left, xs[kt : kt + 2, kr : kr + 2].reshape(CELLS, 3 * CA))
-
-    copies_a = []
-    theirs = gt[1 - core].reshape(128, CELLS)
-    for k in range(9):
-        send_a[k] = chunk_a(theirs, k).astype(BF16).reshape(8, 16, 768)
-        cp = remote(send_a.at[k], recv_a.at[k], sem_a, k, partner)
-        cp.start()
-        copies_a.append(cp)
 
     class Group:
         def __init__(self, s0x, r1x, s1x, r2y, sem1x, sem2y, s0y, r1y, s1y, r2x, sem1y, sem2x):
@@ -342,12 +335,22 @@
 
     group_a = Group(s0xa, r1xa, s1xa, r2ya, sem1xa, sem2ya, s0ya, r1ya, s1ya, r2xa, sem1ya, sem2xa)
 
-    mine = gt[core].reshape(128, CELLS)
+    left = jnp.concatenate([gt[1 - core].reshape(128, CELLS), gt[core].reshape(128, CELLS)], 0)
     cuts = sorted({768 * k for k in range(10)} | {0, XA, HALF_A, HALF_A + XA, 2 * HALF_A})
-    for k in range(9):
-        value = chunk_a(mine, k)
+    copies_a = []
+    for step in range(9 + LAG):
+        if step < 9:
+            value = chunk_a(left, step)
+            send_a[step] = value[0:128].astype(BF16).reshape(8, 16, 768)
+            cp = remote(send_a.at[step], recv_a.at[step], sem_a, step, partner)
+            cp.start()
+            copies_a.append(cp)
+            own_a[step] = value[128:256]
+        k = step - LAG
+        if k < 0:
+            continue
         copies_a[k].wait()
-        value = (value + recv_a[k].reshape(128, 768).astype(F32)).astype(BF16)
+        value = (own_a[k] + recv_a[k].reshape(128, 768).astype(F32)).astype(BF16)
         inside = [c for c in cuts if 768 * k <= c <= 768 * k + 768]
         for lo, hi in zip(inside[:-1], inside[1:]):
             yl, at = lo // HALF_A, lo % HALF_A
@@ -391,8 +394,6 @@
     copy_b.start()
     halo_m.wait_rims()
     halo_m.corners()
-    halo_g.wait_rims()
-    halo_g.corners()
     copy_b.wait()
     for z, j, yl, value in packed(core):
         s0b[z, j, yl] = (value + recv_b[z, j, yl].astype(F32)).astype(BF16)
@@ -403,6 +404,7 @@
     for d in (4, 3, 5, 2, 6, 1, 7):
         first_b[d - 1].start()
 
+    group_a.add_x(0)
     every = CENTRE + EDGE + PAST + CORNERS
     shift_m = Shifts(mown, mbuf, ms, 1, CB)
     shift_m.make("own", (0, 1, 2, 3))
@@ -410,20 +412,23 @@
     halo_m.wait_corners()
     shift_m.make("other", (0, 1, 2, 3))
     out[...] = out[...] + conv(None, ms, kb, CB, every).reshape(2, 2, W, CB)
-    done = [pltpu.make_async_copy(out, out_hbm, sem_o.at[0]), pltpu.make_async_copy(grad_video, grad_video_hbm, sem_o.at[1])]
+    done = [
+        pltpu.make_async_copy(out, out_hbm, sem_o.at[0]),
+        pltpu.make_async_copy(grad_video, grad_video_hbm, sem_o.at[1]),
+    ]
     done[0].start()
-    shift_g = Shifts(gown, gbuf, gs, -1, CA)
-    shift_g.make("own", (0, 1, 2, 3))
-    halo_g.wait_ahead()
-    halo_g.wait_corners()
-    shift_g.make("other", (0, 1, 2, 3))
-    grad_video[...] = back(None, gs, ka, CA, every).reshape(2, 2, W, CA)
-
-    done[1].start()
-
-    group_a.add_x(0)
     group_a.add_x(1)
     group_a.add_y()
+    halo_g.corners()
+    group_a.finish(t_a, XA)
+    for k in range(16):
+        high = jnp.concatenate([t_a[:, 216 * k : 216 * k + 216], jnp.zeros((16, 40), F32)], 1)
+        msg[k] = high.astype(BF16)
+    last = []
+    for d in range(1, 16):
+        cp = remote(msg.at[lax.rem(b + d, 16)], r3.at[d - 1], sem3, d - 1, z_peer(d))
+        cp.start()
+        last.append(cp)
     for cp in first_b:
         cp.wait()
     for j in range(8):
@@ -441,15 +446,14 @@
                 cp = remote(src, r2b.at[slot], sem2b, slot, plane(dx, dy))
                 cp.start()
                 second_b.append(cp)
-    group_a.finish(t_a, XA)
-    for k in range(16):
-        high = jnp.concatenate([t_a[:, 216 * k : 216 * k + 216], jnp.zeros((16, 40), F32)], 1)
-        msg[k] = high.astype(BF16)
-    last = []
-    for d in range(1, 16):
-        cp = remote(msg.at[lax.rem(b + d, 16)], r3.at[d - 1], sem3, d - 1, z_peer(d))
-        cp.start()
-        last.append(cp)
+    shift_g = Shifts(gown, gbuf, gs, -1, CA)
+    halo_g.wait_rims()
+    shift_g.make("own", (0, 1, 2, 3))
+    halo_g.wait_ahead()
+    halo_g.wait_corners()
+    shift_g.make("other", (0, 1, 2, 3))
+    grad_video[...] = back(None, gs, ka, CA, every).reshape(2, 2, W, CA)
+    done[1].start()
     for cp in second_b:
         cp.wait()
     acc = s1b[y // 2, x, lax.rem(y, 2)].astype(F32)
@@ -529,6 +533,7 @@
             pltpu.VMEM((4, 4, W, 3 * CB), BF16), pltpu.VMEM((4, 4, W, 3 * CA), BF16),
             pltpu.VMEM((2, 8, 16, CELLS), BF16), pltpu.VMEM((2, 64, CELLS), BF16),
             pltpu.VMEM((9, 8, 16, 768), BF16), pltpu.VMEM((9, 8, 16, 768), BF16),
+            pltpu.VMEM((9, 128, 768), F32),
             pltpu.VMEM((8, 8, 2, 16, 128), BF16), pltpu.VMEM((8, 8, 2, 16, 128), BF16),
             pltpu.VMEM((2, 8, 8, 27 * CB), F32),
             *group(XA, YA),

time: 61.8 us -> 61.1 us (0.989)
    pallas_call x1, Pallas kernels: 59.1 us -> 58.4 us  [shards(): pl.pallas_call(kernel, out_shape=[jax.ShapeDtypeStruct((2, 2, W, CB), F32...]
where the time goes in v6:
time: 61.1 us; the launch traced here: 61 us
  Pallas kernels  60.4 us (99%)
  between operations  0.64 us (1%)
    pallas_call x1, Pallas kernels, shards(): pl.pallas_call(kernel, out_shape=[jax.ShapeDtypeStruct((2, 2, W, CB), F32...  58.4 us
    pallas_call x1, Pallas kernels, shards(): pl.pallas_call(written, out_shape=[jax.ShapeDtypeStruct(r.shape, F32) for...  1.94 us

profile of v6, /device:TPU:1, one launch (start us, length us, event | category | flops | bytes accessed | tf_op | source)
XLA Modules:
  0.0 61.0 jit_solution(6663023678873618242)
XLA Ops:
  0.6 58.4 %shard_map.92 = (f32[2,2,96,128]{3,2,1,0:T(8,128)}, f32[2,2,96,256]{3,2,1,0:T(8,128)}, f32[32,216]{1,0:T(8,128)}, f32[16,108]{1,0:T(8,128)}, f32[8,16]{1,0:T(8,128)}) custom-call(bf16[2,2,96,256]{3,2,1,0:T(8,128)(2,1)} %video_hbm.1, bf16[2,2,96,128]{3,2,1,0:T(8,128)(2,1)} %cot_hbm.1, bf16[6912,256]{1,0:T(8,128)(2,1)} %ka_hbm.1, ...), custom_call_target="tpu_custom_call" | custom-call | tf_op jit(solution)/shard_map/pallas_call | solution.py:514
  59.1 1.9 %shard_map.93 = (f32[2,2,96,128]{3,2,1,0:T(8,128)}, f32[2,2,96,256]{3,2,1,0:T(8,128)}, f32[32,216]{1,0:T(8,128)}, f32[16,108]{1,0:T(8,128)}, f32[8,16]{1,0:T(8,128)}) custom-call(f32[2,2,96,128]{3,2,1,0:T(8,128)} %get-tuple-element.15.refs_0_, f32[2,2,96,256]{3,2,1,0:T(8,128)} %get-tuple-element.16.refs_1_, f32[32,216]{1,0:T(8,128)} %get-tuple-element.17.refs_2_, ...), custom_call_target="tpu_custom_call" | custom-call | tf_op jit(solution)/shard_map/pallas_call | solution.py:554

commit v7 on v5

--- a/solution.py
+++ b/solution.py
@@ -10,7 +10,7 @@
 CA, CB, W = 256, 128, 96
 CELLS = 4 * W
 HALF_A = 27 * CA // 2
-XA, YA = 1664, HALF_A - 1664
+XA, YA = 1792, HALF_A - 1792
 XB, YB = 512, 512
 PB = 896
 LAG = 3
@@ -28,9 +28,9 @@
     gt, qt, send_a, recv_a, own_a, send_b, recv_b, part,
     s0xa, s0ya, q1xa, q1ya, r1xa, r1ya, s1xa, s1ya, r2ya, r2xa,
     s0xb, s0yb, q1xb, q1yb, r1xb, r1yb, s1xb, s1yb, r2yb, r2xb,
-    t_a, t_b, msg, r3, total,
+    t_a, t_b, msg_a, r3a, total_a, msg_b, r3b, total_b,
     sem_w, sem_v, sem_c, sem_m, sem_g, sem_a, sem_b,
-    sem1xa, sem1ya, sem2ya, sem2xa, sem1xb, sem1yb, sem2yb, sem2xb, sem3, sem_o,
+    sem1xa, sem1ya, sem2ya, sem2xa, sem1xb, sem1yb, sem2yb, sem2xb, sem3a, sem3b, sem_o,
 ):
     tm = lax.axis_index("tm")
     rows = lax.axis_index("rows")
@@ -64,9 +64,9 @@
         )
 
     barrier = pltpu.get_barrier_semaphore()
-    peers = [near(dt, dr) for dt, dr in ((0, 1), (0, -1), (1, 0), (-1, 0))]
-    peers += [x_peer(d) for d in range(1, 4)] + [y_peer(d) for d in range(1, 4)]
-    peers += [z_peer(d) for d in range(1, 16)]
+    peers = [z_peer(d) for d in (8, 9, 7, 10, 6, 11, 5, 12, 4, 13, 3, 14, 2, 15, 1)]
+    peers += [near(dt, dr) for dt, dr in ((0, 1), (0, -1), (1, 0), (-1, 0))]
+    peers += [y_peer(d) for d in (2, 1, 3)] + [x_peer(d) for d in (2, 1, 3)]
     for to in peers:
         pl.semaphore_signal(barrier, inc=1, device_id=to, device_id_type=MESH)
 
@@ -183,11 +183,16 @@
                 acc = term if acc is None else acc + term
         return acc
 
-    halo_c = Halo(cot, cbuf, -1, sem_c)
-    halo_v = Halo(video, vbuf, 1, sem_v)
+    halo_c = Halo(cot_hbm, cbuf, -1, sem_c)
+    halo_v = Halo(video_hbm, vbuf, 1, sem_v)
     shift_c = Shifts(cot, cbuf, us, -1, CB)
     shift_v = Shifts(video, vbuf, xs, 1, CA)
 
+    pl.semaphore_wait(barrier, len(peers))
+    halo_c.rims()
+    halo_v.rims()
+    halo_c.ahead()
+    halo_v.ahead()
     loads[0].wait()
     loads[1].wait()
     shift_c.make("own", (1, 2))
@@ -198,11 +203,6 @@
     loads[4].wait()
     pre = conv(None, xs, ka, CA, CENTRE)
 
-    pl.semaphore_wait(barrier, len(peers))
-    halo_c.rims()
-    halo_v.rims()
-    halo_c.ahead()
-    halo_v.ahead()
     halo_c.wait_rims()
     halo_c.corners()
     halo_v.wait_rims()
@@ -288,11 +288,16 @@
             self.x_near(yl, 0, 1).start()
             self.x_near(yl, 1, 0).start()
 
-        def send_y(self):
-            self.y_far(0).start()
-            self.y_far(1).start()
-            self.y_near(0, 1).start()
-            self.y_near(1, 0).start()
+        def send_y(self, yl):
+            @pl.when(y_lo == yl)
+            def _():
+                self.y_far(0).start()
+                self.y_far(1).start()
+
+            @pl.when(y_lo != yl)
+            def _():
+                self.y_near(0, 1).start()
+                self.y_near(1, 0).start()
 
         def relay_x(self, yl):
             for h in range(2):
@@ -341,13 +346,15 @@
                 if d:
                     self.x2(d).start()
 
-        def finish(self, t_ref, lx):
+        def finish_x(self, t_ref, lx):
             for d in (1, 2, 3):
                 self.y2(d).wait()
             acc = self.s1x[y].astype(F32)
             for s in range(3):
                 acc = acc + self.r2y[s].astype(F32)
             t_ref[:, :lx] = acc
+
+        def finish_y(self, t_ref, lx):
             for d in (1, 2, 3):
                 self.x2(d).wait()
             acc = self.s1y[x].astype(F32)
@@ -385,8 +392,13 @@
                     s0ya[(j // 4) * 2 + yl, j % 4, :, at - XA : at - XA + hi - lo] = cut
             if hi % HALF_A == XA:
                 group_a.send_x(yl)
-    group_a.send_y()
-
+            if hi % HALF_A == 0:
+                group_a.send_y(yl)
+
+    halo_m.wait_rims()
+    halo_m.corners()
+    halo_g.wait_rims()
+    halo_g.corners()
     mid_own = mid.T.astype(BF16)
     for k in range(9):
         kt, kr = k // 3, k % 3
@@ -414,10 +426,6 @@
         send_b[j, yl] = value.astype(BF16)
     copy_b = remote(send_b, recv_b, sem_b, 0, partner)
     copy_b.start()
-    halo_m.wait_rims()
-    halo_m.corners()
-    halo_g.wait_rims()
-    halo_g.corners()
     copy_b.wait()
     for j, yl, value in packed(core):
         value = (value + recv_b[j, yl].astype(F32)).astype(BF16)
@@ -425,14 +433,14 @@
         s0yb[(j // 4) * 2 + yl, j % 4] = value[:, XB:]
     for yl in range(2):
         group_b.send_x(yl)
-    group_b.send_y()
+    for yl in range(2):
+        group_b.send_y(yl)
     for yl in range(2):
         group_a.relay_x(yl)
     group_a.relay_y()
     for yl in range(2):
         group_b.relay_x(yl)
     group_b.relay_y()
-    group_a.add_x(0)
     every = CENTRE + EDGE + PAST + CORNERS
     shift_m = Shifts(mown, mbuf, ms, 1, CB)
     shift_m.make("own", (0, 1, 2, 3))
@@ -445,11 +453,41 @@
         pltpu.make_async_copy(grad_video, grad_video_hbm, sem_o.at[1]),
     ]
     done[0].start()
+    group_a.add_x(0)
     group_a.add_x(1)
     group_a.add_y()
     group_b.add_x(0)
     group_b.add_x(1)
     group_b.add_y()
+    def give(msg, r3, sem, k):
+        d = lax.rem(k - b + 16, 16)
+
+        @pl.when(d > 0)
+        def _():
+            remote(msg.at[k], r3.at[d - 1], sem, d - 1, z_peer(d)).start()
+
+    for k in range(16):
+        if k == 0:
+            group_a.finish_x(t_a, XA)
+        if k == 8:
+            group_a.finish_y(t_a, XA)
+        block = t_a[:, 216 * k : 216 * k + 216]
+        msg_a[k] = jnp.concatenate([block, jnp.zeros((16, 40), F32)], 1).astype(BF16)
+        give(msg_a, r3a, sem3a, k)
+    group_b.finish_x(t_b, XB)
+    group_b.finish_y(t_b, XB)
+    part_b = jnp.concatenate([t_b[0:8, 0:PB], t_b[8:16, 0:PB]], 1)
+    part_b = jnp.where(y_lo == 0, part_b[:, 0:1728], part_b[:, 64:1792])
+    part_p = t_b[0:8, PB : PB + 128]
+    for k in range(16):
+        low = jnp.concatenate(
+            [
+                part_b[:, 108 * k : 108 * k + 108], jnp.zeros((8, 4), F32),
+                part_p[:, 8 * k : 8 * k + 8], jnp.zeros((8, 8), F32),
+            ], 1,
+        )
+        msg_b[k] = jnp.concatenate([low, jnp.zeros((8, 128), F32)], 0).astype(BF16)
+        give(msg_b, r3b, sem3b, k)
     shift_g = Shifts(gown, gbuf, gs, -1, CA)
     shift_g.make("own", (0, 1, 2, 3))
     halo_g.wait_ahead()
@@ -457,40 +495,24 @@
     shift_g.make("other", (0, 1, 2, 3))
     grad_video[...] = back(None, gs, ka, CA, every).reshape(2, 2, W, CA)
     done[1].start()
-    group_a.finish(t_a, XA)
-    group_b.finish(t_b, XB)
-
-    part_b = jnp.concatenate([t_b[0:8, 0:PB], t_b[8:16, 0:PB]], 1)
-    part_b = jnp.where(y_lo == 0, part_b[:, 0:1728], part_b[:, 64:1792])
-    part_p = t_b[0:8, PB : PB + 128]
-    for k in range(16):
-        high = jnp.concatenate([t_a[:, 216 * k : 216 * k + 216], jnp.zeros((16, 40), F32)], 1)
-        low = jnp.concatenate(
-            [
-                part_b[:, 108 * k : 108 * k + 108], jnp.zeros((8, 4), F32),
-                part_p[:, 8 * k : 8 * k + 8], jnp.zeros((8, 8), F32),
-            ], 1,
-        )
-        low = jnp.concatenate([low, jnp.zeros((8, 128), F32)], 0)
-        msg[k] = jnp.concatenate([high, low], 1).astype(BF16)
-    last = []
-    for d in range(1, 16):
-        cp = remote(msg.at[lax.rem(b + d, 16)], r3.at[d - 1], sem3, d - 1, z_peer(d))
-        cp.start()
-        last.append(cp)
-    for cp in last:
-        cp.wait()
-    same = msg[b].astype(F32)
-    for d in range(2, 16, 2):
-        same = same + r3[d - 1].astype(F32)
-    other = r3[0].astype(F32)
-    for d in range(3, 16, 2):
-        other = other + r3[d - 1].astype(F32)
     scale = 1.0 / (64 * 16 * W) ** 0.5
-    total[core] = same * scale
-    total[1 - core] = other * scale
-    grad_a[...] = total[:, :, 0:216].reshape(32, 216)
-    low = jnp.concatenate([total[0, 0:8, 256:384], total[1, 0:8, 256:384]], 0)
+
+    def gathered(msg, r3, sem, total):
+        for d in range(1, 16):
+            remote(msg.at[lax.rem(b + d, 16)], r3.at[d - 1], sem, d - 1, z_peer(d)).wait()
+        same = msg[b].astype(F32)
+        for d in range(2, 16, 2):
+            same = same + r3[d - 1].astype(F32)
+        other = r3[0].astype(F32)
+        for d in range(3, 16, 2):
+            other = other + r3[d - 1].astype(F32)
+        total[core] = same * scale
+        total[1 - core] = other * scale
+
+    gathered(msg_a, r3a, sem3a, total_a)
+    grad_a[...] = total_a[:, :, 0:216].reshape(32, 216)
+    gathered(msg_b, r3b, sem3b, total_b)
+    low = jnp.concatenate([total_b[0, 0:8], total_b[1, 0:8]], 0)
     grad_b[...] = low[:, 0:108]
     grad_p[...] = low.T[112:120]
     for halo in (halo_c, halo_v, halo_m, halo_g):
@@ -554,10 +576,10 @@
             *group(XA, YA),
             *group(XB, YB),
             pltpu.VMEM((16, HALF_A), F32), pltpu.VMEM((16, XB + YB), F32),
-            pltpu.VMEM((16, 16, 384), BF16), pltpu.VMEM((15, 16, 384), BF16),
-            pltpu.VMEM((2, 16, 384), F32),
+            pltpu.VMEM((16, 16, 256), BF16), pltpu.VMEM((15, 16, 256), BF16), pltpu.VMEM((2, 16, 256), F32),
+            pltpu.VMEM((16, 16, 128), BF16), pltpu.VMEM((15, 16, 128), BF16), pltpu.VMEM((2, 16, 128), F32),
             dma((5,)), dma((2, 5)), dma((2, 5)), dma((2, 5)), dma((2, 5)), dma((2, 9)), dma((2, 1)),
-            *[dma((2, n)) for n in (12, 6, 3, 3, 12, 6, 3, 3, 15)],
+            *[dma((2, n)) for n in (12, 6, 3, 3, 12, 6, 3, 3, 15, 15)],
             dma((2,)),
         ],
         compiler_params=pltpu.CompilerParams(

time: 57.7 us -> 54.4 us (0.943)
  Pallas kernels: 56.9 us -> 53.6 us
    pallas_call x1, Pallas kernels: 55 us -> 51.7 us  [shards(): pl.pallas_call(kernel, out_shape=[jax.ShapeDtypeStruct((2, 2, W, CB), F32...]
where the time goes in v7:
time: 54.4 us; the launch traced here: 54.3 us
  Pallas kernels  53.6 us (99%)
  between operations  0.64 us (1%)
    pallas_call x1, Pallas kernels, shards(): pl.pallas_call(kernel, out_shape=[jax.ShapeDtypeStruct((2, 2, W, CB), F32...  51.7 us
    pallas_call x1, Pallas kernels, shards(): pl.pallas_call(written, out_shape=[jax.ShapeDtypeStruct(r.shape, F32) for...  1.94 us

profile of v7, /device:TPU:1, one launch (start us, length us, event | category | flops | bytes accessed | tf_op | source)
XLA Modules:
  0.0 54.3 jit_solution(12284231877727784292)
XLA Ops:
  0.6 51.7 %shard_map.92 = (f32[2,2,96,128]{3,2,1,0:T(8,128)}, f32[2,2,96,256]{3,2,1,0:T(8,128)}, f32[32,216]{1,0:T(8,128)}, f32[16,108]{1,0:T(8,128)}, f32[8,16]{1,0:T(8,128)}) custom-call(bf16[2,2,96,256]{3,2,1,0:T(8,128)(2,1)} %video_hbm.1, bf16[2,2,96,128]{3,2,1,0:T(8,128)(2,1)} %cot_hbm.1, bf16[6912,256]{1,0:T(8,128)(2,1)} %ka_hbm.1, ...), custom_call_target="tpu_custom_call" | custom-call | tf_op jit(solution)/shard_map/pallas_call | solution.py:551
  52.3 1.9 %shard_map.93 = (f32[2,2,96,128]{3,2,1,0:T(8,128)}, f32[2,2,96,256]{3,2,1,0:T(8,128)}, f32[32,216]{1,0:T(8,128)}, f32[16,108]{1,0:T(8,128)}, f32[8,16]{1,0:T(8,128)}) custom-call(f32[2,2,96,128]{3,2,1,0:T(8,128)} %get-tuple-element.15.refs_0_, f32[2,2,96,256]{3,2,1,0:T(8,128)} %get-tuple-element.16.refs_1_, f32[32,216]{1,0:T(8,128)} %get-tuple-element.17.refs_2_, ...), custom_call_target="tpu_custom_call" | custom-call | tf_op jit(solution)/shard_map/pallas_call | solution.py:589

commit v8 on v7

--- a/solution.py
+++ b/solution.py
@@ -232,17 +232,7 @@
     pre = conv(pre, xs, ka, CA, CORNERS)
     sig = jax.nn.sigmoid(pre)
     hidden = (pre * sig).astype(BF16)
-    mid = dot(hidden, project[...])
-    mown[...] = mid.astype(BF16).reshape(2, 2, W, CB)
-    halo_m = Halo(mown, mbuf, 1, sem_m)
-    halo_m.rims()
-    halo_m.ahead()
     grad_pre = grad_h * sig * (1.0 + pre * (1.0 - sig))
-    gown[...] = grad_pre.astype(BF16).reshape(2, 2, W, CA)
-    halo_g = Halo(gown, gbuf, -1, sem_g)
-    halo_g.rims()
-    halo_g.ahead()
-    out[...] = mid.reshape(2, 2, W, CB)
     grad_t = grad_pre.T
     for c in range(2):
         for j in range(8):
@@ -368,6 +358,16 @@
     left = jnp.concatenate([gt[1 - core].reshape(128, CELLS), gt[core].reshape(128, CELLS)], 0)
     cuts = sorted({768 * k for k in range(10)} | {0, XA, HALF_A, HALF_A + XA, 2 * HALF_A})
     copies_a = []
+    mid = dot(hidden, project[...])
+    mown[...] = mid.astype(BF16).reshape(2, 2, W, CB)
+    halo_m = Halo(mown, mbuf, 1, sem_m)
+    halo_m.rims()
+    halo_m.ahead()
+    gown[...] = grad_pre.astype(BF16).reshape(2, 2, W, CA)
+    halo_g = Halo(gown, gbuf, -1, sem_g)
+    halo_g.rims()
+    halo_g.ahead()
+    out[...] = mid.reshape(2, 2, W, CB)
     for step in range(9 + LAG):
         if step < 9:
             value = chunk_a(left, step)
@@ -395,10 +395,6 @@
             if hi % HALF_A == 0:
                 group_a.send_y(yl)
 
-    halo_m.wait_rims()
-    halo_m.corners()
-    halo_g.wait_rims()
-    halo_g.corners()
     mid_own = mid.T.astype(BF16)
     for k in range(9):
         kt, kr = k // 3, k % 3
@@ -435,6 +431,10 @@
         group_b.send_x(yl)
     for yl in range(2):
         group_b.send_y(yl)
+    halo_m.wait_rims()
+    halo_m.corners()
+    halo_g.wait_rims()
+    halo_g.corners()
     for yl in range(2):
         group_a.relay_x(yl)
     group_a.relay_y()

time: 54.4 us -> 54.1 us (level)
  no operation moved by 1% of the time
where the time goes in v8:
time: 54.1 us; the launch traced here: 54 us
  Pallas kernels  53.4 us (99%)
  between operations  0.64 us (1%)
    pallas_call x1, Pallas kernels, shards(): pl.pallas_call(kernel, out_shape=[jax.ShapeDtypeStruct((2, 2, W, CB), F32...  51.4 us
    pallas_call x1, Pallas kernels, shards(): pl.pallas_call(written, out_shape=[jax.ShapeDtypeStruct(r.shape, F32) for...  1.94 us

profile of v8, /device:TPU:1, one launch (start us, length us, event | category | flops | bytes accessed | tf_op | source)
XLA Modules:
  0.0 54.0 jit_solution(16291696759506349002)
XLA Ops:
  0.6 51.4 %shard_map.92 = (f32[2,2,96,128]{3,2,1,0:T(8,128)}, f32[2,2,96,256]{3,2,1,0:T(8,128)}, f32[32,216]{1,0:T(8,128)}, f32[16,108]{1,0:T(8,128)}, f32[8,16]{1,0:T(8,128)}) custom-call(bf16[2,2,96,256]{3,2,1,0:T(8,128)(2,1)} %video_hbm.1, bf16[2,2,96,128]{3,2,1,0:T(8,128)(2,1)} %cot_hbm.1, bf16[6912,256]{1,0:T(8,128)(2,1)} %ka_hbm.1, ...), custom_call_target="tpu_custom_call" | custom-call | tf_op jit(solution)/shard_map/pallas_call | solution.py:551
  52.1 1.9 %shard_map.93 = (f32[2,2,96,128]{3,2,1,0:T(8,128)}, f32[2,2,96,256]{3,2,1,0:T(8,128)}, f32[32,216]{1,0:T(8,128)}, f32[16,108]{1,0:T(8,128)}, f32[8,16]{1,0:T(8,128)}) custom-call(f32[2,2,96,128]{3,2,1,0:T(8,128)} %get-tuple-element.15.refs_0_, f32[2,2,96,256]{3,2,1,0:T(8,128)} %get-tuple-element.16.refs_1_, f32[32,216]{1,0:T(8,128)} %get-tuple-element.17.refs_2_, ...), custom_call_target="tpu_custom_call" | custom-call | tf_op jit(solution)/shard_map/pallas_call | solution.py:589

commit v9 on v8

--- a/solution.py
+++ b/solution.py
@@ -221,10 +221,6 @@
     shift_c.make("other", (0, 3))
     back_b = back(back_b, us, kb, CB, CORNERS)
     grad_mid = cot[...].reshape(CELLS, CB).astype(F32) + back_b
-    mid_t = grad_mid.T
-    for c in range(2):
-        pick = [mid_t[16 * j + 8 * c : 16 * j + 8 * c + 8] for j in range(8)]
-        qt[c] = jnp.concatenate(pick, 0).astype(BF16)
     grad_h = dot(grad_mid.astype(BF16), project[...], 1, 1)
 
     halo_v.wait_corners()
@@ -395,6 +391,10 @@
             if hi % HALF_A == 0:
                 group_a.send_y(yl)
 
+    mid_t = grad_mid.T
+    for c in range(2):
+        pick = [mid_t[16 * j + 8 * c : 16 * j + 8 * c + 8] for j in range(8)]
+        qt[c] = jnp.concatenate(pick, 0).astype(BF16)
     mid_own = mid.T.astype(BF16)
     for k in range(9):
         kt, kr = k // 3, k % 3

time: 54.1 us -> 54.1 us (level)
  no operation moved by 1% of the time
where the time goes in v9:
time: 54.1 us; the launch traced here: 54 us
  Pallas kernels  53.4 us (99%)
  between operations  0.64 us (1%)
    pallas_call x1, Pallas kernels, shards(): pl.pallas_call(kernel, out_shape=[jax.ShapeDtypeStruct((2, 2, W, CB), F32...  51.4 us
    pallas_call x1, Pallas kernels, shards(): pl.pallas_call(written, out_shape=[jax.ShapeDtypeStruct(r.shape, F32) for...  1.94 us

profile of v9, /device:TPU:1, one launch (start us, length us, event | category | flops | bytes accessed | tf_op | source)
XLA Modules:
  0.0 54.0 jit_solution(2395115974960351055)
XLA Ops:
  0.6 51.4 %shard_map.92 = (f32[2,2,96,128]{3,2,1,0:T(8,128)}, f32[2,2,96,256]{3,2,1,0:T(8,128)}, f32[32,216]{1,0:T(8,128)}, f32[16,108]{1,0:T(8,128)}, f32[8,16]{1,0:T(8,128)}) custom-call(bf16[2,2,96,256]{3,2,1,0:T(8,128)(2,1)} %video_hbm.1, bf16[2,2,96,128]{3,2,1,0:T(8,128)(2,1)} %cot_hbm.1, bf16[6912,256]{1,0:T(8,128)(2,1)} %ka_hbm.1, ...), custom_call_target="tpu_custom_call" | custom-call | tf_op jit(solution)/shard_map/pallas_call | solution.py:551
  52.1 1.9 %shard_map.93 = (f32[2,2,96,128]{3,2,1,0:T(8,128)}, f32[2,2,96,256]{3,2,1,0:T(8,128)}, f32[32,216]{1,0:T(8,128)}, f32[16,108]{1,0:T(8,128)}, f32[8,16]{1,0:T(8,128)}) custom-call(f32[2,2,96,128]{3,2,1,0:T(8,128)} %get-tuple-element.15.refs_0_, f32[2,2,96,256]{3,2,1,0:T(8,128)} %get-tuple-element.16.refs_1_, f32[32,216]{1,0:T(8,128)} %get-tuple-element.17.refs_2_, ...), custom_call_target="tpu_custom_call" | custom-call | tf_op jit(solution)/shard_map/pallas_call | solution.py:589
